TPU v7x, 256 devices: a whole 4x4x8 slice. The times are simulated.
256 devices in a mesh: row: 8 (over y, core), col: 32 (over x, z).
Axes of the slice: x: 4, y: 4, z: 8, core: 2. Of those that a mesh axis runs over, the one named last changes fastest.
Arguments:
- features: bfloat16 [65536, 256], P(('col', 'row')), may hold values from -6 to 6
- weight: bfloat16 [256, 256], replicated, may hold values from -0.375 to 0.375
- tile_coords: int32 [8, 32, 144, 2], P('row', 'col'), may hold values from 0 to 63, as said below
- tile_live: int32 [8, 32], P('row', 'col'), may hold values from 36 to 144, as said below
- tile_edges: int32 [8, 32, 144, 128, 128], P('row', 'col'), may hold values 0 or 1
- row_degree: int32 [65536], P(('row', 'col')), may hold values from 1 to 64
- col_degree: int32 [65536], P(('col', 'row')), may hold values from 1 to 64
- cotangent: bfloat16 [65536, 256], P(('row', 'col')), may hold values from -6 to 6
Outputs:
- aggregated: bfloat16 [65536, 256], P(('row', 'col'))
- grad_features: bfloat16 [65536, 256], P(('col', 'row'))
- grad_weight: float32 [256, 256], replicated
Inputs may be any that keep to these rules, and one draw needn't show every extreme that they name: `tile_coords`: entry 0 of a slot is a row tile of the block, 0 to 63, entry 1 a column tile, 0 to 15; slots naming the same position add. `tile_live`: the number of live leading slots of each block's list; some block fills all 144 slots.
All inputs are finite; a program needn't handle non-finite values. No bound on the sum of `tile_edges` on one device may be relied on, other than what follows from the above.
Results may differ from a plain program's by a relative error of at most 0.0055.
Values may be sent and summed in bfloat16 or wider, within the bound.
No kernel may reach another device: no remote copies, remote signals or barrier semaphores. Data moves between devices by JAX's collectives and lax.ppermute only.
A program may use at most 128 MiB of HBM per device.

v0:
```python
import jax
import jax.numpy as jnp
from jax import lax
from jax.sharding import PartitionSpec as P


def tile_products(
    local_edges, source_tiles, source_index, target_index, target_tiles, flipped, valid_slots
):
    weighted = jnp.where(valid_slots[:, None, None], local_edges, 0).astype(jnp.bfloat16)
    picked = jnp.take(source_tiles, source_index, axis=0)
    pattern = "sji,sjf->sif" if flipped else "sij,sjf->sif"
    products = jnp.einsum(pattern, weighted, picked, preferred_element_type=jnp.float32)
    empty = jnp.zeros((target_tiles, products.shape[1], products.shape[2]), jnp.float32)
    totals = empty.at[target_index].add(products)
    return totals.reshape(target_tiles, -1)


def aggregate(
    local_edges, live_count, source_tiles, source_index, target_index, target_tiles, flipped
):
    slots = local_edges.shape[0]
    tile_size = local_edges.shape[1]
    width = source_tiles.shape[2]
    valid_slots = jnp.arange(slots, dtype=jnp.int32) < live_count
    totals = tile_products(
        local_edges, source_tiles, source_index, target_index, target_tiles, flipped, valid_slots
    )
    return totals.reshape(target_tiles * tile_size, width)


def shards(features, weight, tile_coords, tile_live, tile_edges, row_degree, col_degree, cotangent):
    tile_size = tile_edges.shape[-1]
    width = features.shape[1]
    row_scale = lax.rsqrt(row_degree.astype(jnp.float32))
    col_scale = lax.rsqrt(col_degree.astype(jnp.float32))
    coords = tile_coords[0, 0]
    live_count = tile_live[0, 0]
    local_edges = tile_edges[0, 0]
    row_index = coords[:, 0]
    col_index = coords[:, 1]
    own_panel = (
        col_scale[:, None] * jnp.dot(features, weight, preferred_element_type=jnp.float32)
    ).astype(jnp.bfloat16)
    panel = lax.all_gather(own_panel, "row", axis=0, tiled=True)
    col_tiles = panel.shape[0] // tile_size
    row_tiles = col_tiles * lax.axis_size("col") // lax.axis_size("row")
    partial_value = aggregate(
        local_edges,
        live_count,
        panel.reshape(col_tiles, tile_size, width),
        col_index,
        row_index,
        row_tiles,
        False,
    )
    summed = lax.psum_scatter(partial_value, "col", scatter_dimension=0, tiled=True)
    aggregated = (row_scale[:, None] * summed).astype(jnp.bfloat16)
    upstream = (row_scale[:, None] * cotangent.astype(jnp.float32)).astype(jnp.bfloat16)
    row_panel = lax.all_gather(upstream, "col", axis=0, tiled=True)
    back_partial = aggregate(
        local_edges,
        live_count,
        row_panel.reshape(row_tiles, tile_size, width),
        row_index,
        col_index,
        col_tiles,
        True,
    )
    back_summed = lax.psum_scatter(back_partial, "row", scatter_dimension=0, tiled=True)
    grad_panel = (col_scale[:, None] * back_summed).astype(jnp.bfloat16)
    grad_features = jnp.dot(grad_panel, weight.T, preferred_element_type=jnp.float32).astype(
        jnp.bfloat16
    )
    weight_terms = lax.dot_general(
        features, grad_panel, (((0,), (0,)), ((), ())), preferred_element_type=jnp.float32
    )
    grad_weight = lax.psum(weight_terms, ("row", "col"))
    return (aggregated, grad_features, grad_weight)


def solution(mesh):
    in_specs = (
        P(("col", "row"), None),
        P(),
        P("row", "col", None, None),
        P("row", "col"),
        P("row", "col", None, None, None),
        P(("row", "col")),
        P(("col", "row")),
        P(("row", "col"), None),
    )
    out_specs = (P(("row", "col"), None), P(("col", "row"), None), P())
    return jax.shard_map(shards, mesh=mesh, in_specs=in_specs, out_specs=out_specs, check_vma=False)
```

profile of v0, /device:TPU:1, one launch (start us, length us, event | category | flops | bytes accessed | tf_op | source)
XLA Modules:
  0.0 771.9 jit_solution(11502990074820980035)
XLA Ops:
  7.2 0.0 all-gather.3.cloned.1.call-start
  7.2 0.7 convert_rsqrt_fusion
  7.9 0.1 copy-done
  8.1 1.8 fusion.9
  9.8 0.0 all-gather.3.cloned.1.call-update
  9.8 0.0 reduce-scatter.3.cloned.1.call-start
  10.6 0.8 and_reduce_fusion.1
  11.4 29.3 %all-gather.3.cloned.1.call-done = bf16[2048,256]{1,0:T(8,128)(2,1)} async-done(((bf16[256,256]{1,0:T(8,128)(2,1)}), bf16[2048,256]{1,0:T(8,128)(2,1)}) %all-gather.3.cloned.1.call-update) | async-done | bytes 1048592 | tf_op jit(solution)/shard_map/all_gather | solution.py:45
  40.6 8.5 %gather_fusion = bf16[144,128,256]{2,1,0:T(8,128)(2,1)} fusion(bf16[16,128,256]{2,1,0:T(8,128)(2,1)} %bitcast.23, s32[1024]{0:T(1024)S(1)} %pad_clamp_fusion.1), kind=kCustom, calls=%fused_computation | custom fusion | bytes 18874944 | tf_op jit(solution)/shard_map/jit(_take)/gather | solution.py:11
  49.2 15.6 %fusion.3 = f32[144,128,256]{2,1,0:T(8,128)} fusion(bf16[144,128,256]{2,1,0:T(8,128)(2,1)} %gather_fusion, pred[144]{0:T(512)(128)(4,1)S(1)} %get-tuple-element.8, s32[1,1,144,128,128]{4,3,2,1,0:T(8,128)} %param.12, pred[144]{0:T(512)(128)(4,1)S(1)} %iota_compare_fusion), kind=kOutput, calls=%fused_computation.8 | convolution fusion | flops 1217396736 | bytes 37749024 | tf_op jit(solution)/shard_map/sij,sjf->sif/dot_general | solution.py:13
  64.7 4.4 broadcast_in_dim.48
  69.1 43.2 %scatter_fusion = f32[64,128,256]{2,1,0:T(8,128)} fusion(f32[64,128,256]{2,1,0:T(8,128)} %broadcast_in_dim.48, s32[144]{0:T(256)S(1)} %bitcast.27, f32[144,128,256]{2,1,0:T(8,128)} %fusion.3), kind=kCustom, calls=%fused_computation.2 | custom fusion | flops 4718592 | bytes 56623680 | tf_op jit(solution)/shard_map/scatter-add | solution.py:15
  112.4 0.0 reduce-scatter.3.cloned.1.call-update
  112.4 0.0 all-gather.5.cloned.1.call-start
  112.5 224.7 %reduce-scatter.3.cloned.1.call-done = f32[256,256]{1,0:T(8,128)} async-done(((f32[8192,256]{1,0:T(8,128)}), f32[256,256]{1,0:T(8,128)}) %reduce-scatter.3.cloned.1.call-update) | async-done | bytes 262160 | tf_op jit(solution)/shard_map/reduce_scatter | solution.py:57
  337.2 1.8 multiply_convert_fusion.1
  338.9 0.0 all-gather.5.cloned.1.call-update
  338.9 0.0 reduce-scatter.5.cloned.1.call-start
  339.0 83.1 %all-gather.5.cloned.1.call-done = bf16[8192,256]{1,0:T(8,128)(2,1)} async-done(((bf16[256,256]{1,0:T(8,128)(2,1)}), bf16[8192,256]{1,0:T(8,128)(2,1)}) %all-gather.5.cloned.1.call-update) | async-done | bytes 4194320 | tf_op jit(solution)/shard_map/all_gather | solution.py:60
  422.1 9.5 %gather_fusion.1 = bf16[144,128,256]{2,1,0:T(8,128)(2,1)} fusion(bf16[64,128,256]{2,1,0:T(8,128)(2,1)} %bitcast.24, s32[1024]{0:T(1024)S(1)} %pad_clamp_fusion), kind=kCustom, calls=%fused_computation.1 | custom fusion | bytes 18874944 | tf_op jit(solution)/shard_map/jit(_take)/gather | solution.py:11
  431.6 12.2 %fusion.1 = f32[144,128,256]{2,1,0:T(8,128)} fusion(bf16[144,128,256]{2,1,0:T(8,128)(2,1)} %gather_fusion.1, pred[144]{0:T(512)(128)(4,1)S(1)} %get-tuple-element.10, s32[1,1,144,128,128]{4,3,2,1,0:T(8,128)} %param.12, pred[144]{0:T(512)(128)(4,1)S(1)} %iota_compare_fusion), kind=kOutput, calls=%fused_computation.6 | convolution fusion | flops 1217396736 | bytes 37749024 | tf_op jit(solution)/shard_map/sji,sjf->sif/dot_general | solution.py:13
  443.9 0.2 broadcast_in_dim.53
  444.1 27.3 %scatter_fusion.1 = f32[16,128,256]{2,1,0:T(8,128)S(1)} fusion(f32[16,128,256]{2,1,0:T(8,128)S(1)} %broadcast_in_dim.53, s32[144]{0:T(256)S(1)} %bitcast.26, f32[144,128,256]{2,1,0:T(8,128)} %fusion.1), kind=kCustom, calls=%fused_computation.3 | custom fusion | flops 4718592 | bytes 56623680 | tf_op jit(solution)/shard_map/scatter-add | solution.py:15
  471.3 1.3 copy-done.1
  472.7 0.0 reduce-scatter.5.cloned.1.call-update
  472.7 0.0 all-reduce.2.cloned.1.call-start
  472.8 33.6 %reduce-scatter.5.cloned.1.call-done = f32[256,256]{1,0:T(8,128)} async-done(((f32[2048,256]{1,0:T(8,128)}), f32[256,256]{1,0:T(8,128)}) %reduce-scatter.5.cloned.1.call-update) | async-done | bytes 262160 | tf_op jit(solution)/shard_map/reduce_scatter | solution.py:70
  506.4 2.0 convolution_bitcast_fusion
  508.3 0.0 all-reduce.2.cloned.1.call-update
  508.4 1.8 convolution_convert_fusion
  510.2 253.4 %all-reduce.2.cloned.1.call-done = f32[256,256]{0,1:T(8,128)} async-done(((f32[256,256]{0,1:T(8,128)}), f32[256,256]{0,1:T(8,128)}) %all-reduce.2.cloned.1.call-update) | async-done | bytes 262160 | tf_op jit(solution)/shard_map/psum | solution.py:78
  763.6 1.8 copy.12
  (12 shorter events, 0.0 us)
Async XLA Ops:
  7.2 0.9 copy-start
  7.2 33.5 %all-gather.3.cloned.1.call-start = ((), (), s32[]{:S(2)}) async-start(), calls=%async_computation.2 | async-start | bytes 1179648 | tf_op jit(solution)/shard_map/all_gather | solution.py:45
  9.8 327.3 %reduce-scatter.3.cloned.1.call-start = ((), (), s32[]{:S(2)}) async-start(), calls=%async_computation.3 | async-start | bytes 8650752 | tf_op jit(solution)/shard_map/reduce_scatter | solution.py:57
  69.1 43.3 %copy-start.4 = (s32[256]{0:T(256)S(1)}, s32[256]{0:T(256)}, u32[]{:S(2)}) copy-start(s32[256]{0:T(256)} %param.13) | copy-start | bytes 3076
  69.1 268.0 %copy-start.3 = (bf16[256,256]{1,0:T(8,128)(2,1)S(1)}, bf16[256,256]{1,0:T(8,128)(2,1)}, u32[]{:S(2)}) copy-start(bf16[256,256]{1,0:T(8,128)(2,1)} %param.15) | copy-start | bytes 393220
  112.4 309.7 %all-gather.5.cloned.1.call-start = ((), (), s32[]{:S(2)}) async-start(), calls=%async_computation.4 | async-start | bytes 4325376 | tf_op jit(solution)/shard_map/all_gather | solution.py:60
  338.9 167.4 %reduce-scatter.5.cloned.1.call-start = ((), (), s32[]{:S(2)}) async-start(), calls=%async_computation.5 | async-start | bytes 2359296 | tf_op jit(solution)/shard_map/reduce_scatter | solution.py:70
  444.1 64.3 %copy-start.2 = (bf16[256,256]{1,0:T(8,128)(2,1)S(1)}, bf16[256,256]{1,0:T(8,128)(2,1)}, u32[]{:S(2)}) copy-start(bf16[256,256]{1,0:T(8,128)(2,1)} %param.9) | copy-start | bytes 393220
  471.3 1.3 copy-start.1
  472.7 290.9 %all-reduce.2.cloned.1.call-start = ((), (), s32[]{:S(2)}) async-start(), calls=%async_computation.6 | async-start | bytes 524288 | tf_op jit(solution)/shard_map/psum | solution.py:78
Sparse Core Ops, SparseCore 0:
  10.4 30.1 all-gather.2
  112.5 224.6 reduce-scatter.2
  340.7 81.3 all-gather.4
  472.8 33.4 reduce-scatter.4
  513.1 250.3 all-reduce.1
where the time goes:
time: 773 us; the launch traced here: 772 us
  waiting for transfers between devices  624 us (81%)
  other arithmetic  73.8 us (10%)
  matrix products  33.3 us (4%)
  local copies, waits for them, and re-layouts  25.9 us (3%)
  between operations  14.5 us (2%)
    psum x1, waiting for transfers between devices, shards(): grad_weight = lax.psum(weight_terms, ('row', 'col'))  253 us
    reduce_scatter x1, waiting for transfers between devices, shards(): lax.psum_scatter(partial_value, 'col', scatter_dimension=0, tiled=True)  225 us
    all_gather x1, waiting for transfers between devices, shards(): row_panel = lax.all_gather(upstream, 'col', axis=0, tiled=True)  83.1 us
    scatter-add x2, other arithmetic, tile_products(): totals = empty.at[target_index].add(products)  70.5 us
    reduce_scatter x1, waiting for transfers between devices, shards(): lax.psum_scatter(back_partial, 'row', scatter_dimension=0, tiled=True)  33.6 us
    all_gather x1, waiting for transfers between devices, shards(): panel = lax.all_gather(own_panel, 'row', axis=0, tiled=True)  29.3 us
    dot_general x2, matrix products, tile_products(): jnp.einsum(pattern, weighted, picked, preferred_element_type=jnp.float32)  27.8 us
    gather x2, local copies, waits for them, and re-layouts, tile_products(): picked = jnp.take(source_tiles, source_index, axis=0)  18.1 us
  transfers between devices with their start and end apart: 5, of which 5 were waited for; matrix products, arithmetic and copies ran while one was open for 0% of the time, Pallas kernels for 0%

commit v1 on v0

v1 whole, which is shorter than its diff:
```python
import functools

import jax
import jax.numpy as jnp
from jax import lax
from jax.experimental import pallas as pl
from jax.experimental.pallas import tpu as pltpu
from jax.sharding import PartitionSpec as P

X, Z = 4, 8
Y = 4
CHUNK = 16
GROUP = 4


def along_z(d):
    return [(x * Z + z, x * Z + (z + d) % Z) for x in range(X) for z in range(Z)]


def along_x(d):
    return [(x * Z + z, ((x + d) % X) * Z + z) for x in range(X) for z in range(Z)]


def along_y(d):
    return [(y * 2 + c, ((y + d) % Y) * 2 + c) for y in range(Y) for c in range(2)]


OTHER_CORE = [(r, r ^ 1) for r in range(2 * Y)]
Z_GROUPS = [[x * Z + z for z in range(Z)] for x in range(X)]


def send(value, axis, pairs):
    return lax.ppermute(value, axis, pairs)


def exchange_z(value):
    return lax.all_to_all(value, "col", 0, 0, axis_index_groups=Z_GROUPS)


def chunk_tiles(meta_ref, live, chunk, edges_ref, product_ref, visit):
    first = chunk * CHUNK
    count = jnp.minimum(live - first, CHUNK)

    @pl.loop(0, (count + GROUP - 1) // GROUP)
    def _(step):
        spots = []
        for k in range(GROUP):
            here = step * GROUP + k
            at = first + here
            tile = jnp.where(at < live, edges_ref[here], 0).astype(jnp.float32).astype(jnp.bfloat16)
            spots.append((meta_ref[0, at], meta_ref[1, at]))
            product_ref[k] = visit.product(tile, *spots[-1])
        for k in range(GROUP):
            visit.add(product_ref[k], *spots[k])


class Forward:
    def __init__(self, panel_ref, total_ref):
        self.panel_ref, self.total_ref = panel_ref, total_ref

    def product(self, tile, slot, column):
        return jnp.dot(tile, self.panel_ref[column], preferred_element_type=jnp.float32)

    def add(self, product, slot, column):
        self.total_ref[slot] += product


class Backward:
    def __init__(self, upstream_ref, total_ref):
        self.upstream_ref, self.total_ref = upstream_ref, total_ref

    def product(self, tile, slot, column):
        return lax.dot_general(
            tile, self.upstream_ref[slot], (((0,), (0,)), ((), ())),
            preferred_element_type=jnp.float32,
        )

    def add(self, product, slot, column):
        self.total_ref[column] += product


def forward_kernel(
    meta_ref, live_ref, edges_ref, panel_ref,
    x_up_ref, x_down_ref, x_up_later_ref, x_down_later_ref, x_own_ref,
    z_up_ref, z_down_ref, z_later_ref,
    total, products,
):
    chunk = pl.program_id(0)
    live = live_ref[0]

    @pl.when(chunk == 0)
    def _():
        total[...] = jnp.zeros_like(total)

    @pl.when(chunk * CHUNK < live)
    def _():
        chunk_tiles(meta_ref, live, chunk, edges_ref, products, Forward(panel_ref, total))

    @pl.when(chunk == pl.num_programs(0) - 1)
    def _():
        bf16 = jnp.bfloat16
        for z in range(4):
            x_up_ref[z] = total[16 + z].astype(bf16)
            x_up_ref[4 + z] = total[8 + 4 + z].astype(bf16)
            x_down_ref[z] = total[24 + z].astype(bf16)
            x_down_ref[4 + z] = total[16 + 4 + z].astype(bf16)
            x_up_later_ref[z] = total[8 + z]
            x_down_later_ref[z] = total[24 + 4 + z]
        for z in range(8):
            x_own_ref[z] = total[z]
        for d in range(2):
            z_up_ref[d] = total[32 + 16 + d].astype(bf16)
            z_down_ref[d] = total[32 + 16 + 2 + d].astype(bf16)
        for k, dz in enumerate((3, 5, 2, 6, 1, 7, 0)):
            for d in range(4):
                z_later_ref[k, d] = total[32 + dz * 4 + d]


def backward_kernel(places, meta_ref, live_ref, edges_ref, *refs):
    pieces = refs[: len(places)]
    total_ref, upstream, products, sems = refs[len(places) :]
    chunk = pl.program_id(0)
    live = live_ref[0]

    @pl.when(chunk == 0)
    def _():
        copies = [
            pltpu.make_async_copy(piece, upstream.at[pl.ds(at, piece.shape[0])], sems.at[k])
            for k, (piece, at) in enumerate(zip(pieces, places))
        ]
        for copy in copies:
            copy.start()
        total_ref[...] = jnp.zeros_like(total_ref)
        for copy in copies:
            copy.wait()

    @pl.when(chunk * CHUNK < live)
    def _():
        chunk_tiles(meta_ref, live, chunk, edges_ref, products, Backward(upstream, total_ref))


def edges_spec(size):
    return pl.BlockSpec(
        (CHUNK, size, size),
        lambda i, meta, live: (jnp.minimum(i, (live[0] - 1) // CHUNK), 0, 0),
    )


def whole(shape):
    return pl.BlockSpec(shape, lambda i, meta, live: (0,) * len(shape))


PARAMS = dict(vmem_limit_bytes=48 * 1024 * 1024)


def forward(meta, live, edges, panel):
    slots, size, _ = edges.shape
    width = panel.shape[-1]
    f32, bf16 = jnp.float32, jnp.bfloat16
    outs = [
        ((8, size, width), bf16), ((8, size, width), bf16),
        ((4, size, width), f32), ((4, size, width), f32), ((8, size, width), f32),
        ((2, size, width), bf16), ((2, size, width), bf16), ((7, 4, size, width), f32),
    ]
    return pl.pallas_call(
        forward_kernel,
        grid_spec=pltpu.PrefetchScalarGridSpec(
            num_scalar_prefetch=2,
            grid=(slots // CHUNK,),
            in_specs=[edges_spec(size), whole(panel.shape)],
            out_specs=[whole(shape) for shape, _ in outs],
            scratch_shapes=[
                pltpu.VMEM((64, size, width), f32),
                pltpu.VMEM((GROUP, size, width), f32),
            ],
        ),
        out_shape=[jax.ShapeDtypeStruct(shape, dtype) for shape, dtype in outs],
        compiler_params=pltpu.CompilerParams(**PARAMS),
        cost_estimate=pl.CostEstimate(flops=10**10, bytes_accessed=2 * 10**7, transcendentals=0),
        name="forward_tiles",
    )(meta, live, edges, panel)


def backward(meta, live, edges, pieces, places, col_tiles):
    slots, size, _ = edges.shape
    width = pieces[0].shape[-1]
    f32 = jnp.float32
    return pl.pallas_call(
        functools.partial(backward_kernel, places),
        grid_spec=pltpu.PrefetchScalarGridSpec(
            num_scalar_prefetch=2,
            grid=(slots // CHUNK,),
            in_specs=[edges_spec(size)] + [pl.BlockSpec(memory_space=pl.ANY)] * len(pieces),
            out_specs=whole((col_tiles, size, width)),
            scratch_shapes=[
                pltpu.VMEM((64, size, width), jnp.bfloat16),
                pltpu.VMEM((GROUP, size, width), f32),
                pltpu.SemaphoreType.DMA((len(pieces),)),
            ],
        ),
        out_shape=jax.ShapeDtypeStruct((col_tiles, size, width), f32),
        compiler_params=pltpu.CompilerParams(**PARAMS),
        cost_estimate=pl.CostEstimate(flops=10**10, bytes_accessed=2 * 10**7, transcendentals=0),
        name="backward_tiles",
    )(meta, live, edges, *pieces)


def gather_col(own, size):
    first, second = own[:size], own[size:]
    z_all = exchange_z(jnp.broadcast_to(first, (Z,) + first.shape))
    x_all = jnp.stack(
        [
            second,
            send(second, "col", along_x(-1)),
            send(second, "col", along_x(2)),
            send(second, "col", along_x(1)),
        ]
    )
    places = [(z_all, 0), (x_all, 32)]
    left = send(z_all, "col", along_x(1))
    right = send(z_all, "col", along_x(-1))
    places += [(left, 24), (right, 8)]
    places += [
        (send(left[:4], "col", along_x(1)), 16),
        (send(right[4:], "col", along_x(-1)), 20),
    ]
    up = down = x_all
    for k in range(1, 4):
        up = send(up, "col", along_z(1))
        down = send(down, "col", along_z(-1))
        places += [(up, 32 + 4 * (8 - k)), (down, 32 + 4 * k)]
    places += [
        (send(up[:2], "col", along_z(1)), 32 + 16),
        (send(down[2:], "col", along_z(-1)), 32 + 18),
    ]
    return [piece for piece, _ in places], [at for _, at in places]


def scatter_col(parts):
    x_up, x_down, x_up_later, x_down_later, x_own, z_up, z_down, z_later = parts
    f32, bf16 = jnp.float32, jnp.bfloat16
    from_left = send(x_up, "col", along_x(1))
    from_right = send(x_down, "col", along_x(-1))
    from_below = send(z_up, "col", along_z(1))
    from_above = send(z_down, "col", along_z(-1))

    up = z_later[0] + jnp.concatenate([from_below, jnp.zeros_like(from_below)]).astype(f32)
    down = z_later[1] + jnp.concatenate([jnp.zeros_like(from_above), from_above]).astype(f32)
    up, down = up.astype(bf16), down.astype(bf16)
    for k in (2, 4):
        from_below = send(up, "col", along_z(1))
        from_above = send(down, "col", along_z(-1))
        up = (z_later[k] + from_below.astype(f32)).astype(bf16)
        down = (z_later[k + 1] + from_above.astype(f32)).astype(bf16)
    from_below = send(up, "col", along_z(1))
    from_above = send(down, "col", along_z(-1))
    column = z_later[6] + from_below.astype(f32) + from_above.astype(f32)
    packed = column.astype(bf16)
    second = column[0] + sum(
        send(packed[d], "col", along_x(d)).astype(f32) for d in range(1, X)
    )

    last_left = send((x_up_later + from_left[:4].astype(f32)).astype(bf16), "col", along_x(1))
    last_right = send((x_down_later + from_right[4:].astype(f32)).astype(bf16), "col", along_x(-1))
    plane = (
        x_own
        + jnp.concatenate([last_left, from_left[4:]]).astype(f32)
        + jnp.concatenate([from_right[:4], last_right]).astype(f32)
    )
    first = jnp.sum(exchange_z(plane.astype(bf16)).astype(f32), axis=0)
    return jnp.concatenate([first, second])


def sum_all(terms):
    rows, width = terms.shape
    y, core = lax.axis_index("row") // 2, lax.axis_index("row") % 2
    blocks = terms.reshape(2, rows // 2, width)
    own = lax.dynamic_index_in_dim(blocks, core, 0, False)
    other = lax.dynamic_index_in_dim(blocks, 1 - core, 0, False)
    half = own + send(other, "row", OTHER_CORE)
    quarters = half.reshape(Y, rows // 2 // Y, width)

    def quarter(d):
        return lax.dynamic_index_in_dim(quarters, (y + d) % Y, 0, False)

    part = quarter(0) + sum(send(quarter(d), "row", along_y(d)) for d in range(1, Y))
    part = jnp.sum(exchange_z(jnp.broadcast_to(part, (Z,) + part.shape)), axis=0)
    arrived = [send(part, "col", along_x(d)) for d in range(1, X)]
    ordered = [part] + arrived
    x = lax.axis_index("col") // Z
    stacked = jnp.stack(ordered)
    part = jnp.sum(
        jnp.take(stacked, (x - jnp.arange(X, dtype=jnp.int32)) % X, axis=0), axis=0
    )
    got = jnp.stack([part] + [send(part, "row", along_y(d)) for d in range(1, Y)])
    half = jnp.take(got, (y - jnp.arange(Y, dtype=jnp.int32)) % Y, axis=0)
    half = half.reshape(rows // 2, width)
    other = send(half, "row", OTHER_CORE)
    return jnp.where(
        core == 0, jnp.concatenate([half, other]), jnp.concatenate([other, half])
    )


def shards(features, weight, tile_coords, tile_live, tile_edges, row_degree, col_degree, cotangent):
    f32, bf16 = jnp.float32, jnp.bfloat16
    size = tile_edges.shape[-1]
    nodes, width = features.shape
    row_scale = lax.rsqrt(row_degree.astype(f32))
    col_scale = lax.rsqrt(col_degree.astype(f32))
    coords = tile_coords[0, 0]
    live = tile_live[0]
    edges = tile_edges[0, 0]

    col = lax.axis_index("col")
    owner, half = coords[:, 0] // 2, coords[:, 0] % 2
    dx = (owner // Z - col // Z) % X
    dz = (owner % Z - col % Z) % Z
    slot = jnp.where(half == 0, dx * Z + owner % Z, 32 + dz * X + dx)
    meta = jnp.stack([slot, coords[:, 1]]).astype(jnp.int32)

    upstream = (row_scale[:, None] * cotangent.astype(f32)).astype(bf16)
    pieces, places = gather_col(upstream, size)

    degrees = jnp.zeros((16, width), bf16).at[0].set(col_degree.astype(bf16))
    block = lax.all_gather(jnp.concatenate([features, degrees]), "row", axis=0)
    block_features = block[:, :nodes].reshape(-1, width)
    block_scale = lax.rsqrt(block[:, nodes].astype(f32)).reshape(-1, 1)
    panel = (
        block_scale * jnp.dot(block_features, weight, preferred_element_type=f32)
    ).astype(bf16)
    panel = panel.reshape(-1, size, width)

    parts = forward(meta, live, edges, panel)
    aggregated = (row_scale[:, None] * scatter_col(parts)).astype(bf16)

    back = backward(meta, live, edges, pieces, places, panel.shape[0]).reshape(-1, width)
    terms = lax.dot_general(
        block_features,
        (block_scale * back).astype(bf16),
        (((0,), (0,)), ((), ())),
        preferred_element_type=f32,
    )
    grad_weight = sum_all(terms)
    back_summed = lax.psum_scatter(back, "row", scatter_dimension=0, tiled=True)
    grad_panel = (col_scale[:, None] * back_summed).astype(bf16)
    grad_features = jnp.dot(grad_panel, weight.T, preferred_element_type=f32).astype(bf16)
    return aggregated, grad_features, grad_weight


def solution(mesh):
    in_specs = (
        P(("col", "row"), None),
        P(),
        P("row", "col", None, None),
        P("row", "col"),
        P("row", "col", None, None, None),
        P(("row", "col")),
        P(("col", "row")),
        P(("row", "col"), None),
    )
    out_specs = (P(("row", "col"), None), P(("col", "row"), None), P())
    return jax.shard_map(shards, mesh=mesh, in_specs=in_specs, out_specs=out_specs, check_vma=False)
```

time: 773 us -> 248 us (0.32)
  waiting for transfers between devices: 624 us -> 92.9 us
  starting transfers between devices: 0.21 us -> 95.6 us
  other arithmetic: 73.8 us -> 14 us
  matrix products: 33.3 us -> 2.71 us
  Pallas kernels: 0 us -> 19.6 us
  local copies, waits for them, and re-layouts: 25.9 us -> 7.25 us
    reduce_scatter x2 -> x1, waiting for transfers between devices: 258 us -> 0.01 us  [shards(): back_summed = lax.psum_scatter(back, 'row', scatter_dimension=0, tiled=True)]
    psum x1 -> x0, waiting for transfers between devices: 253 us -> none  [shards(): grad_weight = lax.psum(weight_terms, ('row', 'col'))]
    all_gather x2 -> x1, waiting for transfers between devices: 112 us -> 29.1 us  [shards(): block = lax.all_gather(jnp.concatenate([features, degrees]), 'row', axis=0)]
    ppermute x0 -> x41, starting transfers between devices: none -> 76.8 us  [send(): return lax.ppermute(value, axis, pairs)]
    scatter-add x2 -> x0, other arithmetic: 70.5 us -> none  [tile_products(): totals = empty.at[target_index].add(products)]
    ppermute x0 -> x41, waiting for transfers between devices: none -> 48.3 us  [send(): return lax.ppermute(value, axis, pairs)]
    dot_general x5 -> x3, matrix products: 33.3 us -> 2.71 us  [the longest x1 1.83 us: shards(): jnp.dot(grad_panel, weight.T, preferred_element_type=f32).astype(bf16)]
    pallas_call x0 -> x2, Pallas kernels: none -> 19.6 us  [the longest x1 9.89 us: forward(): pl.pallas_call(forward_kernel, grid_spec=pltpu.PrefetchScalarGridSpec(num...]
  transfers between devices with their start and end apart: 5 -> 46, of which waited for: 5 -> 30; matrix products, arithmetic and copies ran while one was open for 0% -> 5% of each run, Pallas kernels for 0% -> 0%
where the time goes in v1:
time: 248 us; the launch traced here: 247 us
  starting transfers between devices  95.6 us (39%)
  waiting for transfers between devices  92.9 us (37%)
  Pallas kernels  19.6 us (8%)
  between operations  15.1 us (6%)
  other arithmetic  14 us (6%)
  local copies, waits for them, and re-layouts  7.25 us (3%)
  matrix products  2.71 us (1%)
    ppermute x41, starting transfers between devices, send(): return lax.ppermute(value, axis, pairs)  76.8 us
    ppermute x41, waiting for transfers between devices, send(): return lax.ppermute(value, axis, pairs)  48.3 us
    all_gather x1, waiting for transfers between devices, shards(): block = lax.all_gather(jnp.concatenate([features, degrees]), 'row', axis=0)  29.1 us
    all_to_all x3, starting transfers between devices, exchange_z(): return lax.all_to_all(value, 'col', 0, 0, axis_index_groups=Z_GROUPS)  18.8 us
    all_to_all x3, waiting for transfers between devices, exchange_z(): return lax.all_to_all(value, 'col', 0, 0, axis_index_groups=Z_GROUPS)  15.4 us
    pallas_call x1, Pallas kernels, forward(): pl.pallas_call(forward_kernel, grid_spec=pltpu.PrefetchScalarGridSpec(num...  9.89 us
    pallas_call x1, Pallas kernels, backward(): pl.pallas_call(functools.partial(backward_kernel, places), grid_spec=pltp...  9.72 us
  transfers between devices with their start and end apart: 46, of which 30 were waited for; matrix products, arithmetic and copies ran while one was open for 5% of the time, Pallas kernels for 0%

profile of v1, /device:TPU:1, one launch (start us, length us, event | category | flops | bytes accessed | tf_op | source)
XLA Modules:
  0.0 247.1 jit_solution(13501458871588691078)
XLA Ops:
  11.6 29.1 %all-gather.3.cloned.1.call-done = bf16[2176,256]{1,0:T(8,128)(2,1)} async-done(((bf16[272,256]{1,0:T(8,128)(2,1)}), bf16[2176,256]{1,0:T(8,128)(2,1)}) %all-gather.3.cloned.1.call-update) | async-done | bytes 1114128 | tf_op jit(solution)/shard_map/all_gather | solution.py:325
  43.3 9.9 %forward_tiles.1 = (bf16[8,128,256]{2,1,0:T(8,128)(2,1)S(1)}, bf16[8,128,256]{2,1,0:T(8,128)(2,1)S(1)}, f32[4,128,256]{2,1,0:T(8,128)S(1)}, f32[4,128,256]{2,1,0...) custom-call(s32[2,144]{1,0:T(2,128)S(1)} %pad_add_fusion.meta_ref, ...), custom_call_target="tpu_custom_call" | custom-call | flops 10000000000 | bytes 20000000 | tf_op jit(solution)/shard_map/forward_tiles/pallas_call | solution.py:165
  53.6 6.6 %collective-permute-done.4 = bf16[2,128,256]{2,1,0:T(8,128)(2,1)S(1)} collective-permute-done((bf16[2,128,256]{2,1,0:T(8,128)(2,1)S(1)}, bf16[2,128,256]{2,1,0:T(8,128)(2,1)S(1)}, u32[]{:S(2)}, u32[]{:S(2)}) %collective-permute-start.4) | collective-permute-done | bytes 131104 | tf_op jit(solution)/shard_map/ppermute | solution.py:33
  62.3 5.6 %collective-permute-done.5 = bf16[4,128,256]{2,1,0:T(8,128)(2,1)S(1)} collective-permute-done((bf16[4,128,256]{2,1,0:T(8,128)(2,1)S(1)}, bf16[4,128,256]{2,1,0:T(8,128)(2,1)S(1)}, u32[]{:S(2)}, u32[]{:S(2)}) %collective-permute-start.5) | collective-permute-done | bytes 262176 | tf_op jit(solution)/shard_map/ppermute | solution.py:33
  68.9 2.2 collective-permute-start.6
  71.2 4.0 %collective-permute-start.2 = (bf16[8,128,256]{2,1,0:T(8,128)(2,1)S(1)}, bf16[8,128,256]{2,1,0:T(8,128)(2,1)S(1)}, u32[]{:S(2)}, u32[]{:S(2)}) collective-permute-start(bf16[8,128,256]{2,1,0:T(8,128)(2,1)S(1)} %get-tuple-element.27), channel_id=1, source_target_pairs={{0,24},{1,25},{2,26},{3,27},{4,28},{5,29},{6,30},{7,31},{8,0},{9,1... | collective-permute-start | bytes 1572872 | tf_op jit(solution)/shard_map/ppermute | solution.py:33
  75.2 2.6 %collective-permute-start.8 = (bf16[2,128,256]{2,1,0:T(8,128)(2,1)S(1)}, bf16[2,128,256]{2,1,0:T(8,128)(2,1)S(1)}, u32[]{:S(2)}, u32[]{:S(2)}) collective-permute-start(bf16[2,128,256]{2,1,0:T(8,128)(2,1)S(1)} %get-tuple-element.31), channel_id=1, source_target_pairs={{0,7},{1,0},{2,1},{3,2},{4,3},{5,4},{6,5},{7,6},{8,15},{9,8},{10,9... | collective-permute-start | bytes 393224 | tf_op jit(solution)/shard_map/ppermute | solution.py:33
  81.5 3.5 %collective-permute-start.9 = (bf16[4,128,256]{2,1,0:T(8,128)(2,1)S(1)}, bf16[4,128,256]{2,1,0:T(8,128)(2,1)S(1)}, u32[]{:S(2)}, u32[]{:S(2)}) collective-permute-start(bf16[4,128,256]{2,1,0:T(8,128)(2,1)S(1)} %get-tuple-element.35), channel_id=1, source_target_pairs={{0,7},{1,0},{2,1},{3,2},{4,3},{5,4},{6,5},{7,6},{8,15},{9,8},{10,9... | collective-permute-start | bytes 786440 | tf_op jit(solution)/shard_map/ppermute | solution.py:33
  86.9 2.6 %collective-permute-start.3 = (bf16[4,128,256]{2,1,0:T(8,128)(2,1)S(1)}, bf16[4,128,256]{2,1,0:T(8,128)(2,1)S(1)}, u32[]{:S(2)}, u32[]{:S(2)}) collective-permute-start(bf16[4,128,256]{2,1,0:T(8,128)(2,1)S(1)} %add_convert_fusion.1), channel_id=1, source_target_pairs={{0,24},{1,25},{2,26},{3,27},{4,28},{5,29},{6,30},{7,31},{8,0},{9,1... | collective-permute-start | bytes 786440 | tf_op jit(solution)/shard_map/ppermute | solution.py:33
  90.6 3.4 %collective-permute-start.10 = (bf16[4,128,256]{2,1,0:T(8,128)(2,1)S(1)}, bf16[4,128,256]{2,1,0:T(8,128)(2,1)S(1)}, u32[]{:S(2)}, u32[]{:S(2)}) collective-permute-start(bf16[4,128,256]{2,1,0:T(8,128)(2,1)S(1)} %fusion.2), channel_id=1, source_target_pairs={{0,7},{1,0},{2,1},{3,2},{4,3},{5,4},{6,5},{7,6},{8,15},{9,8},{10,9... | collective-permute-start | bytes 786440 | tf_op jit(solution)/shard_map/ppermute | solution.py:33
  94.2 3.0 %collective-permute-done.10 = bf16[4,128,256]{2,1,0:T(8,128)(2,1)S(1)} collective-permute-done((bf16[4,128,256]{2,1,0:T(8,128)(2,1)S(1)}, bf16[4,128,256]{2,1,0:T(8,128)(2,1)S(1)}, u32[]{:S(2)}, u32[]{:S(2)}) %collective-permute-start.10) | collective-permute-done | bytes 262176 | tf_op jit(solution)/shard_map/ppermute | solution.py:33
  98.4 3.6 %collective-permute-start.11 = (bf16[4,128,256]{2,1,0:T(8,128)(2,1)S(1)}, bf16[4,128,256]{2,1,0:T(8,128)(2,1)S(1)}, u32[]{:S(2)}, u32[]{:S(2)}) collective-permute-start(bf16[4,128,256]{2,1,0:T(8,128)(2,1)S(1)} %fusion.3), channel_id=1, source_target_pairs={{0,7},{1,0},{2,1},{3,2},{4,3},{5,4},{6,5},{7,6},{8,15},{9,8},{10,9... | collective-permute-start | bytes 786440 | tf_op jit(solution)/shard_map/ppermute | solution.py:33
  103.0 3.8 %all-to-all-start = ((bf16[8,128,256]{2,1,0:T(8,128)(2,1)}), bf16[8,128,256]{2,1,0:T(8,128)(2,1)S(1)}, u32[]{:S(2)}, u32[]{:S(2)}) async-start(bf16[8,128,256]{2,1,0:T(8,128)(2,1)} %add_convert_fusion), calls=%async_computation | async-start | bytes 1048576 | tf_op jit(solution)/shard_map/all_to_all | solution.py:37
  108.1 3.4 %collective-permute-start.13 = (bf16[128,256]{1,0:T(8,128)(2,1)S(1)}, bf16[128,256]{1,0:T(8,128)(2,1)S(1)}, u32[]{:S(2)}, u32[]{:S(2)}) collective-permute-start(bf16[128,256]{1,0:T(8,128)(2,1)S(1)} %get-tuple-element.38), channel_id=1, source_target_pairs={{0,16},{1,17},{2,18},{3,19},{4,20},{5,21},{6,22},{7,23},{8,24},{9,... | collective-permute-start | bytes 196616 | tf_op jit(solution)/shard_map/ppermute | solution.py:33
  114.9 3.9 %all-to-all-done = bf16[8,128,256]{2,1,0:T(8,128)(2,1)S(1)} async-done(((bf16[8,128,256]{2,1,0:T(8,128)(2,1)}), bf16[8,128,256]{2,1,0:T(8,128)(2,1)S(1)}, u32[]{:S(2)}, u32[]{:S(2)}) %all-to-all-start) | async-done | bytes 524320 | tf_op jit(solution)/shard_map/all_to_all | solution.py:37
  120.5 3.8 %all-to-all-start.1 = ((bf16[8,128,256]{2,1,0:T(8,128)(2,1)}), bf16[8,128,256]{2,1,0:T(8,128)(2,1)S(1)}, u32[]{:S(2)}, u32[]{:S(2)}) async-start(bf16[8,128,256]{2,1,0:T(8,128)(2,1)} %broadcast_in_dim.19), calls=%async_computation.1 | async-start | bytes 1048576 | tf_op jit(solution)/shard_map/all_to_all | solution.py:37
  124.3 2.2 collective-permute-start.15
  127.9 3.4 %collective-permute-done.16 = bf16[128,256]{1,0:T(8,128)(2,1)S(1)} collective-permute-done((bf16[128,256]{1,0:T(8,128)(2,1)S(1)}, bf16[128,256]{1,0:T(8,128)(2,1)S(1)}, u32[]{:S(2)}, u32[]{:S(2)}) %collective-permute-start.16) | collective-permute-done | bytes 65568 | tf_op jit(solution)/shard_map/ppermute | solution.py:33
  136.4 2.7 %collective-permute-start.19 = (bf16[8,128,256]{2,1,0:T(8,128)(2,1)S(1)}, bf16[8,128,256]{2,1,0:T(8,128)(2,1)S(1)}, u32[]{:S(2)}, u32[]{:S(2)}) collective-permute-start(bf16[8,128,256]{2,1,0:T(8,128)(2,1)S(1)} %all-to-all-done.1.refs_0_), channel_id=1, source_target_pairs={{0,24},{1,25},{2,26},{3,27},{4,28},{5,29},{6,30},{7,31},{8,0},{9,1... | collective-permute-start | bytes 1572872 | tf_op jit(solution)/shard_map/ppermute | solution.py:33
  139.1 2.7 %collective-permute-start.25 = (bf16[4,128,256]{2,1,0:T(8,128)(2,1)S(1)}, bf16[4,128,256]{2,1,0:T(8,128)(2,1)S(1)}, u32[]{:S(2)}, u32[]{:S(2)}) collective-permute-start(bf16[4,128,256]{2,1,0:T(8,128)(2,1)S(1)} %collective-permute-done.23.refs_7_), channel_id=1, source_target_pairs={{0,7},{1,0},{2,1},{3,2},{4,3},{5,4},{6,5},{7,6},{8,15},{9,8},{10,9... | collective-permute-start | bytes 786440 | tf_op jit(solution)/shard_map/ppermute | solution.py:33
  141.8 6.1 %collective-permute-done.24.refs_8_ = bf16[4,128,256]{2,1,0:T(8,128)(2,1)S(1)} collective-permute-done((bf16[4,128,256]{2,1,0:T(8,128)(2,1)S(1)}, bf16[4,128,256]{2,1,0:T(8,128)(2,1)S(1)}, u32[]{:S(2)}, u32[]{:S(2)}) %collective-permute-start.24) | collective-permute-done | bytes 262176 | tf_op jit(solution)/shard_map/ppermute | solution.py:33
  148.1 2.5 %collective-permute-start.27 = (bf16[4,128,256]{2,1,0:T(8,128)(2,1)S(1)}, bf16[4,128,256]{2,1,0:T(8,128)(2,1)S(1)}, u32[]{:S(2)}, u32[]{:S(2)}) collective-permute-start(bf16[4,128,256]{2,1,0:T(8,128)(2,1)S(1)} %collective-permute-done.25.refs_9_), channel_id=1, source_target_pairs={{0,7},{1,0},{2,1},{3,2},{4,3},{5,4},{6,5},{7,6},{8,15},{9,8},{10,9... | collective-permute-start | bytes 786440 | tf_op jit(solution)/shard_map/ppermute | solution.py:33
  151.2 2.5 %collective-permute-start.21 = (bf16[4,128,256]{2,1,0:T(8,128)(2,1)S(1)}, bf16[4,128,256]{2,1,0:T(8,128)(2,1)S(1)}, u32[]{:S(2)}, u32[]{:S(2)}) collective-permute-start(bf16[4,128,256]{2,1,0:T(8,128)(2,1)S(1)} %slice.134), channel_id=1, source_target_pairs={{0,24},{1,25},{2,26},{3,27},{4,28},{5,29},{6,30},{7,31},{8,0},{9,1... | collective-permute-start | bytes 786440 | tf_op jit(solution)/shard_map/ppermute | solution.py:33
  153.7 2.3 collective-permute-done.26.refs_10_
  156.4 2.4 collective-permute-start.29
  158.9 3.7 %collective-permute-done.28.refs_12_ = bf16[2,128,256]{2,1,0:T(8,128)(2,1)S(1)} collective-permute-done((bf16[2,128,256]{2,1,0:T(8,128)(2,1)S(1)}, bf16[2,128,256]{2,1,0:T(8,128)(2,1)S(1)}, u32[]{:S(2)}, u32[]{:S(2)}) %collective-permute-start.28) | collective-permute-done | bytes 131104 | tf_op jit(solution)/shard_map/ppermute | solution.py:33
  162.6 9.7 %backward_tiles.1 = f32[16,128,256]{2,1,0:T(8,128)} custom-call(s32[2,144]{1,0:T(2,128)S(1)} %pad_add_fusion.meta_ref, s32[1]{0:T(128)} %bitcast.93.live_ref, s32[144,128,128]{2,1,0:T(8,128)} %bitcast.122, bf16[8,128,256]{2,1,0:T(8,128)(2,1)S(1)} %all-to-all-done.1.refs_0_, bf16[4,128,256]{2,1,0:T(8,128)(2,1)S(1)} %pad_maximum_fusion.refs_1_, ...), custom_call_target="tpu_custom_call" | custom-call | flops 10000000000 | bytes 20000000 | tf_op jit(solution)/shard_map/backward_tiles/pallas_call | solution.py:188
  175.6 14.5 %collective-permute-start.30 = (f32[128,256]{1,0:T(8,128)S(1)}, f32[128,256]{1,0:T(8,128)S(1)}, u32[]{:S(2)}, u32[]{:S(2)}) collective-permute-start(f32[128,256]{1,0:T(8,128)S(1)} %dynamic-slice_bitcast_fusion), channel_id=1, source_target_pairs={{0,32},{32,0},{64,96},{96,64},{128,160},{160,128},{192,224},{224,1... | collective-permute-start | bytes 393224 | tf_op jit(solution)/shard_map/ppermute | solution.py:33
  191.4 2.6 %collective-permute-start.33 = (f32[32,256]{1,0:T(8,128)S(1)}, f32[32,256]{1,0:T(8,128)S(1)}, u32[]{:S(2)}, u32[]{:S(2)}) collective-permute-start(f32[32,256]{1,0:T(8,128)S(1)} %get-tuple-element.40), channel_id=1, source_target_pairs={{0,192},{32,224},{64,0},{96,32},{128,64},{160,96},{192,128},{224,1... | collective-permute-start | bytes 98312 | tf_op jit(solution)/shard_map/ppermute | solution.py:33
  197.2 11.2 %all-to-all-start.2 = ((f32[8,32,256]{2,1,0:T(8,128)}), f32[8,32,256]{2,1,0:T(8,128)S(1)}, u32[]{:S(2)}, u32[]{:S(2)}) async-start(f32[8,32,256]{2,1,0:T(8,128)} %broadcast_in_dim.20), calls=%async_computation.3 | async-start | bytes 524288 | tf_op jit(solution)/shard_map/all_to_all | solution.py:37
  208.5 9.5 %all-to-all-done.2 = f32[8,32,256]{2,1,0:T(8,128)S(1)} async-done(((f32[8,32,256]{2,1,0:T(8,128)}), f32[8,32,256]{2,1,0:T(8,128)S(1)}, u32[]{:S(2)}, u32[]{:S(2)}) %all-to-all-start.2) | async-done | bytes 262176 | tf_op jit(solution)/shard_map/all_to_all | solution.py:37
  229.7 7.1 %collective-permute-start.40 = (f32[128,256]{1,0:T(8,128)S(1)}, f32[128,256]{1,0:T(8,128)S(1)}, u32[]{:S(2)}, u32[]{:S(2)}) collective-permute-start(f32[128,256]{1,0:T(8,128)S(1)} %bitcast.102), channel_id=1, source_target_pairs={{0,32},{32,0},{64,96},{96,64},{128,160},{160,128},{192,224},{224,1... | collective-permute-start | bytes 393224 | tf_op jit(solution)/shard_map/ppermute | solution.py:33
  (131 shorter events, 55.8 us)
Async XLA Ops:
  7.2 33.6 %all-gather.3.cloned.1.call-start = ((), (), s32[]{:S(2)}) async-start(), calls=%async_computation.5 | async-start | bytes 1253376 | tf_op jit(solution)/shard_map/all_gather | solution.py:325
  53.2 7.0 %collective-permute-start.4 = (bf16[2,128,256]{2,1,0:T(8,128)(2,1)S(1)}, bf16[2,128,256]{2,1,0:T(8,128)(2,1)S(1)}, u32[]{:S(2)}, u32[]{:S(2)}) collective-permute-start(bf16[2,128,256]{2,1,0:T(8,128)(2,1)S(1)} %get-tuple-element.30), channel_id=1, source_target_pairs={{0,1},{1,2},{2,3},{3,4},{4,5},{5,6},{6,7},{7,0},{8,9},{9,10},{10,1... | collective-permute-start | bytes 393224 | tf_op jit(solution)/shard_map/ppermute | solution.py:33
  61.3 6.5 %collective-permute-start.5 = (bf16[4,128,256]{2,1,0:T(8,128)(2,1)S(1)}, bf16[4,128,256]{2,1,0:T(8,128)(2,1)S(1)}, u32[]{:S(2)}, u32[]{:S(2)}) collective-permute-start(bf16[4,128,256]{2,1,0:T(8,128)(2,1)S(1)} %fusion.4), channel_id=1, source_target_pairs={{0,1},{1,2},{2,3},{3,4},{4,5},{5,6},{6,7},{7,0},{8,9},{9,10},{10,1... | collective-permute-start | bytes 786440 | tf_op jit(solution)/shard_map/ppermute | solution.py:33
  68.9 11.3 %collective-permute-start.6 = (bf16[4,128,256]{2,1,0:T(8,128)(2,1)S(1)}, bf16[4,128,256]{2,1,0:T(8,128)(2,1)S(1)}, u32[]{:S(2)}, u32[]{:S(2)}) collective-permute-start(bf16[4,128,256]{2,1,0:T(8,128)(2,1)S(1)} %fusion.5), channel_id=1, source_target_pairs={{0,1},{1,2},{2,3},{3,4},{4,5},{5,6},{6,7},{7,0},{8,9},{9,10},{10,1... | collective-permute-start | bytes 786440 | tf_op jit(solution)/shard_map/ppermute | solution.py:33
  71.2 15.6 %collective-permute-start.2 = (bf16[8,128,256]{2,1,0:T(8,128)(2,1)S(1)}, bf16[8,128,256]{2,1,0:T(8,128)(2,1)S(1)}, u32[]{:S(2)}, u32[]{:S(2)}) collective-permute-start(bf16[8,128,256]{2,1,0:T(8,128)(2,1)S(1)} %get-tuple-element.27), channel_id=1, source_target_pairs={{0,24},{1,25},{2,26},{3,27},{4,28},{5,29},{6,30},{7,31},{8,0},{9,1... | collective-permute-start | bytes 1572872 | tf_op jit(solution)/shard_map/ppermute | solution.py:33
  77.8 16.2 %collective-permute-start = (bf16[8,128,256]{2,1,0:T(8,128)(2,1)S(1)}, bf16[8,128,256]{2,1,0:T(8,128)(2,1)S(1)}, u32[]{:S(2)}, u32[]{:S(2)}) collective-permute-start(bf16[8,128,256]{2,1,0:T(8,128)(2,1)S(1)} %get-tuple-element.26), channel_id=1, source_target_pairs={{0,8},{1,9},{2,10},{3,11},{4,12},{5,13},{6,14},{7,15},{8,16},{9,17... | collective-permute-start | bytes 1572872 | tf_op jit(solution)/shard_map/ppermute | solution.py:33
  81.5 8.0 %collective-permute-start.9 = (bf16[4,128,256]{2,1,0:T(8,128)(2,1)S(1)}, bf16[4,128,256]{2,1,0:T(8,128)(2,1)S(1)}, u32[]{:S(2)}, u32[]{:S(2)}) collective-permute-start(bf16[4,128,256]{2,1,0:T(8,128)(2,1)S(1)} %get-tuple-element.35), channel_id=1, source_target_pairs={{0,7},{1,0},{2,1},{3,2},{4,3},{5,4},{6,5},{7,6},{8,15},{9,8},{10,9... | collective-permute-start | bytes 786440 | tf_op jit(solution)/shard_map/ppermute | solution.py:33
  86.9 15.1 %collective-permute-start.3 = (bf16[4,128,256]{2,1,0:T(8,128)(2,1)S(1)}, bf16[4,128,256]{2,1,0:T(8,128)(2,1)S(1)}, u32[]{:S(2)}, u32[]{:S(2)}) collective-permute-start(bf16[4,128,256]{2,1,0:T(8,128)(2,1)S(1)} %add_convert_fusion.1), channel_id=1, source_target_pairs={{0,24},{1,25},{2,26},{3,27},{4,28},{5,29},{6,30},{7,31},{8,0},{9,1... | collective-permute-start | bytes 786440 | tf_op jit(solution)/shard_map/ppermute | solution.py:33
  90.6 6.7 %collective-permute-start.10 = (bf16[4,128,256]{2,1,0:T(8,128)(2,1)S(1)}, bf16[4,128,256]{2,1,0:T(8,128)(2,1)S(1)}, u32[]{:S(2)}, u32[]{:S(2)}) collective-permute-start(bf16[4,128,256]{2,1,0:T(8,128)(2,1)S(1)} %fusion.2), channel_id=1, source_target_pairs={{0,7},{1,0},{2,1},{3,2},{4,3},{5,4},{6,5},{7,6},{8,15},{9,8},{10,9... | collective-permute-start | bytes 786440 | tf_op jit(solution)/shard_map/ppermute | solution.py:33
  94.0 8.0 %collective-permute-start.1 = (bf16[4,128,256]{2,1,0:T(8,128)(2,1)S(1)}, bf16[4,128,256]{2,1,0:T(8,128)(2,1)S(1)}, u32[]{:S(2)}, u32[]{:S(2)}) collective-permute-start(bf16[4,128,256]{2,1,0:T(8,128)(2,1)S(1)} %add_convert_fusion.2), channel_id=1, source_target_pairs={{0,8},{1,9},{2,10},{3,11},{4,12},{5,13},{6,14},{7,15},{8,16},{9,17... | collective-permute-start | bytes 786440 | tf_op jit(solution)/shard_map/ppermute | solution.py:33
  94.2 12.6 %collective-permute-start.7 = (bf16[4,128,256]{2,1,0:T(8,128)(2,1)S(1)}, bf16[4,128,256]{2,1,0:T(8,128)(2,1)S(1)}, u32[]{:S(2)}, u32[]{:S(2)}) collective-permute-start(bf16[4,128,256]{2,1,0:T(8,128)(2,1)S(1)} %get-tuple-element.34), channel_id=1, source_target_pairs={{0,1},{1,2},{2,3},{3,4},{4,5},{5,6},{6,7},{7,0},{8,9},{9,10},{10,1... | collective-permute-start | bytes 786440 | tf_op jit(solution)/shard_map/ppermute | solution.py:33
  98.4 8.4 %collective-permute-start.11 = (bf16[4,128,256]{2,1,0:T(8,128)(2,1)S(1)}, bf16[4,128,256]{2,1,0:T(8,128)(2,1)S(1)}, u32[]{:S(2)}, u32[]{:S(2)}) collective-permute-start(bf16[4,128,256]{2,1,0:T(8,128)(2,1)S(1)} %fusion.3), channel_id=1, source_target_pairs={{0,7},{1,0},{2,1},{3,2},{4,3},{5,4},{6,5},{7,6},{8,15},{9,8},{10,9... | collective-permute-start | bytes 786440 | tf_op jit(solution)/shard_map/ppermute | solution.py:33
  103.0 15.9 %all-to-all-start = ((bf16[8,128,256]{2,1,0:T(8,128)(2,1)}), bf16[8,128,256]{2,1,0:T(8,128)(2,1)S(1)}, u32[]{:S(2)}, u32[]{:S(2)}) async-start(bf16[8,128,256]{2,1,0:T(8,128)(2,1)} %add_convert_fusion), calls=%async_computation | async-start | bytes 1048576 | tf_op jit(solution)/shard_map/all_to_all | solution.py:37
  108.1 5.8 %collective-permute-start.13 = (bf16[128,256]{1,0:T(8,128)(2,1)S(1)}, bf16[128,256]{1,0:T(8,128)(2,1)S(1)}, u32[]{:S(2)}, u32[]{:S(2)}) collective-permute-start(bf16[128,256]{1,0:T(8,128)(2,1)S(1)} %get-tuple-element.38), channel_id=1, source_target_pairs={{0,16},{1,17},{2,18},{3,19},{4,20},{5,21},{6,22},{7,23},{8,24},{9,... | collective-permute-start | bytes 196616 | tf_op jit(solution)/shard_map/ppermute | solution.py:33
  120.5 15.9 %all-to-all-start.1 = ((bf16[8,128,256]{2,1,0:T(8,128)(2,1)}), bf16[8,128,256]{2,1,0:T(8,128)(2,1)S(1)}, u32[]{:S(2)}, u32[]{:S(2)}) async-start(bf16[8,128,256]{2,1,0:T(8,128)(2,1)} %broadcast_in_dim.19), calls=%async_computation.1 | async-start | bytes 1048576 | tf_op jit(solution)/shard_map/all_to_all | solution.py:37
  124.3 114.2 %reduce-scatter.2.cloned.1.call-start = ((), (), s32[]{:S(2)}) async-start(), calls=%async_computation.4 | async-start | bytes 2359296 | tf_op jit(solution)/shard_map/reduce_scatter | solution.py:344
  131.7 7.5 %collective-permute-start.22 = (bf16[4,128,256]{2,1,0:T(8,128)(2,1)S(1)}, bf16[4,128,256]{2,1,0:T(8,128)(2,1)S(1)}, u32[]{:S(2)}, u32[]{:S(2)}) collective-permute-start(bf16[4,128,256]{2,1,0:T(8,128)(2,1)S(1)} %pad_maximum_fusion.refs_1_), channel_id=1, source_target_pairs={{0,1},{1,2},{2,3},{3,4},{4,5},{5,6},{6,7},{7,0},{8,9},{9,10},{10,1... | collective-permute-start | bytes 786440 | tf_op jit(solution)/shard_map/ppermute | solution.py:33
  133.0 6.2 %collective-permute-start.23 = (bf16[4,128,256]{2,1,0:T(8,128)(2,1)S(1)}, bf16[4,128,256]{2,1,0:T(8,128)(2,1)S(1)}, u32[]{:S(2)}, u32[]{:S(2)}) collective-permute-start(bf16[4,128,256]{2,1,0:T(8,128)(2,1)S(1)} %pad_maximum_fusion.refs_1_), channel_id=1, source_target_pairs={{0,7},{1,0},{2,1},{3,2},{4,3},{5,4},{6,5},{7,6},{8,15},{9,8},{10,9... | collective-permute-start | bytes 786440 | tf_op jit(solution)/shard_map/ppermute | solution.py:33
  136.4 14.2 %collective-permute-start.18 = (bf16[8,128,256]{2,1,0:T(8,128)(2,1)S(1)}, bf16[8,128,256]{2,1,0:T(8,128)(2,1)S(1)}, u32[]{:S(2)}, u32[]{:S(2)}) collective-permute-start(bf16[8,128,256]{2,1,0:T(8,128)(2,1)S(1)} %all-to-all-done.1.refs_0_), channel_id=1, source_target_pairs={{0,8},{1,9},{2,10},{3,11},{4,12},{5,13},{6,14},{7,15},{8,16},{9,17... | collective-permute-start | bytes 1572872 | tf_op jit(solution)/shard_map/ppermute | solution.py:33
  136.4 14.8 %collective-permute-start.19 = (bf16[8,128,256]{2,1,0:T(8,128)(2,1)S(1)}, bf16[8,128,256]{2,1,0:T(8,128)(2,1)S(1)}, u32[]{:S(2)}, u32[]{:S(2)}) collective-permute-start(bf16[8,128,256]{2,1,0:T(8,128)(2,1)S(1)} %all-to-all-done.1.refs_0_), channel_id=1, source_target_pairs={{0,24},{1,25},{2,26},{3,27},{4,28},{5,29},{6,30},{7,31},{8,0},{9,1... | collective-permute-start | bytes 1572872 | tf_op jit(solution)/shard_map/ppermute | solution.py:33
  139.1 8.8 %collective-permute-start.24 = (bf16[4,128,256]{2,1,0:T(8,128)(2,1)S(1)}, bf16[4,128,256]{2,1,0:T(8,128)(2,1)S(1)}, u32[]{:S(2)}, u32[]{:S(2)}) collective-permute-start(bf16[4,128,256]{2,1,0:T(8,128)(2,1)S(1)} %collective-permute-done.22.refs_6_), channel_id=1, source_target_pairs={{0,1},{1,2},{2,3},{3,4},{4,5},{5,6},{6,7},{7,0},{8,9},{9,10},{10,1... | collective-permute-start | bytes 786440 | tf_op jit(solution)/shard_map/ppermute | solution.py:33
  139.1 8.9 %collective-permute-start.25 = (bf16[4,128,256]{2,1,0:T(8,128)(2,1)S(1)}, bf16[4,128,256]{2,1,0:T(8,128)(2,1)S(1)}, u32[]{:S(2)}, u32[]{:S(2)}) collective-permute-start(bf16[4,128,256]{2,1,0:T(8,128)(2,1)S(1)} %collective-permute-done.23.refs_7_), channel_id=1, source_target_pairs={{0,7},{1,0},{2,1},{3,2},{4,3},{5,4},{6,5},{7,6},{8,15},{9,8},{10,9... | collective-permute-start | bytes 786440 | tf_op jit(solution)/shard_map/ppermute | solution.py:33
  147.9 8.1 %collective-permute-start.26 = (bf16[4,128,256]{2,1,0:T(8,128)(2,1)S(1)}, bf16[4,128,256]{2,1,0:T(8,128)(2,1)S(1)}, u32[]{:S(2)}, u32[]{:S(2)}) collective-permute-start(bf16[4,128,256]{2,1,0:T(8,128)(2,1)S(1)} %collective-permute-done.24.refs_8_), channel_id=1, source_target_pairs={{0,1},{1,2},{2,3},{3,4},{4,5},{5,6},{6,7},{7,0},{8,9},{9,10},{10,1... | collective-permute-start | bytes 786440 | tf_op jit(solution)/shard_map/ppermute | solution.py:33
  148.1 8.3 %collective-permute-start.27 = (bf16[4,128,256]{2,1,0:T(8,128)(2,1)S(1)}, bf16[4,128,256]{2,1,0:T(8,128)(2,1)S(1)}, u32[]{:S(2)}, u32[]{:S(2)}) collective-permute-start(bf16[4,128,256]{2,1,0:T(8,128)(2,1)S(1)} %collective-permute-done.25.refs_9_), channel_id=1, source_target_pairs={{0,7},{1,0},{2,1},{3,2},{4,3},{5,4},{6,5},{7,6},{8,15},{9,8},{10,9... | collective-permute-start | bytes 786440 | tf_op jit(solution)/shard_map/ppermute | solution.py:33
  150.6 12.0 %collective-permute-start.20 = (bf16[4,128,256]{2,1,0:T(8,128)(2,1)S(1)}, bf16[4,128,256]{2,1,0:T(8,128)(2,1)S(1)}, u32[]{:S(2)}, u32[]{:S(2)}) collective-permute-start(bf16[4,128,256]{2,1,0:T(8,128)(2,1)S(1)} %slice.133), channel_id=1, source_target_pairs={{0,8},{1,9},{2,10},{3,11},{4,12},{5,13},{6,14},{7,15},{8,16},{9,17... | collective-permute-start | bytes 786440 | tf_op jit(solution)/shard_map/ppermute | solution.py:33
  151.2 11.4 %collective-permute-start.21 = (bf16[4,128,256]{2,1,0:T(8,128)(2,1)S(1)}, bf16[4,128,256]{2,1,0:T(8,128)(2,1)S(1)}, u32[]{:S(2)}, u32[]{:S(2)}) collective-permute-start(bf16[4,128,256]{2,1,0:T(8,128)(2,1)S(1)} %slice.134), channel_id=1, source_target_pairs={{0,24},{1,25},{2,26},{3,27},{4,28},{5,29},{6,30},{7,31},{8,0},{9,1... | collective-permute-start | bytes 786440 | tf_op jit(solution)/shard_map/ppermute | solution.py:33
  156.0 6.6 %collective-permute-start.28 = (bf16[2,128,256]{2,1,0:T(8,128)(2,1)S(1)}, bf16[2,128,256]{2,1,0:T(8,128)(2,1)S(1)}, u32[]{:S(2)}, u32[]{:S(2)}) collective-permute-start(bf16[2,128,256]{2,1,0:T(8,128)(2,1)S(1)} %slice.135), channel_id=1, source_target_pairs={{0,1},{1,2},{2,3},{3,4},{4,5},{5,6},{6,7},{7,0},{8,9},{9,10},{10,1... | collective-permute-start | bytes 393224 | tf_op jit(solution)/shard_map/ppermute | solution.py:33
  156.4 6.2 %collective-permute-start.29 = (bf16[2,128,256]{2,1,0:T(8,128)(2,1)S(1)}, bf16[2,128,256]{2,1,0:T(8,128)(2,1)S(1)}, u32[]{:S(2)}, u32[]{:S(2)}) collective-permute-start(bf16[2,128,256]{2,1,0:T(8,128)(2,1)S(1)} %slice.136), channel_id=1, source_target_pairs={{0,7},{1,0},{2,1},{3,2},{4,3},{5,4},{6,5},{7,6},{8,15},{9,8},{10,9... | collective-permute-start | bytes 393224 | tf_op jit(solution)/shard_map/ppermute | solution.py:33
  175.6 15.5 %collective-permute-start.30 = (f32[128,256]{1,0:T(8,128)S(1)}, f32[128,256]{1,0:T(8,128)S(1)}, u32[]{:S(2)}, u32[]{:S(2)}) collective-permute-start(f32[128,256]{1,0:T(8,128)S(1)} %dynamic-slice_bitcast_fusion), channel_id=1, source_target_pairs={{0,32},{32,0},{64,96},{96,64},{128,160},{160,128},{192,224},{224,1... | collective-permute-start | bytes 393224 | tf_op jit(solution)/shard_map/ppermute | solution.py:33
  191.4 5.1 %collective-permute-start.33 = (f32[32,256]{1,0:T(8,128)S(1)}, f32[32,256]{1,0:T(8,128)S(1)}, u32[]{:S(2)}, u32[]{:S(2)}) collective-permute-start(f32[32,256]{1,0:T(8,128)S(1)} %get-tuple-element.40), channel_id=1, source_target_pairs={{0,192},{32,224},{64,0},{96,32},{128,64},{160,96},{192,128},{224,1... | collective-permute-start | bytes 98312 | tf_op jit(solution)/shard_map/ppermute | solution.py:33
  197.2 20.7 %all-to-all-start.2 = ((f32[8,32,256]{2,1,0:T(8,128)}), f32[8,32,256]{2,1,0:T(8,128)S(1)}, u32[]{:S(2)}, u32[]{:S(2)}) async-start(f32[8,32,256]{2,1,0:T(8,128)} %broadcast_in_dim.20), calls=%async_computation.3 | async-start | bytes 524288 | tf_op jit(solution)/shard_map/all_to_all | solution.py:37
  229.7 8.0 %collective-permute-start.40 = (f32[128,256]{1,0:T(8,128)S(1)}, f32[128,256]{1,0:T(8,128)S(1)}, u32[]{:S(2)}, u32[]{:S(2)}) collective-permute-start(f32[128,256]{1,0:T(8,128)S(1)} %bitcast.102), channel_id=1, source_target_pairs={{0,32},{32,0},{64,96},{96,64},{128,160},{160,128},{192,224},{224,1... | collective-permute-start | bytes 393224 | tf_op jit(solution)/shard_map/ppermute | solution.py:33
  (20 other events, 182.2 us)
Sparse Core Ops, SparseCore 0:
  10.4 30.3 all-gather.2
  172.5 49.0 reduce-scatter.1

commit v2 on v0

v2 whole, which is shorter than its diff:
```python
import functools

import jax
import jax.numpy as jnp
from jax import lax
from jax.experimental import pallas as pl
from jax.experimental.pallas import tpu as pltpu
from jax.sharding import PartitionSpec as P

X, Z = 4, 8
Y = 4
CHUNK = 16
GROUP = 8
VMEM_MIB = 60


def along_z(d):
    return [(x * Z + z, x * Z + (z + d) % Z) for x in range(X) for z in range(Z)]


def along_x(d):
    return [(x * Z + z, ((x + d) % X) * Z + z) for x in range(X) for z in range(Z)]


def along_y(d):
    return [(y * 2 + c, ((y + d) % Y) * 2 + c) for y in range(Y) for c in range(2)]


def by_core(along):
    return [
        (row * X * Z + a, row * X * Z + b)
        for row in range(2 * Y)
        for a, b in along(1 - 2 * (row % 2))
    ]


OTHER_CORE = [(r, r ^ 1) for r in range(2 * Y)]
Z_GROUPS = [[x * Z + z for z in range(Z)] for x in range(X)]
X_GROUPS = [[x * Z + z for x in range(X)] for z in range(Z)]


def send(value, axis, pairs):
    return lax.ppermute(value, axis, pairs)


def exchange_z(value):
    return lax.all_to_all(value, "col", 0, 0, axis_index_groups=Z_GROUPS)


def exchange_x(value):
    return lax.all_to_all(value, "col", 0, 0, axis_index_groups=X_GROUPS)


def scale_of(degrees):
    scale = lax.rsqrt(degrees.astype(jnp.float32))
    return jnp.transpose(jnp.broadcast_to(scale, (128,) + scale.shape[1:]))


def tile_sums(live, edges_hbm, edges, sems, totals, prepare, product, target):
    chunks = (live + CHUNK - 1) // CHUNK

    def load(chunk):
        part = pl.ds(chunk * CHUNK, CHUNK)
        return pltpu.make_async_copy(edges_hbm.at[part], edges.at[part], sems.at[chunk])

    @pl.loop(0, chunks)
    def _(chunk):
        load(chunk).start()

    for total in totals:
        total[...] = jnp.zeros_like(total)
    prepare()

    @pl.loop(0, chunks)
    def _(chunk):
        load(chunk).wait()
        count = jnp.minimum(live - chunk * CHUNK, CHUNK)

        @pl.loop(0, (count + GROUP - 1) // GROUP)
        def _(step):
            for k in range(GROUP):
                at = chunk * CHUNK + step * GROUP + k
                tile = jnp.where(at < live, edges[at], 0)
                value = product(tile.astype(jnp.float32).astype(jnp.bfloat16), at)
                slot = target(at)
                for half, total in enumerate(totals):
                    total[slot] += value[:, half * 128 : half * 128 + 128]


def forward_kernel(
    deps, meta_ref, scalars_ref, edges_hbm, own_ref, other_ref, weight_ref, *refs
):
    out_ref, panel, left, right, edges, sems = refs[deps:]
    live = scalars_ref[0]
    size = left.shape[1]

    def prepare():
        for block in range(2 * Y):
            ref, dy = (own_ref, other_ref)[block // Y], block % Y
            scale = scale_of(ref[dy, 2 * size :][:1])
            value = jnp.dot(
                ref[dy, : 2 * size], weight_ref[...], preferred_element_type=jnp.float32
            )
            value = value * jnp.concatenate([scale, scale], axis=1)
            panel[pl.ds(2 * block, 2)] = value.astype(jnp.bfloat16).reshape(2, size, -1)

    def product(tile, at):
        return jnp.dot(tile, panel[meta_ref[2, at]], preferred_element_type=jnp.float32)

    tile_sums(
        live, edges_hbm, edges, sems, (left, right), prepare, product,
        lambda at: meta_ref[0, at],
    )
    for slot in range(out_ref.shape[0]):
        out_ref[slot, :, :128] = left[slot].astype(jnp.bfloat16)
        out_ref[slot, :, 128:] = right[slot].astype(jnp.bfloat16)


def backward_kernel(
    places, deps, meta_ref, scalars_ref, edges_hbm, own_ref, other_ref, *refs
):
    pieces = refs[: len(places)]
    (keep_ref, far_ref, left, right, upstream, terms, edges, sems, piece_sems) = refs[
        len(places) + deps :
    ]
    live, row = scalars_ref[0], scalars_ref[1]
    size = left.shape[1]
    copies = [
        pltpu.make_async_copy(piece, upstream.at[pl.ds(at, piece.shape[0])], piece_sems.at[k])
        for k, (piece, at) in enumerate(zip(pieces, places))
    ]
    for copy in copies:
        copy.start()

    def prepare():
        for copy in copies:
            copy.wait()

    def product(tile, at):
        return lax.dot_general(
            tile, upstream[meta_ref[1, at]], (((0,), (0,)), ((), ())),
            preferred_element_type=jnp.float32,
        )

    tile_sums(
        live, edges_hbm, edges, sems, (left, right), prepare, product,
        lambda at: meta_ref[2, at],
    )
    y, core = row // 2, row % 2
    result = None
    for block in range(2 * Y):
        far, dy = block // Y, block % Y
        value = jnp.concatenate(
            [ref[pl.ds(2 * block, 2)].reshape(2 * size, 128) for ref in (left, right)], axis=1
        )
        if far:
            far_ref[dy, : 2 * size] = value.astype(jnp.bfloat16)
        else:
            keep_ref[dy, : 2 * size] = value
        ref = other_ref if far else own_ref
        scale = scale_of(ref[dy, 2 * size :][:1])
        scaled = (value * jnp.concatenate([scale, scale], axis=1)).astype(jnp.bfloat16)
        term = lax.dot_general(
            ref[dy, : 2 * size], scaled, (((0,), (0,)), ((), ())),
            preferred_element_type=jnp.float32,
        )
        result = term if result is None else result + term
    terms[...] = result.reshape(terms.shape)
    for block in range(2 * Y):
        far, dy = block // Y, block % Y
        value = terms[((y + dy) % Y) * 2 + (core + far) % 2]
        if far:
            far_ref[dy, 2 * size :] = value.astype(jnp.bfloat16)
        else:
            keep_ref[dy, 2 * size :] = value


PARAMS = dict(vmem_limit_bytes=VMEM_MIB * 1024 * 1024)
ANY = pl.BlockSpec(memory_space=pl.ANY)
VMEM = pl.BlockSpec(memory_space=pltpu.VMEM)
SMEM = pl.BlockSpec(memory_space=pltpu.SMEM)


def forward(meta, scalars, edges, own, other, weight, deps=()):
    slots, size, _ = edges.shape
    width = weight.shape[-1]
    f32, bf16 = jnp.float32, jnp.bfloat16
    return pl.pallas_call(
        functools.partial(forward_kernel, len(deps)),
        in_specs=[SMEM, SMEM, ANY, VMEM, VMEM, VMEM] + [ANY] * len(deps),
        out_specs=VMEM,
        scratch_shapes=[
            pltpu.VMEM((4 * Y, size, width), bf16),
            pltpu.VMEM((2 * X * Z, size, 128), f32),
            pltpu.VMEM((2 * X * Z, size, 128), f32),
            pltpu.VMEM(edges.shape, edges.dtype),
            pltpu.SemaphoreType.DMA((slots // CHUNK,)),
        ],
        out_shape=jax.ShapeDtypeStruct((2 * X * Z, size, width), bf16),
        compiler_params=pltpu.CompilerParams(**PARAMS),
        cost_estimate=pl.CostEstimate(flops=10**6, bytes_accessed=10**4, transcendentals=0),
        name="forward_tiles",
    )(meta, scalars, edges, own, other, weight, *deps)


def backward(meta, scalars, edges, own, other, pieces, places, deps):
    slots, size, _ = edges.shape
    width = pieces[0].shape[-1]
    rows = 2 * size + width // (2 * Y)
    f32, bf16 = jnp.float32, jnp.bfloat16
    outs = [((Y, rows, width), f32), ((Y, rows, width), bf16)]
    return pl.pallas_call(
        functools.partial(backward_kernel, places, len(deps)),
        in_specs=[SMEM, SMEM, ANY, VMEM, VMEM] + [ANY] * len(pieces + deps),
        out_specs=[VMEM] * len(outs),
        scratch_shapes=[
            pltpu.VMEM((4 * Y, size, 128), f32),
            pltpu.VMEM((4 * Y, size, 128), f32),
            pltpu.VMEM((2 * X * Z, size, width), bf16),
            pltpu.VMEM((2 * Y, width // (2 * Y), width), f32),
            pltpu.VMEM(edges.shape, edges.dtype),
            pltpu.SemaphoreType.DMA((slots // CHUNK,)),
            pltpu.SemaphoreType.DMA((len(pieces),)),
        ],
        out_shape=[jax.ShapeDtypeStruct(shape, dtype) for shape, dtype in outs],
        compiler_params=pltpu.CompilerParams(**PARAMS),
        cost_estimate=pl.CostEstimate(flops=10**6, bytes_accessed=10**4, transcendentals=0),
        name="backward_tiles",
    )(meta, scalars, edges, own, other, *pieces, *deps)


def gather_col(own, size, core):
    line = jnp.concatenate(
        [
            own,
            send(own, "col", along_x(-1)),
            send(own, "col", along_x(2)),
            send(own, "col", along_x(1)),
        ]
    ).reshape(2 * X, size, -1)
    places = [(line, 0)]
    up = down = line
    for k in range(1, 4):
        up = send(up, "col", along_z(1))
        down = send(down, "col", along_z(-1))
        places += [(up, 8 * (8 - k)), (down, 8 * k)]
    far = send(jnp.where(core == 0, up, down), ("row", "col"), by_core(along_z))
    places += [(far, 8 * 4)]
    return [piece for piece, _ in places], [at for _, at in places]


def gather_row(own):
    mine = jnp.stack(
        [
            own,
            send(own, "row", along_y(-1)),
            send(own, "row", along_y(2)),
            send(own, "row", along_y(1)),
        ]
    )
    return mine, send(mine, "row", OTHER_CORE)


def fold_cores_kernel(keep, recv, *outs):
    for d in range(Y):
        value = keep[d] + recv[d].astype(jnp.float32)
        outs[d][...] = value.astype(outs[d].dtype)


def scatter_row(keep, far):
    recv = send(far, "row", OTHER_CORE)
    shape = keep.shape[1:]
    own, *parts = pl.pallas_call(
        fold_cores_kernel,
        out_shape=[jax.ShapeDtypeStruct(shape, jnp.float32)]
        + [jax.ShapeDtypeStruct(shape, jnp.bfloat16)] * (Y - 1),
        name="fold_cores",
    )(keep, recv)
    return own + sum(
        send(part, "row", along_y(d)).astype(jnp.float32) for d, part in enumerate(parts, 1)
    )


def all_rows(value, y, core):
    got = jnp.stack([value] + [send(value, "row", along_y(d)) for d in range(1, Y)])
    mine = jnp.take(got, (y - jnp.arange(Y, dtype=jnp.int32)) % Y, axis=0)
    other = send(mine, "row", OTHER_CORE)
    pair = jnp.where(core == 0, jnp.stack([mine, other], 1), jnp.stack([other, mine], 1))
    return pair.reshape(-1, value.shape[-1])


def sum_col(value, bits):
    for bit in bits:
        value = value + send(value, "col", [(a, a ^ bit) for a in range(X * Z)])
    return value


def shards(features, weight, tile_coords, tile_live, tile_edges, row_degree, col_degree, cotangent):
    f32, bf16 = jnp.float32, jnp.bfloat16
    size = tile_edges.shape[-1]
    nodes, width = features.shape
    row_scale = lax.rsqrt(row_degree.astype(f32))
    col_scale = lax.rsqrt(col_degree.astype(f32))
    coords = tile_coords[0, 0]
    edges = tile_edges[0, 0]
    row, col = lax.axis_index("row"), lax.axis_index("col")
    y, core = row // 2, row % 2

    upstream = (row_scale[:, None] * cotangent.astype(f32)).astype(bf16)
    pieces, places = gather_col(upstream, size, core)

    degrees = jnp.zeros((16, width), bf16).at[0].set(col_degree.astype(bf16))
    mine, other = gather_row(jnp.concatenate([features, degrees]))

    owner, half = coords[:, 0] // 2, coords[:, 0] % 2
    dx = (owner // Z - col // Z) % X
    dz = (owner % Z - col % Z) % Z
    back_row = (dz * X + dx) * 2 + half
    col_owner, half = coords[:, 1] // 2, coords[:, 1] % 2
    column = ((col_owner + core) % 2 * Y + (col_owner // 2 - y) % Y) * 2 + half
    meta = jnp.stack([coords[:, 0], back_row, column]).astype(jnp.int32)
    scalars = jnp.stack([tile_live[0, 0], row]).astype(jnp.int32)

    first = forward(meta, scalars, edges, mine, other, weight, pieces[:1])
    first, *pieces[1:3] = lax.optimization_barrier((first, *pieces[1:3]))
    from_x = exchange_x(first.reshape(X, Z * nodes, width))
    from_x, pieces[-1] = lax.optimization_barrier((from_x, pieces[-1]))
    plane = jnp.sum(from_x.astype(f32), axis=0).astype(bf16)
    from_z = exchange_z(plane.reshape(Z, nodes, width))
    keep, far = backward(meta, scalars, edges, mine, other, pieces, places, [plane])
    back = scatter_row(keep, far)
    terms = sum_col(back[nodes:], (Z, 2 * Z))
    terms, from_z = lax.optimization_barrier((terms, from_z))
    grad_weight = all_rows(sum_col(terms, (1, 2, 4)), y, core)

    summed = jnp.sum(from_z.astype(f32), axis=0)
    aggregated = (row_scale[:, None] * summed).astype(bf16)

    grad_panel = (col_scale[:, None] * back[:nodes]).astype(bf16)
    grad_features = jnp.dot(grad_panel, weight.T, preferred_element_type=f32).astype(bf16)
    return aggregated, grad_features, grad_weight


def solution(mesh):
    in_specs = (
        P(("col", "row"), None),
        P(),
        P("row", "col", None, None),
        P("row", "col"),
        P("row", "col", None, None, None),
        P(("row", "col")),
        P(("col", "row")),
        P(("row", "col"), None),
    )
    out_specs = (P(("row", "col"), None), P(("col", "row"), None), P())
    return jax.shard_map(shards, mesh=mesh, in_specs=in_specs, out_specs=out_specs, check_vma=False)
```

time: 773 us -> 168 us (0.22)
  waiting for transfers between devices: 624 us -> 61.7 us
  starting transfers between devices: 0.21 us -> 64.1 us
  other arithmetic: 73.8 us -> 11.7 us
  matrix products: 33.3 us -> 0.88 us
  Pallas kernels: 0 us -> 23.4 us
  local copies, waits for them, and re-layouts: 25.9 us -> 3.65 us
  between operations: 14.5 us -> 1.53 us
    reduce_scatter x2 -> x0, waiting for transfers between devices: 258 us -> none  [the longest x1 225 us: shards(): lax.psum_scatter(partial_value, 'col', scatter_dimension=0, tiled=True)]
    psum x1 -> x0, waiting for transfers between devices: 253 us -> none  [shards(): grad_weight = lax.psum(weight_terms, ('row', 'col'))]
    all_gather x2 -> x0, waiting for transfers between devices: 112 us -> none  [the longest x1 83.1 us: shards(): row_panel = lax.all_gather(upstream, 'col', axis=0, tiled=True)]
    scatter-add x2 -> x0, other arithmetic: 70.5 us -> none  [tile_products(): totals = empty.at[target_index].add(products)]
    ppermute x0 -> x27, waiting for transfers between devices: none -> 52.8 us  [send(): return lax.ppermute(value, axis, pairs)]
    ppermute x0 -> x27, starting transfers between devices: none -> 50.8 us  [send(): return lax.ppermute(value, axis, pairs)]
    dot_general x5 -> x1, matrix products: 33.3 us -> 0.88 us  [shards(): jnp.dot(grad_panel, weight.T, preferred_element_type=f32).astype(bf16)]
    pallas_call x0 -> x3, Pallas kernels: none -> 23.4 us  [the longest x1 11.3 us: backward(): pl.pallas_call(functools.partial(backward_kernel, places, len(deps)), in_...]
  transfers between devices with their start and end apart: 5 -> 29, of which waited for: 5 -> 17; matrix products, arithmetic and copies ran while one was open for 0% -> 4% of each run, Pallas kernels for 0% -> 14%
where the time goes in v2:
time: 168 us; the launch traced here: 167 us
  starting transfers between devices  64.1 us (38%)
  waiting for transfers between devices  61.7 us (37%)
  Pallas kernels  23.4 us (14%)
  other arithmetic  11.7 us (7%)
  local copies, waits for them, and re-layouts  3.65 us (2%)
    ppermute x27, waiting for transfers between devices, send(): return lax.ppermute(value, axis, pairs)  52.8 us
    ppermute x27, starting transfers between devices, send(): return lax.ppermute(value, axis, pairs)  50.8 us
    pallas_call x1, Pallas kernels, backward(): pl.pallas_call(functools.partial(backward_kernel, places, len(deps)), in_...  11.3 us
    pallas_call x1, Pallas kernels, forward(): pl.pallas_call(functools.partial(forward_kernel, len(deps)), in_specs=[SM...  9.81 us
    all_to_all x1, waiting for transfers between devices, exchange_x(): return lax.all_to_all(value, 'col', 0, 0, axis_index_groups=X_GROUPS)  8.88 us
    all_to_all x1, starting transfers between devices, exchange_z(): return lax.all_to_all(value, 'col', 0, 0, axis_index_groups=Z_GROUPS)  8.46 us
    all_to_all x1, starting transfers between devices, exchange_x(): return lax.all_to_all(value, 'col', 0, 0, axis_index_groups=X_GROUPS)  4.89 us
    reduce_sum x1, other arithmetic, shards(): plane = jnp.sum(from_x.astype(f32), axis=0).astype(bf16)  4.08 us
  transfers between devices with their start and end apart: 29, of which 17 were waited for; matrix products, arithmetic and copies ran while one was open for 4% of the time, Pallas kernels for 14%

profile of v2, /device:TPU:1, one launch (start us, length us, event | category | flops | bytes accessed | tf_op | source)
XLA Modules:
  0.0 167.0 jit_solution(12251922455306418793)
XLA Ops:
  2.3 3.4 %collective-permute-start.4 = (bf16[256,256]{1,0:T(8,128)(2,1)S(1)}, bf16[256,256]{1,0:T(8,128)(2,1)S(1)}, u32[]{:S(2)}, u32[]{:S(2)}) collective-permute-start(bf16[256,256]{1,0:T(8,128)(2,1)S(1)} %multiply_convert_fusion.1), channel_id=1, source_target_pairs={{0,24},{1,25},{2,26},{3,27},{4,28},{5,29},{6,30},{7,31},{8,0},{9,1... | collective-permute-start | bytes 393224 | tf_op jit(solution)/shard_map/ppermute | solution.py:43
  8.5 2.8 %collective-permute-start = (bf16[272,256]{1,0:T(8,128)(2,1)S(1)}, bf16[272,256]{1,0:T(8,128)(2,1)S(1)}, u32[]{:S(2)}, u32[]{:S(2)}) collective-permute-start(bf16[272,256]{1,0:T(8,128)(2,1)S(1)} %get-tuple-element.42), channel_id=1, source_target_pairs={{0,192},{32,224},{64,0},{96,32},{128,64},{160,96},{192,128},{224,1... | collective-permute-start | bytes 417800 | tf_op jit(solution)/shard_map/ppermute | solution.py:43
  13.6 1.6 collective-permute-done.6
  15.3 1.7 %collective-permute-start.7 = (bf16[8,128,256]{2,1,0:T(8,128)(2,1)S(1)}, bf16[8,128,256]{2,1,0:T(8,128)(2,1)S(1)}, u32[]{:S(2)}, u32[]{:S(2)}) collective-permute-start(bf16[8,128,256]{2,1,0:T(8,128)(2,1)S(1)} %bitcast.35), channel_id=1, source_target_pairs={{0,1},{1,2},{2,3},{3,4},{4,5},{5,6},{6,7},{7,0},{8,9},{9,10},{10,1... | collective-permute-start | bytes 1572872 | tf_op jit(solution)/shard_map/ppermute | solution.py:43
  17.0 4.0 %collective-permute-start.8 = (bf16[8,128,256]{2,1,0:T(8,128)(2,1)S(1)}, bf16[8,128,256]{2,1,0:T(8,128)(2,1)S(1)}, u32[]{:S(2)}, u32[]{:S(2)}) collective-permute-start(bf16[8,128,256]{2,1,0:T(8,128)(2,1)S(1)} %bitcast.36), channel_id=1, source_target_pairs={{0,7},{1,0},{2,1},{3,2},{4,3},{5,4},{6,5},{7,6},{8,15},{9,8},{10,9... | collective-permute-start | bytes 1572872 | tf_op jit(solution)/shard_map/ppermute | solution.py:43
  25.2 9.8 %forward_tiles.1 = bf16[64,128,256]{2,1,0:T(8,128)(2,1)} custom-call(s32[3,144]{1,0:T(4,128)} %pad_add_fusion.meta_ref, s32[2]{0:T(128)} %pad_add_fusion.1.scalars_ref, s32[144,128,128]{2,1,0:T(8,128)} %bitcast.32, bf16[4,272,256]{2,1,0:T(8,128)(2,1)} %copy-done, bf16[4,272,256]{2,1,0:T(8,128)(2,1)} %copy-done.2, bf16[256,256]{1,0:T(8,128)(2,1)} %weight_ref.1, ...), custom_call_target="tpu_custom_call" | custom-call | flops 1000000 | bytes 10000 | tf_op jit(solution)/shard_map/forward_tiles/pallas_call | solution.py:188
  35.0 4.9 %all-to-all-start = ((bf16[4,2048,256]{2,1,0:T(8,128)(2,1)}), bf16[4,2048,256]{2,1,0:T(8,128)(2,1)}, u32[]{:S(2)}, u32[]{:S(2)}) async-start(bf16[4,2048,256]{2,1,0:T(8,128)(2,1)} %bitcast.34), calls=%async_computation | async-start | bytes 8388608 | tf_op jit(solution)/shard_map/all_to_all | solution.py:51
  39.9 1.5 collective-permute-start.9
  41.4 3.3 %collective-permute-start.10 = (bf16[8,128,256]{2,1,0:T(8,128)(2,1)S(1)}, bf16[8,128,256]{2,1,0:T(8,128)(2,1)S(1)}, u32[]{:S(2)}, u32[]{:S(2)}) collective-permute-start(bf16[8,128,256]{2,1,0:T(8,128)(2,1)S(1)} %collective-permute-done.8.refs_2_), channel_id=1, source_target_pairs={{0,7},{1,0},{2,1},{3,2},{4,3},{5,4},{6,5},{7,6},{8,15},{9,8},{10,9... | collective-permute-start | bytes 1572872 | tf_op jit(solution)/shard_map/ppermute | solution.py:43
  44.7 12.0 %collective-permute-done.9.refs_3_ = bf16[8,128,256]{2,1,0:T(8,128)(2,1)S(1)} collective-permute-done((bf16[8,128,256]{2,1,0:T(8,128)(2,1)S(1)}, bf16[8,128,256]{2,1,0:T(8,128)(2,1)S(1)}, u32[]{:S(2)}, u32[]{:S(2)}) %collective-permute-start.9) | collective-permute-done | bytes 524320 | tf_op jit(solution)/shard_map/ppermute | solution.py:43
  56.8 2.7 %collective-permute-start.12 = (bf16[8,128,256]{2,1,0:T(8,128)(2,1)S(1)}, bf16[8,128,256]{2,1,0:T(8,128)(2,1)S(1)}, u32[]{:S(2)}, u32[]{:S(2)}) collective-permute-start(bf16[8,128,256]{2,1,0:T(8,128)(2,1)S(1)} %collective-permute-done.10.refs_4_), channel_id=1, source_target_pairs={{0,7},{1,0},{2,1},{3,2},{4,3},{5,4},{6,5},{7,6},{8,15},{9,8},{10,9... | collective-permute-start | bytes 1572872 | tf_op jit(solution)/shard_map/ppermute | solution.py:43
  59.5 11.3 %collective-permute-done.11.refs_5_ = bf16[8,128,256]{2,1,0:T(8,128)(2,1)S(1)} collective-permute-done((bf16[8,128,256]{2,1,0:T(8,128)(2,1)S(1)}, bf16[8,128,256]{2,1,0:T(8,128)(2,1)S(1)}, u32[]{:S(2)}, u32[]{:S(2)}) %collective-permute-start.11) | collective-permute-done | bytes 524320 | tf_op jit(solution)/shard_map/ppermute | solution.py:43
  70.9 2.6 %collective-permute-start.13 = (bf16[8,128,256]{2,1,0:T(8,128)(2,1)S(1)}, bf16[8,128,256]{2,1,0:T(8,128)(2,1)S(1)}, u32[]{:S(2)}, u32[]{:S(2)}) collective-permute-start(bf16[8,128,256]{2,1,0:T(8,128)(2,1)S(1)} %broadcast_select_fusion), channel_id=1, source_target_pairs={{0,1},{1,2},{2,3},{3,4},{4,5},{5,6},{6,7},{7,0},{8,9},{9,10},{10,1... | collective-permute-start | bytes 1572872 | tf_op jit(solution)/shard_map/ppermute | solution.py:43
  73.5 6.1 %collective-permute-done.13.refs_7_ = bf16[8,128,256]{2,1,0:T(8,128)(2,1)S(1)} collective-permute-done((bf16[8,128,256]{2,1,0:T(8,128)(2,1)S(1)}, bf16[8,128,256]{2,1,0:T(8,128)(2,1)S(1)}, u32[]{:S(2)}, u32[]{:S(2)}) %collective-permute-start.13) | collective-permute-done | bytes 524320 | tf_op jit(solution)/shard_map/ppermute | solution.py:43
  79.6 8.9 %all-to-all-done = bf16[4,2048,256]{2,1,0:T(8,128)(2,1)} async-done(((bf16[4,2048,256]{2,1,0:T(8,128)(2,1)}), bf16[4,2048,256]{2,1,0:T(8,128)(2,1)}, u32[]{:S(2)}, u32[]{:S(2)}) %all-to-all-start) | async-done | bytes 4194336 | tf_op jit(solution)/shard_map/all_to_all | solution.py:51
  88.5 4.1 %reduce_sum.21.refs_8_ = bf16[2048,256]{1,0:T(8,128)(2,1)} reduce(bf16[4,2048,256]{2,1,0:T(8,128)(2,1)} %all-to-all-done, bf16[]{:T(256)} %constant.179.clone.1), dimensions={0}, to_apply=%region_0.1 | reduce | flops 1572864 | bytes 5242882 | tf_op jit(solution)/shard_map/reduce_sum | solution.py:328
  92.6 8.5 %all-to-all-start.1 = ((bf16[8,256,256]{2,1,0:T(8,128)(2,1)}), bf16[8,256,256]{2,1,0:T(8,128)(2,1)S(1)}, u32[]{:S(2)}, u32[]{:S(2)}) async-start(bf16[8,256,256]{2,1,0:T(8,128)(2,1)} %bitcast.12), calls=%async_computation.1 | async-start | bytes 2097152 | tf_op jit(solution)/shard_map/all_to_all | solution.py:47
  101.1 11.3 %backward_tiles.1 = (f32[4,288,256]{2,1,0:T(8,128)}, bf16[4,288,256]{2,1,0:T(8,128)(2,1)}) custom-call(s32[3,144]{1,0:T(4,128)} %pad_add_fusion.meta_ref, s32[2]{0:T(128)} %pad_add_fusion.1.scalars_ref, s32[144,128,128]{2,1,0:T(8,128)} %bitcast.33, bf16[4,272,256]{2,1,0:T(8,128)(2,1)} %copy-done, bf16[4,272,256]{2,1,0:T(8,128)(2,1)} %copy-done.2, ...), custom_call_target="tpu_custom_call" | custom-call | flops 1000000 | bytes 10000 | tf_op jit(solution)/shard_map/backward_tiles/pallas_call | solution.py:212
  112.5 2.2 %collective-permute-done.14.recv = bf16[4,288,256]{2,1,0:T(8,128)(2,1)S(1)} collective-permute-done((bf16[4,288,256]{2,1,0:T(8,128)(2,1)}, bf16[4,288,256]{2,1,0:T(8,128)(2,1)S(1)}, u32[]{:S(2)}, u32[]{:S(2)}) %collective-permute-start.14) | collective-permute-done | bytes 589856 | tf_op jit(solution)/shard_map/ppermute | solution.py:43
  115.5 2.3 %fold_cores.1 = (f32[288,256]{1,0:T(8,128)}, bf16[288,256]{1,0:T(8,128)(2,1)}, bf16[288,256]{1,0:T(8,128)(2,1)}, bf16[288,256]{1,0:T(8,128)(2,1)}) custom-call(f32[4,288,256]{2,1,0:T(8,128)} %get-tuple-element.33.keep, bf16[4,288,256]{2,1,0:T(8,128)(2,1)} %copy-done.5), custom_call_target="tpu_custom_call" | custom-call | tf_op jit(solution)/shard_map/fold_cores/pallas_call | solution.py:273
  117.8 2.8 %collective-permute-start.16 = (bf16[288,256]{1,0:T(8,128)(2,1)}, bf16[288,256]{1,0:T(8,128)(2,1)S(1)}, u32[]{:S(2)}, u32[]{:S(2)}) collective-permute-start(bf16[288,256]{1,0:T(8,128)(2,1)} %get-tuple-element.37), channel_id=1, source_target_pairs={{0,128},{32,160},{64,192},{96,224},{128,0},{160,32},{192,64},{224,... | collective-permute-start | bytes 442376 | tf_op jit(solution)/shard_map/ppermute | solution.py:43
  120.6 4.0 %collective-permute-done.15 = bf16[288,256]{1,0:T(8,128)(2,1)S(1)} collective-permute-done((bf16[288,256]{1,0:T(8,128)(2,1)}, bf16[288,256]{1,0:T(8,128)(2,1)S(1)}, u32[]{:S(2)}, u32[]{:S(2)}) %collective-permute-start.15) | collective-permute-done | bytes 147488 | tf_op jit(solution)/shard_map/ppermute | solution.py:43
  124.7 2.9 %collective-permute-done.16 = bf16[288,256]{1,0:T(8,128)(2,1)S(1)} collective-permute-done((bf16[288,256]{1,0:T(8,128)(2,1)}, bf16[288,256]{1,0:T(8,128)(2,1)S(1)}, u32[]{:S(2)}, u32[]{:S(2)}) %collective-permute-start.16) | collective-permute-done | bytes 147488 | tf_op jit(solution)/shard_map/ppermute | solution.py:43
  130.2 1.7 %collective-permute-done.18 = f32[32,256]{1,0:T(8,128)S(1)} collective-permute-done((f32[32,256]{1,0:T(8,128)S(1)}, f32[32,256]{1,0:T(8,128)S(1)}, u32[]{:S(2)}, u32[]{:S(2)}) %collective-permute-start.18) | collective-permute-done | bytes 32800 | tf_op jit(solution)/shard_map/ppermute | solution.py:43
  132.7 3.5 %collective-permute-done.19 = f32[32,256]{1,0:T(8,128)S(1)} collective-permute-done((f32[32,256]{1,0:T(8,128)S(1)}, f32[32,256]{1,0:T(8,128)S(1)}, u32[]{:S(2)}, u32[]{:S(2)}) %collective-permute-start.19) | collective-permute-done | bytes 32800 | tf_op jit(solution)/shard_map/ppermute | solution.py:43
  136.2 1.5 collective-permute-start.20
  137.8 1.6 collective-permute-done.20
  139.4 2.7 %collective-permute-start.21 = (f32[32,256]{1,0:T(8,128)S(1)}, f32[32,256]{1,0:T(8,128)S(1)}, u32[]{:S(2)}, u32[]{:S(2)}) collective-permute-start(f32[32,256]{1,0:T(8,128)S(1)} %add.255), channel_id=1, source_target_pairs={{0,2},{1,3},{2,0},{3,1},{4,6},{5,7},{6,4},{7,5},{8,10},{9,11},{10,... | collective-permute-start | bytes 98312 | tf_op jit(solution)/shard_map/ppermute | solution.py:43
  143.4 4.7 %collective-permute-start.22 = (f32[32,256]{1,0:T(8,128)S(1)}, f32[32,256]{1,0:T(8,128)S(1)}, u32[]{:S(2)}, u32[]{:S(2)}) collective-permute-start(f32[32,256]{1,0:T(8,128)S(1)} %add.256), channel_id=1, source_target_pairs={{0,4},{1,5},{2,6},{3,7},{4,0},{5,1},{6,2},{7,3},{8,12},{9,13},{10,... | collective-permute-start | bytes 98312 | tf_op jit(solution)/shard_map/ppermute | solution.py:43
  148.3 1.8 %collective-permute-done.22 = f32[32,256]{1,0:T(8,128)S(1)} collective-permute-done((f32[32,256]{1,0:T(8,128)S(1)}, f32[32,256]{1,0:T(8,128)S(1)}, u32[]{:S(2)}, u32[]{:S(2)}) %collective-permute-start.22) | collective-permute-done | bytes 32800 | tf_op jit(solution)/shard_map/ppermute | solution.py:43
  151.3 2.7 %collective-permute-start.24 = (f32[32,256]{1,0:T(8,128)S(1)}, f32[32,256]{1,0:T(8,128)S(1)}, u32[]{:S(2)}, u32[]{:S(2)}) collective-permute-start(f32[32,256]{1,0:T(8,128)S(1)} %add.257), channel_id=1, source_target_pairs={{0,128},{32,160},{64,192},{96,224},{128,0},{160,32},{192,64},{224,... | collective-permute-start | bytes 98312 | tf_op jit(solution)/shard_map/ppermute | solution.py:43
  157.5 7.8 %collective-permute-start.26 = (f32[4,32,256]{2,1,0:T(8,128)S(1)}, f32[4,32,256]{2,1,0:T(8,128)S(1)}, u32[]{:S(2)}, u32[]{:S(2)}) collective-permute-start(f32[4,32,256]{2,1,0:T(8,128)S(1)} %broadcast_select_fusion.1), channel_id=1, source_target_pairs={{0,32},{32,0},{64,96},{96,64},{128,160},{160,128},{192,224},{224,1... | collective-permute-start | bytes 393224 | tf_op jit(solution)/shard_map/ppermute | solution.py:43
  (88 shorter events, 22.5 us)
Async XLA Ops:
  2.3 9.9 %collective-permute-start.4 = (bf16[256,256]{1,0:T(8,128)(2,1)S(1)}, bf16[256,256]{1,0:T(8,128)(2,1)S(1)}, u32[]{:S(2)}, u32[]{:S(2)}) collective-permute-start(bf16[256,256]{1,0:T(8,128)(2,1)S(1)} %multiply_convert_fusion.1), channel_id=1, source_target_pairs={{0,24},{1,25},{2,26},{3,27},{4,28},{5,29},{6,30},{7,31},{8,0},{9,1... | collective-permute-start | bytes 393224 | tf_op jit(solution)/shard_map/ppermute | solution.py:43
  5.7 7.9 %collective-permute-start.5 = (bf16[256,256]{1,0:T(8,128)(2,1)S(1)}, bf16[256,256]{1,0:T(8,128)(2,1)S(1)}, u32[]{:S(2)}, u32[]{:S(2)}) collective-permute-start(bf16[256,256]{1,0:T(8,128)(2,1)S(1)} %multiply_convert_fusion.1), channel_id=1, source_target_pairs={{0,16},{1,17},{2,18},{3,19},{4,20},{5,21},{6,22},{7,23},{8,24},{9,... | collective-permute-start | bytes 393224 | tf_op jit(solution)/shard_map/ppermute | solution.py:43
  6.2 9.0 %collective-permute-start.6 = (bf16[256,256]{1,0:T(8,128)(2,1)S(1)}, bf16[256,256]{1,0:T(8,128)(2,1)S(1)}, u32[]{:S(2)}, u32[]{:S(2)}) collective-permute-start(bf16[256,256]{1,0:T(8,128)(2,1)S(1)} %multiply_convert_fusion.1), channel_id=1, source_target_pairs={{0,8},{1,9},{2,10},{3,11},{4,12},{5,13},{6,14},{7,15},{8,16},{9,17... | collective-permute-start | bytes 393224 | tf_op jit(solution)/shard_map/ppermute | solution.py:43
  8.5 12.6 %collective-permute-start = (bf16[272,256]{1,0:T(8,128)(2,1)S(1)}, bf16[272,256]{1,0:T(8,128)(2,1)S(1)}, u32[]{:S(2)}, u32[]{:S(2)}) collective-permute-start(bf16[272,256]{1,0:T(8,128)(2,1)S(1)} %get-tuple-element.42), channel_id=1, source_target_pairs={{0,192},{32,224},{64,0},{96,32},{128,64},{160,96},{192,128},{224,1... | collective-permute-start | bytes 417800 | tf_op jit(solution)/shard_map/ppermute | solution.py:43
  11.3 9.8 %collective-permute-start.1 = (bf16[272,256]{1,0:T(8,128)(2,1)S(1)}, bf16[272,256]{1,0:T(8,128)(2,1)S(1)}, u32[]{:S(2)}, u32[]{:S(2)}) collective-permute-start(bf16[272,256]{1,0:T(8,128)(2,1)S(1)} %get-tuple-element.42), channel_id=1, source_target_pairs={{0,128},{32,160},{64,192},{96,224},{128,0},{160,32},{192,64},{224,... | collective-permute-start | bytes 417800 | tf_op jit(solution)/shard_map/ppermute | solution.py:43
  12.3 8.8 %collective-permute-start.2 = (bf16[272,256]{1,0:T(8,128)(2,1)S(1)}, bf16[272,256]{1,0:T(8,128)(2,1)S(1)}, u32[]{:S(2)}, u32[]{:S(2)}) collective-permute-start(bf16[272,256]{1,0:T(8,128)(2,1)S(1)} %get-tuple-element.42), channel_id=1, source_target_pairs={{0,64},{32,96},{64,128},{96,160},{128,192},{160,224},{192,0},{224,... | collective-permute-start | bytes 417800 | tf_op jit(solution)/shard_map/ppermute | solution.py:43
  15.3 19.7 %collective-permute-start.7 = (bf16[8,128,256]{2,1,0:T(8,128)(2,1)S(1)}, bf16[8,128,256]{2,1,0:T(8,128)(2,1)S(1)}, u32[]{:S(2)}, u32[]{:S(2)}) collective-permute-start(bf16[8,128,256]{2,1,0:T(8,128)(2,1)S(1)} %bitcast.35), channel_id=1, source_target_pairs={{0,1},{1,2},{2,3},{3,4},{4,5},{5,6},{6,7},{7,0},{8,9},{9,10},{10,1... | collective-permute-start | bytes 1572872 | tf_op jit(solution)/shard_map/ppermute | solution.py:43
  17.0 18.0 %collective-permute-start.8 = (bf16[8,128,256]{2,1,0:T(8,128)(2,1)S(1)}, bf16[8,128,256]{2,1,0:T(8,128)(2,1)S(1)}, u32[]{:S(2)}, u32[]{:S(2)}) collective-permute-start(bf16[8,128,256]{2,1,0:T(8,128)(2,1)S(1)} %bitcast.36), channel_id=1, source_target_pairs={{0,7},{1,0},{2,1},{3,2},{4,3},{5,4},{6,5},{7,6},{8,15},{9,8},{10,9... | collective-permute-start | bytes 1572872 | tf_op jit(solution)/shard_map/ppermute | solution.py:43
  21.1 3.2 %collective-permute-start.3 = (bf16[4,272,256]{2,1,0:T(8,128)(2,1)S(1)}, bf16[4,272,256]{2,1,0:T(8,128)(2,1)S(1)}, u32[]{:S(2)}, u32[]{:S(2)}) collective-permute-start(bf16[4,272,256]{2,1,0:T(8,128)(2,1)S(1)} %pad_maximum_fusion.own_ref), channel_id=1, source_target_pairs={{0,32},{32,0},{64,96},{96,64},{128,160},{160,128},{192,224},{224,1... | collective-permute-start | bytes 1671176 | tf_op jit(solution)/shard_map/ppermute | solution.py:43
  35.0 53.5 %all-to-all-start = ((bf16[4,2048,256]{2,1,0:T(8,128)(2,1)}), bf16[4,2048,256]{2,1,0:T(8,128)(2,1)}, u32[]{:S(2)}, u32[]{:S(2)}) async-start(bf16[4,2048,256]{2,1,0:T(8,128)(2,1)} %bitcast.34), calls=%async_computation | async-start | bytes 8388608 | tf_op jit(solution)/shard_map/all_to_all | solution.py:51
  39.9 16.9 %collective-permute-start.9 = (bf16[8,128,256]{2,1,0:T(8,128)(2,1)S(1)}, bf16[8,128,256]{2,1,0:T(8,128)(2,1)S(1)}, u32[]{:S(2)}, u32[]{:S(2)}) collective-permute-start(bf16[8,128,256]{2,1,0:T(8,128)(2,1)S(1)} %collective-permute-done.7.refs_1_), channel_id=1, source_target_pairs={{0,1},{1,2},{2,3},{3,4},{4,5},{5,6},{6,7},{7,0},{8,9},{9,10},{10,1... | collective-permute-start | bytes 1572872 | tf_op jit(solution)/shard_map/ppermute | solution.py:43
  41.4 15.4 %collective-permute-start.10 = (bf16[8,128,256]{2,1,0:T(8,128)(2,1)S(1)}, bf16[8,128,256]{2,1,0:T(8,128)(2,1)S(1)}, u32[]{:S(2)}, u32[]{:S(2)}) collective-permute-start(bf16[8,128,256]{2,1,0:T(8,128)(2,1)S(1)} %collective-permute-done.8.refs_2_), channel_id=1, source_target_pairs={{0,7},{1,0},{2,1},{3,2},{4,3},{5,4},{6,5},{7,6},{8,15},{9,8},{10,9... | collective-permute-start | bytes 1572872 | tf_op jit(solution)/shard_map/ppermute | solution.py:43
  56.8 35.8 %copy-start.9 = (bf16[8,128,256]{2,1,0:T(8,128)(2,1)}, bf16[8,128,256]{2,1,0:T(8,128)(2,1)S(1)}, u32[]{:S(2)}) copy-start(bf16[8,128,256]{2,1,0:T(8,128)(2,1)S(1)} %collective-permute-done.9.refs_3_) | copy-start | bytes 1572868
  56.8 14.0 %collective-permute-start.11 = (bf16[8,128,256]{2,1,0:T(8,128)(2,1)S(1)}, bf16[8,128,256]{2,1,0:T(8,128)(2,1)S(1)}, u32[]{:S(2)}, u32[]{:S(2)}) collective-permute-start(bf16[8,128,256]{2,1,0:T(8,128)(2,1)S(1)} %collective-permute-done.9.refs_3_), channel_id=1, source_target_pairs={{0,1},{1,2},{2,3},{3,4},{4,5},{5,6},{6,7},{7,0},{8,9},{9,10},{10,1... | collective-permute-start | bytes 1572872 | tf_op jit(solution)/shard_map/ppermute | solution.py:43
  56.8 35.8 %copy-start.10 = (bf16[8,128,256]{2,1,0:T(8,128)(2,1)}, bf16[8,128,256]{2,1,0:T(8,128)(2,1)S(1)}, u32[]{:S(2)}) copy-start(bf16[8,128,256]{2,1,0:T(8,128)(2,1)S(1)} %collective-permute-done.10.refs_4_) | copy-start | bytes 1572868
  56.8 14.0 %collective-permute-start.12 = (bf16[8,128,256]{2,1,0:T(8,128)(2,1)S(1)}, bf16[8,128,256]{2,1,0:T(8,128)(2,1)S(1)}, u32[]{:S(2)}, u32[]{:S(2)}) collective-permute-start(bf16[8,128,256]{2,1,0:T(8,128)(2,1)S(1)} %collective-permute-done.10.refs_4_), channel_id=1, source_target_pairs={{0,7},{1,0},{2,1},{3,2},{4,3},{5,4},{6,5},{7,6},{8,15},{9,8},{10,9... | collective-permute-start | bytes 1572872 | tf_op jit(solution)/shard_map/ppermute | solution.py:43
  70.9 8.7 %collective-permute-start.13 = (bf16[8,128,256]{2,1,0:T(8,128)(2,1)S(1)}, bf16[8,128,256]{2,1,0:T(8,128)(2,1)S(1)}, u32[]{:S(2)}, u32[]{:S(2)}) collective-permute-start(bf16[8,128,256]{2,1,0:T(8,128)(2,1)S(1)} %broadcast_select_fusion), channel_id=1, source_target_pairs={{0,1},{1,2},{2,3},{3,4},{4,5},{5,6},{6,7},{7,0},{8,9},{9,10},{10,1... | collective-permute-start | bytes 1572872 | tf_op jit(solution)/shard_map/ppermute | solution.py:43
  92.6 43.6 %all-to-all-start.1 = ((bf16[8,256,256]{2,1,0:T(8,128)(2,1)}), bf16[8,256,256]{2,1,0:T(8,128)(2,1)S(1)}, u32[]{:S(2)}, u32[]{:S(2)}) async-start(bf16[8,256,256]{2,1,0:T(8,128)(2,1)} %bitcast.12), calls=%async_computation.1 | async-start | bytes 2097152 | tf_op jit(solution)/shard_map/all_to_all | solution.py:47
  101.1 41.0 %copy-start.6 = (bf16[256,256]{1,0:T(8,128)(2,1)S(1)}, bf16[256,256]{1,0:T(8,128)(2,1)}, u32[]{:S(2)}) copy-start(bf16[256,256]{1,0:T(8,128)(2,1)} %weight_ref.1) | copy-start | bytes 393220
  112.4 2.3 %collective-permute-start.14 = (bf16[4,288,256]{2,1,0:T(8,128)(2,1)}, bf16[4,288,256]{2,1,0:T(8,128)(2,1)S(1)}, u32[]{:S(2)}, u32[]{:S(2)}) collective-permute-start(bf16[4,288,256]{2,1,0:T(8,128)(2,1)} %get-tuple-element.34), channel_id=1, source_target_pairs={{0,32},{32,0},{64,96},{96,64},{128,160},{160,128},{192,224},{224,1... | collective-permute-start | bytes 1769480 | tf_op jit(solution)/shard_map/ppermute | solution.py:43
  117.8 6.8 %collective-permute-start.15 = (bf16[288,256]{1,0:T(8,128)(2,1)}, bf16[288,256]{1,0:T(8,128)(2,1)S(1)}, u32[]{:S(2)}, u32[]{:S(2)}) collective-permute-start(bf16[288,256]{1,0:T(8,128)(2,1)} %get-tuple-element.36), channel_id=1, source_target_pairs={{0,64},{32,96},{64,128},{96,160},{128,192},{160,224},{192,0},{224,... | collective-permute-start | bytes 442376 | tf_op jit(solution)/shard_map/ppermute | solution.py:43
  117.8 9.8 %collective-permute-start.16 = (bf16[288,256]{1,0:T(8,128)(2,1)}, bf16[288,256]{1,0:T(8,128)(2,1)S(1)}, u32[]{:S(2)}, u32[]{:S(2)}) collective-permute-start(bf16[288,256]{1,0:T(8,128)(2,1)} %get-tuple-element.37), channel_id=1, source_target_pairs={{0,128},{32,160},{64,192},{96,224},{128,0},{160,32},{192,64},{224,... | collective-permute-start | bytes 442376 | tf_op jit(solution)/shard_map/ppermute | solution.py:43
  120.6 7.4 %collective-permute-start.17 = (bf16[288,256]{1,0:T(8,128)(2,1)}, bf16[288,256]{1,0:T(8,128)(2,1)S(1)}, u32[]{:S(2)}, u32[]{:S(2)}) collective-permute-start(bf16[288,256]{1,0:T(8,128)(2,1)} %get-tuple-element.38), channel_id=1, source_target_pairs={{0,192},{32,224},{64,0},{96,32},{128,64},{160,96},{192,128},{224,1... | collective-permute-start | bytes 442376 | tf_op jit(solution)/shard_map/ppermute | solution.py:43
  129.1 2.9 %collective-permute-start.18 = (f32[32,256]{1,0:T(8,128)S(1)}, f32[32,256]{1,0:T(8,128)S(1)}, u32[]{:S(2)}, u32[]{:S(2)}) collective-permute-start(f32[32,256]{1,0:T(8,128)S(1)} %slice.37), channel_id=1, source_target_pairs={{0,8},{1,9},{2,10},{3,11},{4,12},{5,13},{6,14},{7,15},{8,0},{9,1},... | collective-permute-start | bytes 98312 | tf_op jit(solution)/shard_map/ppermute | solution.py:43
  131.9 4.3 %collective-permute-start.19 = (f32[32,256]{1,0:T(8,128)S(1)}, f32[32,256]{1,0:T(8,128)S(1)}, u32[]{:S(2)}, u32[]{:S(2)}) collective-permute-start(f32[32,256]{1,0:T(8,128)S(1)} %slice_add_fusion), channel_id=1, source_target_pairs={{0,16},{1,17},{2,18},{3,19},{4,20},{5,21},{6,22},{7,23},{8,24},{9,... | collective-permute-start | bytes 98312 | tf_op jit(solution)/shard_map/ppermute | solution.py:43
  136.2 3.1 %collective-permute-start.20 = (f32[32,256]{1,0:T(8,128)S(1)}, f32[32,256]{1,0:T(8,128)S(1)}, u32[]{:S(2)}, u32[]{:S(2)}) collective-permute-start(f32[32,256]{1,0:T(8,128)S(1)} %add.252), channel_id=1, source_target_pairs={{0,1},{1,0},{2,3},{3,2},{4,5},{5,4},{6,7},{7,6},{8,9},{9,8},{10,11... | collective-permute-start | bytes 98312 | tf_op jit(solution)/shard_map/ppermute | solution.py:43
  139.4 4.1 %collective-permute-start.21 = (f32[32,256]{1,0:T(8,128)S(1)}, f32[32,256]{1,0:T(8,128)S(1)}, u32[]{:S(2)}, u32[]{:S(2)}) collective-permute-start(f32[32,256]{1,0:T(8,128)S(1)} %add.255), channel_id=1, source_target_pairs={{0,2},{1,3},{2,0},{3,1},{4,6},{5,7},{6,4},{7,5},{8,10},{9,11},{10,... | collective-permute-start | bytes 98312 | tf_op jit(solution)/shard_map/ppermute | solution.py:43
  143.4 6.7 %collective-permute-start.22 = (f32[32,256]{1,0:T(8,128)S(1)}, f32[32,256]{1,0:T(8,128)S(1)}, u32[]{:S(2)}, u32[]{:S(2)}) collective-permute-start(f32[32,256]{1,0:T(8,128)S(1)} %add.256), channel_id=1, source_target_pairs={{0,4},{1,5},{2,6},{3,7},{4,0},{5,1},{6,2},{7,3},{8,12},{9,13},{10,... | collective-permute-start | bytes 98312 | tf_op jit(solution)/shard_map/ppermute | solution.py:43
  150.1 4.7 %collective-permute-start.23 = (f32[32,256]{1,0:T(8,128)S(1)}, f32[32,256]{1,0:T(8,128)S(1)}, u32[]{:S(2)}, u32[]{:S(2)}) collective-permute-start(f32[32,256]{1,0:T(8,128)S(1)} %add.257), channel_id=1, source_target_pairs={{0,64},{32,96},{64,128},{96,160},{128,192},{160,224},{192,0},{224,... | collective-permute-start | bytes 98312 | tf_op jit(solution)/shard_map/ppermute | solution.py:43
  151.3 4.7 %collective-permute-start.24 = (f32[32,256]{1,0:T(8,128)S(1)}, f32[32,256]{1,0:T(8,128)S(1)}, u32[]{:S(2)}, u32[]{:S(2)}) collective-permute-start(f32[32,256]{1,0:T(8,128)S(1)} %add.257), channel_id=1, source_target_pairs={{0,128},{32,160},{64,192},{96,224},{128,0},{160,32},{192,64},{224,... | collective-permute-start | bytes 98312 | tf_op jit(solution)/shard_map/ppermute | solution.py:43
  154.1 2.8 %collective-permute-start.25 = (f32[32,256]{1,0:T(8,128)S(1)}, f32[32,256]{1,0:T(8,128)S(1)}, u32[]{:S(2)}, u32[]{:S(2)}) collective-permute-start(f32[32,256]{1,0:T(8,128)S(1)} %add.257), channel_id=1, source_target_pairs={{0,192},{32,224},{64,0},{96,32},{128,64},{160,96},{192,128},{224,1... | collective-permute-start | bytes 98312 | tf_op jit(solution)/shard_map/ppermute | solution.py:43
  157.5 8.7 %collective-permute-start.26 = (f32[4,32,256]{2,1,0:T(8,128)S(1)}, f32[4,32,256]{2,1,0:T(8,128)S(1)}, u32[]{:S(2)}, u32[]{:S(2)}) collective-permute-start(f32[4,32,256]{2,1,0:T(8,128)S(1)} %broadcast_select_fusion.1), channel_id=1, source_target_pairs={{0,32},{32,0},{64,96},{96,64},{128,160},{160,128},{192,224},{224,1... | collective-permute-start | bytes 393224 | tf_op jit(solution)/shard_map/ppermute | solution.py:43
  (10 other events, 109.8 us)

commit v3 on v2

v3 whole, which is shorter than its diff:
```python
import functools

import jax
import jax.numpy as jnp
from jax import lax
from jax.experimental import pallas as pl
from jax.experimental.pallas import tpu as pltpu
from jax.sharding import PartitionSpec as P

X, Z = 4, 8
Y = 4
GROUP = 16
CHUNK = 16
VMEM_MIB = 60
FORWARD_ROW, BACK_ROW, COLUMN, ORDER = range(4)
FAR_X = X // 2
Z_ORDER = (Z // 2, 3, 5, 2, 6, 1, 7, 0)


def along_z(d):
    return [(x * Z + z, x * Z + (z + d) % Z) for x in range(X) for z in range(Z)]


def along_x(d):
    return [(x * Z + z, ((x + d) % X) * Z + z) for x in range(X) for z in range(Z)]


def along_y(d):
    return [(y * 2 + c, ((y + d) % Y) * 2 + c) for y in range(Y) for c in range(2)]


def by_core(along):
    return [
        (row * X * Z + a, row * X * Z + b)
        for row in range(2 * Y)
        for a, b in along(1 - 2 * (row % 2))
    ]


OTHER_CORE = [(r, r ^ 1) for r in range(2 * Y)]
Z_GROUPS = [[x * Z + z for z in range(Z)] for x in range(X)]


def send(value, axis, pairs):
    return lax.ppermute(value, axis, pairs)


def exchange_z(value):
    return lax.all_to_all(value, "col", 0, 0, axis_index_groups=Z_GROUPS)


def scale_of(degrees):
    scale = lax.rsqrt(degrees.astype(jnp.float32))
    return jnp.transpose(jnp.broadcast_to(scale, (128,) + scale.shape[1:]))


def load_all(live, edges_hbm, edges, sems):
    def load(chunk):
        part = pl.ds(chunk * CHUNK, CHUNK)
        return pltpu.make_async_copy(edges_hbm.at[part], edges.at[part], sems.at[chunk])

    @pl.loop(0, (live + CHUNK - 1) // CHUNK)
    def _(chunk):
        load(chunk).start()

    return lambda chunk: load(chunk).wait()


def add_tiles(begin, end, tile_of, product, target, totals):
    @pl.loop(0, (end - begin + GROUP - 1) // GROUP)
    def _(step):
        for k in range(GROUP):
            at = begin + step * GROUP + k
            value = product(tile_of(at).astype(jnp.float32).astype(jnp.bfloat16), at)
            slot = target(at)
            for half, total in enumerate(totals):
                total[slot] += value[:, half * 128 : half * 128 + 128]


def add_chunks(live, wait, tile_of, product, target, totals):
    @pl.loop(0, (live + CHUNK - 1) // CHUNK)
    def _(chunk):
        wait(chunk)
        begin = chunk * CHUNK
        add_tiles(begin, jnp.minimum(live, begin + CHUNK), tile_of, product, target, totals)


def forward_kernel(
    deps, meta_ref, scalars_ref, edges_hbm, own_ref, other_ref, weight_ref, *refs
):
    out_refs = refs[deps : deps + Z]
    panel, left, right, edges, sems = refs[deps + Z :]
    live = scalars_ref[0]
    size = left.shape[1]

    wait = load_all(live, edges_hbm, edges, sems)
    for total in (left, right):
        total[...] = jnp.zeros_like(total)
    for block in range(2 * Y):
        ref, dy = (own_ref, other_ref)[block // Y], block % Y
        scale = scale_of(ref[dy, 2 * size :][:1])
        value = jnp.dot(
            ref[dy, : 2 * size], weight_ref[...], preferred_element_type=jnp.float32
        )
        value = value * jnp.concatenate([scale, scale], axis=1)
        panel[pl.ds(2 * block, 2)] = value.astype(jnp.bfloat16).reshape(2, size, -1)

    def product(tile, at):
        return jnp.dot(tile, panel[meta_ref[COLUMN, at]], preferred_element_type=jnp.float32)

    add_chunks(
        live, wait, lambda at: jnp.where(at < live, edges[at], 0), product,
        lambda at: meta_ref[FORWARD_ROW, at], (left, right),
    )
    for out_ref, dz in zip(out_refs, Z_ORDER):
        for slot in range(2 * X):
            out_ref[slot, :, :128] = left[dz * 2 * X + slot].astype(jnp.bfloat16)
            out_ref[slot, :, 128:] = right[dz * 2 * X + slot].astype(jnp.bfloat16)


def back_product(upstream, tile, slot):
    return lax.dot_general(
        tile, upstream[slot], (((0,), (0,)), ((), ())), preferred_element_type=jnp.float32
    )


def backward_near_kernel(base, places, meta_ref, scalars_ref, edges_hbm, *refs):
    pieces = refs[: len(places)]
    own_hbm, other_hbm, left, right, features_ref, token_ref = refs[len(places) : len(places) + 6]
    own_ref, other_ref, upstream, edges, sems, piece_sems = refs[len(places) + 6 :]
    token_ref[...] = jnp.zeros_like(token_ref)
    live = scalars_ref[0]
    copies = [
        pltpu.make_async_copy(piece, upstream.at[pl.ds(at, piece.shape[0])], piece_sems.at[k])
        for k, (piece, at) in enumerate(zip(pieces, places))
    ]
    for k, (src, dst) in enumerate([(own_hbm, own_ref), (other_hbm, other_ref)], len(places)):
        copies.append(pltpu.make_async_copy(src, dst, piece_sems.at[k]))
    for copy in copies:
        copy.start()
    wait = load_all(live, edges_hbm, edges, sems)
    for total in (left, right):
        total[...] = jnp.zeros_like(total)
    for copy in copies:
        copy.wait()
    nodes = 2 * left.shape[1]
    for block in range(2 * Y):
        ref, dy = (own_ref, other_ref)[block // Y], block % Y
        scale = scale_of(ref[dy, nodes:][:1])
        scaled = ref[dy, :nodes].astype(jnp.float32) * jnp.concatenate([scale, scale], axis=1)
        features_ref[block] = jnp.transpose(scaled).astype(jnp.bfloat16)

    def here(at):
        row = meta_ref[BACK_ROW, at]
        return jnp.logical_and(at < live, jnp.logical_or(row < base, row >= base + 2 * Z))

    add_chunks(
        live, wait, lambda at: jnp.where(here(at), edges[at], 0),
        lambda tile, at: back_product(
            upstream, tile, jnp.where(here(at), meta_ref[BACK_ROW, at], 0)
        ),
        lambda at: meta_ref[COLUMN, at], (left, right),
    )


def backward_far_kernel(
    base, meta_ref, scalars_ref, edges_hbm, piece, near_left, near_right, features_hbm, _,
    keep_ref, far_ref, terms_keep_ref, terms_far_ref,
    left, right, upstream, features_ref, terms, edges, sems, input_sems,
):
    row, count = scalars_ref[1], scalars_ref[2]
    size = left.shape[1]
    pairs = [
        (piece, upstream), (near_left, left), (near_right, right),
        (features_hbm, features_ref),
    ]
    copies = [
        pltpu.make_async_copy(src, dst, input_sems.at[k]) for k, (src, dst) in enumerate(pairs)
    ]

    def load(at):
        return pltpu.make_async_copy(edges_hbm.at[meta_ref[ORDER, at]], edges.at[at], sems.at[at])

    for copy in copies[:3]:
        copy.start()

    @pl.loop(0, count)
    def _(at):
        load(at).start()

    for copy in copies[3:]:
        copy.start()
    for copy in copies[:3]:
        copy.wait()

    @pl.loop(0, count)
    def _(at):
        load(at).wait()

    def number(name, at):
        return meta_ref[name, meta_ref[ORDER, at]]

    add_tiles(
        0, count, lambda at: jnp.where(at < count, edges[at], 0),
        lambda tile, at: back_product(
            upstream, tile, jnp.where(at < count, number(BACK_ROW, at) - base, 0)
        ),
        lambda at: number(COLUMN, at), (left, right),
    )
    for copy in copies[3:]:
        copy.wait()
    y, core = row // 2, row % 2
    result = None
    for block in range(2 * Y):
        far, dy = block // Y, block % Y
        part = pl.ds(2 * block, 2)
        value = jnp.concatenate(
            [
                ref[part].reshape(2 * size, 128) for ref in (left, right)
            ],
            axis=1,
        )
        if far:
            far_ref[dy] = value.astype(jnp.bfloat16)
        else:
            keep_ref[dy] = value
        term = jnp.dot(
            features_ref[block], value.astype(jnp.bfloat16), preferred_element_type=jnp.float32
        )
        result = term if result is None else result + term
    terms[...] = result.reshape(terms.shape)
    for block in range(2 * Y):
        far, dy = block // Y, block % Y
        value = terms[((y + dy) % Y) * 2 + (core + far) % 2]
        (terms_far_ref if far else terms_keep_ref)[dy] = value


PARAMS = dict(vmem_limit_bytes=VMEM_MIB * 1024 * 1024)
ANY = pl.BlockSpec(memory_space=pl.ANY)
VMEM = pl.BlockSpec(memory_space=pltpu.VMEM)
SMEM = pl.BlockSpec(memory_space=pltpu.SMEM)


def forward(meta, scalars, edges, own, other, weight, deps=()):
    slots, size, _ = edges.shape
    width = weight.shape[-1]
    f32, bf16 = jnp.float32, jnp.bfloat16
    return pl.pallas_call(
        functools.partial(forward_kernel, len(deps)),
        in_specs=[SMEM, SMEM, ANY, VMEM, VMEM, VMEM] + [ANY] * len(deps),
        out_specs=[VMEM] * Z,
        scratch_shapes=[
            pltpu.VMEM((4 * Y, size, width), bf16),
            pltpu.VMEM((2 * X * Z, size, 128), f32),
            pltpu.VMEM((2 * X * Z, size, 128), f32),
            pltpu.VMEM(edges.shape, edges.dtype),
            pltpu.SemaphoreType.DMA((slots // CHUNK,)),
        ],
        out_shape=[jax.ShapeDtypeStruct((2 * X, size, width), bf16)] * Z,
        compiler_params=pltpu.CompilerParams(**PARAMS),
        cost_estimate=pl.CostEstimate(flops=10**6, bytes_accessed=10**4, transcendentals=0),
        name="forward_tiles",
    )(meta, scalars, edges, own, other, weight, *deps)


def backward_near(meta, scalars, edges, pieces, places, base, own, other):
    slots, size, _ = edges.shape
    width = pieces[0].shape[-1]
    f32, bf16 = jnp.float32, jnp.bfloat16
    return pl.pallas_call(
        functools.partial(backward_near_kernel, base, places),
        in_specs=[SMEM, SMEM, ANY] + [ANY] * (len(pieces) + 2),
        out_specs=[VMEM] * 4,
        scratch_shapes=[
            pltpu.VMEM(own.shape, bf16),
            pltpu.VMEM(other.shape, bf16),
            pltpu.VMEM((2 * X * Z, size, width), bf16),
            pltpu.VMEM(edges.shape, edges.dtype),
            pltpu.SemaphoreType.DMA((slots // CHUNK,)),
            pltpu.SemaphoreType.DMA((len(pieces) + 2,)),
        ],
        out_shape=[jax.ShapeDtypeStruct((4 * Y, size, 128), f32)] * 2
        + [
            jax.ShapeDtypeStruct((2 * Y, width, 2 * size), bf16),
            jax.ShapeDtypeStruct((8, 128), f32),
        ],
        compiler_params=pltpu.CompilerParams(**PARAMS),
        cost_estimate=pl.CostEstimate(flops=10**6, bytes_accessed=10**4, transcendentals=0),
        name="backward_near",
    )(meta, scalars, edges, *pieces, own, other)


def backward_far(meta, scalars, edges, piece, place, left, right, features, after):
    slots, size, _ = edges.shape
    width = piece.shape[-1]
    rows = width // (2 * Y)
    f32, bf16 = jnp.float32, jnp.bfloat16
    outs = [((Y, 2 * size, width), f32), ((Y, 2 * size, width), bf16)]
    outs += [((Y, rows, width), f32)] * 2
    return pl.pallas_call(
        functools.partial(backward_far_kernel, place),
        in_specs=[SMEM, SMEM] + [ANY] * 6,
        out_specs=[VMEM] * len(outs),
        scratch_shapes=[
            pltpu.VMEM((4 * Y, size, 128), f32),
            pltpu.VMEM((4 * Y, size, 128), f32),
            pltpu.VMEM(piece.shape, bf16),
            pltpu.VMEM(features.shape, bf16),
            pltpu.VMEM((2 * Y, rows, width), f32),
            pltpu.VMEM(edges.shape, edges.dtype),
            pltpu.SemaphoreType.DMA((slots,)),
            pltpu.SemaphoreType.DMA((4,)),
        ],
        out_shape=[jax.ShapeDtypeStruct(shape, dtype) for shape, dtype in outs],
        compiler_params=pltpu.CompilerParams(**PARAMS),
        cost_estimate=pl.CostEstimate(flops=10**6, bytes_accessed=10**4, transcendentals=0),
        name="backward_far",
    )(meta, scalars, edges, piece, left, right, features, after)


def gather_z(own, size, core):
    parts = {0: own}
    up = down = own
    for k in range(1, Z // 2):
        up, down = send(up, "col", along_z(1)), send(down, "col", along_z(-1))
        parts[Z - k], parts[k] = up, down
    parts[Z // 2] = send(jnp.where(core == 0, up, down), ("row", "col"), by_core(along_z))
    return jnp.concatenate([parts[k] for k in range(Z)]).reshape(2 * Z, size, -1)


def gather_x(plane, core):
    left = send(plane, "col", along_x(1))
    right = send(plane, "col", along_x(-1))
    far = send(jnp.where(core == 0, left, right), ("row", "col"), by_core(along_x))
    return [plane, left, right, far], [0, 3 * 2 * Z, 2 * Z, FAR_X * 2 * Z]


def gather_row(own):
    mine = jnp.stack(
        [
            own,
            send(own, "row", along_y(-1)),
            send(own, "row", along_y(2)),
            send(own, "row", along_y(1)),
        ]
    )
    return mine, send(mine, "row", OTHER_CORE)


def fold_cores_kernel(keep, recv, own, *outs):
    own[...] = keep[0] + recv[0].astype(jnp.float32)
    for d, out in enumerate(outs, 1):
        out[...] = (keep[d] + recv[d].astype(jnp.float32)).astype(out.dtype)


def scatter_row(keep, far):
    recv = send(far, "row", OTHER_CORE)
    shape = keep.shape[1:]
    own, *parts = pl.pallas_call(
        fold_cores_kernel,
        out_shape=[jax.ShapeDtypeStruct(shape, jnp.float32)]
        + [jax.ShapeDtypeStruct(shape, far.dtype)] * (Y - 1),
        name="fold_cores",
    )(keep, recv)
    return own + sum(
        send(part, "row", along_y(d)).astype(jnp.float32) for d, part in enumerate(parts, 1)
    )


def all_rows(value, y, core):
    mine = jnp.stack([value] + [send(value, "row", along_y(d)) for d in range(1, Y)])
    got = jnp.concatenate([mine, send(mine, "row", OTHER_CORE)])
    row = jnp.arange(2 * Y, dtype=jnp.int32)
    order = (row + core) % 2 * Y + (y - row // 2) % Y
    return jnp.take(got, order, axis=0).reshape(-1, value.shape[-1])


def scatter_start(far, first_up, first_down, core):
    f32, bf16 = jnp.float32, jnp.bfloat16
    recv = send(far, ("row", "col"), by_core(along_z)).astype(f32)
    up = (first_up.astype(f32) + jnp.where(core == 0, recv, 0)).astype(bf16)
    down = (first_down.astype(f32) + jnp.where(core == 0, 0, recv)).astype(bf16)
    return up, down


def scatter_round(up, down):
    return send(up, "col", along_z(1)), send(down, "col", along_z(-1))


def fold(received, own):
    return [(b.astype(jnp.float32) + a.astype(jnp.float32)).astype(a.dtype)
            for a, b in zip(received, own)]


def scatter_end(below, above, own):
    f32, bf16 = jnp.float32, jnp.bfloat16
    column = own.astype(f32) + below.astype(f32) + above.astype(f32)
    column = column.reshape(X, -1, column.shape[-1])
    return column[0] + sum(
        send(column[d].astype(bf16), "col", along_x(d)).astype(f32) for d in range(1, X)
    )


def sum_x(value, x):
    got = jnp.stack([value] + [send(value, "col", along_x(d)) for d in range(1, X)])
    order = (x - jnp.arange(X, dtype=jnp.int32)) % X
    return jnp.sum(jnp.take(got, order, axis=0), axis=0)


def sum_z(value):
    return jnp.sum(exchange_z(jnp.broadcast_to(value, (Z,) + value.shape)), axis=0)


def shards(features, weight, tile_coords, tile_live, tile_edges, row_degree, col_degree, cotangent):
    f32, bf16 = jnp.float32, jnp.bfloat16
    size = tile_edges.shape[-1]
    nodes, width = features.shape
    row_scale = lax.rsqrt(row_degree.astype(f32))
    col_scale = lax.rsqrt(col_degree.astype(f32))
    coords = tile_coords[0, 0]
    edges = tile_edges[0, 0]
    row, col = lax.axis_index("row"), lax.axis_index("col")
    y, core = row // 2, row % 2

    upstream = (row_scale[:, None] * cotangent.astype(f32)).astype(bf16)
    plane = gather_z(upstream, size, core)

    degrees = jnp.zeros((16, width), bf16).at[0].set(col_degree.astype(bf16))
    mine, other = gather_row(jnp.concatenate([features, degrees]))

    owner, half = coords[:, 0] // 2, coords[:, 0] % 2
    dx = (owner // Z - col // Z) % X
    dz = (owner % Z - col % Z) % Z
    forward_row = (dz * X + dx) * 2 + half
    back_row = (dx * Z + dz) * 2 + half
    col_owner, half = coords[:, 1] // 2, coords[:, 1] % 2
    column = ((col_owner + core) % 2 * Y + (col_owner // 2 - y) % Y) * 2 + half
    live = tile_live[0, 0]
    index = jnp.arange(coords.shape[0], dtype=jnp.int32)
    key = index + 256 * jnp.logical_or(index >= live, dx != FAR_X)
    place = jnp.sum(key[None, :] < key[:, None], axis=1)
    order = jnp.sum(jnp.where(place[:, None] == index, index[:, None], 0), axis=0)
    meta = jnp.stack([forward_row, back_row, column, order]).astype(jnp.int32)
    scalars = jnp.stack([live, row, jnp.sum(key < 256)]).astype(jnp.int32)

    far, *parts = forward(meta, scalars, edges, mine, other, weight)
    (plane, left, right, last), places = gather_x(plane, core)
    up, down = scatter_start(far, *parts[:2], core)
    up, down, left, right = lax.optimization_barrier((up, down, left, right))
    received = scatter_round(up, down)
    *sums, token = backward_near(
        meta, scalars, edges, [plane, left, right], places[:-1], places[-1], mine, other
    )
    up, down = fold(received, parts[2:4])
    up, down, token = lax.optimization_barrier((up, down, token))
    received = scatter_round(up, down)
    keep, far, terms_keep, terms_far = backward_far(
        meta, scalars, edges, last, places[-1], *sums, token
    )
    received = scatter_round(*fold(received, parts[4:6]))
    aggregated = (row_scale[:, None] * scatter_end(*received, parts[6])).astype(bf16)

    terms = terms_keep + send(terms_far, "row", OTHER_CORE)
    terms = terms[0] + sum(send(terms[d], "row", along_y(d)) for d in range(1, Y))
    terms = sum_x(terms, col // Z)
    grad_weight = all_rows(sum_z(terms), y, core)
    back = scatter_row(keep, far)
    grad_panel = (col_scale[:, None] * back).astype(bf16)
    grad_features = jnp.dot(grad_panel, weight.T, preferred_element_type=f32).astype(bf16)
    return aggregated, grad_features, grad_weight


def solution(mesh):
    in_specs = (
        P(("col", "row"), None),
        P(),
        P("row", "col", None, None),
        P("row", "col"),
        P("row", "col", None, None, None),
        P(("row", "col")),
        P(("col", "row")),
        P(("row", "col"), None),
    )
    out_specs = (P(("row", "col"), None), P(("col", "row"), None), P())
    return jax.shard_map(shards, mesh=mesh, in_specs=in_specs, out_specs=out_specs, check_vma=False)
```

time: 168 us -> 148 us (0.88)
  waiting for transfers between devices: 61.7 us -> 16.5 us
  other arithmetic: 11.7 us -> 21.6 us
  starting transfers between devices: 64.1 us -> 71.8 us
  local copies, waits for them, and re-layouts: 3.65 us -> 8.78 us
  Pallas kernels: 23.4 us -> 25.5 us
    ppermute x27 -> x39, waiting for transfers between devices: 52.8 us -> 16.5 us  [send(): return lax.ppermute(value, axis, pairs)]
    ppermute x27 -> x39, starting transfers between devices: 50.8 us -> 65.8 us  [send(): return lax.ppermute(value, axis, pairs)]
    all_to_all x1 -> x0, waiting for transfers between devices: 8.88 us -> none  [exchange_x(): return lax.all_to_all(value, 'col', 0, 0, axis_index_groups=X_GROUPS)]
    convert_element_type x2 -> x6, other arithmetic: 1.76 us -> 7.12 us  [the longest x4 3.87 us: fold(): (b.astype(jnp.float32) + a.astype(jnp.float32)).astype(a.dtype)]
    all_to_all x1 -> x0, starting transfers between devices: 4.89 us -> none  [exchange_x(): return lax.all_to_all(value, 'col', 0, 0, axis_index_groups=X_GROUPS)]
    unnamed x26 -> x31, local copies, waits for them, and re-layouts: 1.68 us -> 6.01 us
    pallas_call x1 -> x2, Pallas kernels: 11.3 us -> 15.3 us  [the longest x1 8.58 us: backward_near(): pl.pallas_call(functools.partial(backward_near_kernel, base, places), in_...]
    select_n x5 -> x6, other arithmetic: 0.26 us -> 3.92 us  [the longest x2 1.33 us: all_rows(): return jnp.take(got, order, axis=0).reshape(-1, value.shape[-1])]
  transfers between devices with their start and end apart: 29 -> 40, of which waited for: 17 -> 10; matrix products, arithmetic and copies ran while one was open for 4% -> 18% of each run, Pallas kernels for 14% -> 17%
where the time goes in v3:
time: 148 us
  starting transfers between devices  71.8 us (49%)
  Pallas kernels  25.5 us (17%)
  other arithmetic  21.6 us (15%)
  waiting for transfers between devices  16.5 us (11%)
  local copies, waits for them, and re-layouts  8.78 us (6%)
  matrix products  1.84 us (1%)
  between operations  1.72 us (1%)
    ppermute x39, starting transfers between devices, send(): return lax.ppermute(value, axis, pairs)  65.8 us
    ppermute x39, waiting for transfers between devices, send(): return lax.ppermute(value, axis, pairs)  16.5 us
    pallas_call x1, Pallas kernels, backward_near(): pl.pallas_call(functools.partial(backward_near_kernel, base, places), in_...  8.58 us
    pallas_call x1, Pallas kernels, forward(): pl.pallas_call(functools.partial(forward_kernel, len(deps)), in_specs=[SM...  7.97 us
    pallas_call x1, Pallas kernels, backward_far(): pl.pallas_call(functools.partial(backward_far_kernel, place), in_specs=[S...  6.72 us
    all_to_all x1, starting transfers between devices, exchange_z(): return lax.all_to_all(value, 'col', 0, 0, axis_index_groups=Z_GROUPS)  6.07 us
    unnamed x31, local copies, waits for them, and re-layouts  6.01 us
    convert_element_type x4, other arithmetic, fold(): (b.astype(jnp.float32) + a.astype(jnp.float32)).astype(a.dtype)  3.87 us
  transfers between devices with their start and end apart: 40, of which 10 were waited for; matrix products, arithmetic and copies ran while one was open for 18% of the time, Pallas kernels for 17%

profile of v3, /device:TPU:1, one launch (start us, length us, event | category | flops | bytes accessed | tf_op | source)
XLA Modules:
  0.0 147.7 jit_solution(17726262194953974228)
XLA Ops:
  2.2 2.2 %collective-permute-start.2 = (bf16[272,256]{1,0:T(8,128)(2,1)S(1)}, bf16[272,256]{1,0:T(8,128)(2,1)S(1)}, u32[]{:S(2)}, u32[]{:S(2)}) collective-permute-start(bf16[272,256]{1,0:T(8,128)(2,1)S(1)} %get-tuple-element.86), channel_id=1, source_target_pairs={{0,64},{32,96},{64,128},{96,160},{128,192},{160,224},{192,0},{224,... | collective-permute-start | bytes 417800 | tf_op jit(solution)/shard_map/ppermute | solution.py:45
  4.5 2.6 %collective-permute-start.1 = (bf16[272,256]{1,0:T(8,128)(2,1)S(1)}, bf16[272,256]{1,0:T(8,128)(2,1)S(1)}, u32[]{:S(2)}, u32[]{:S(2)}) collective-permute-start(bf16[272,256]{1,0:T(8,128)(2,1)S(1)} %get-tuple-element.86), channel_id=1, source_target_pairs={{0,128},{32,160},{64,192},{96,224},{128,0},{160,32},{192,64},{224,... | collective-permute-start | bytes 417800 | tf_op jit(solution)/shard_map/ppermute | solution.py:45
  8.8 1.7 %constant_dynamic-update-slice_fusion.7 = (bf16[2048,256]{1,0:T(8,128)(2,1)}, bf16[256,256]{1,0:T(8,128)(2,1)S(1)}) fusion(bf16[256,256]{1,0:T(8,128)(2,1)} %param.17, f32[256]{0:T(256)S(1)} %convert_rsqrt_fusion.1), kind=kLoop, calls=%fused_computation.45 | loop fusion | flops 196607 | bytes 394240
  10.5 1.6 %collective-permute-start.8 = (bf16[256,256]{1,0:T(8,128)(2,1)S(1)}, bf16[256,256]{1,0:T(8,128)(2,1)S(1)}, u32[]{:S(2)}, u32[]{:S(2)}) collective-permute-start(bf16[256,256]{1,0:T(8,128)(2,1)S(1)} %get-tuple-element.72), channel_id=1, source_target_pairs={{0,1},{1,2},{2,3},{3,4},{4,5},{5,6},{6,7},{7,0},{8,9},{9,10},{10,1... | collective-permute-start | bytes 393224 | tf_op jit(solution)/shard_map/ppermute | solution.py:45
  12.1 3.9 %collective-permute-start.5 = (bf16[256,256]{1,0:T(8,128)(2,1)S(1)}, bf16[256,256]{1,0:T(8,128)(2,1)S(1)}, u32[]{:S(2)}, u32[]{:S(2)}) collective-permute-start(bf16[256,256]{1,0:T(8,128)(2,1)S(1)} %get-tuple-element.72), channel_id=1, source_target_pairs={{0,7},{1,0},{2,1},{3,2},{4,3},{5,4},{6,5},{7,6},{8,15},{9,8},{10,9... | collective-permute-start | bytes 393224 | tf_op jit(solution)/shard_map/ppermute | solution.py:45
  18.4 2.7 %collective-permute-start.6 = (bf16[256,256]{1,0:T(8,128)(2,1)S(1)}, bf16[256,256]{1,0:T(8,128)(2,1)S(1)}, u32[]{:S(2)}, u32[]{:S(2)}) collective-permute-start(bf16[256,256]{1,0:T(8,128)(2,1)S(1)} %collective-permute-done.5), channel_id=1, source_target_pairs={{0,7},{1,0},{2,1},{3,2},{4,3},{5,4},{6,5},{7,6},{8,15},{9,8},{10,9... | collective-permute-start | bytes 393224 | tf_op jit(solution)/shard_map/ppermute | solution.py:45
  21.8 1.7 %collective-permute-done.9 = bf16[256,256]{1,0:T(8,128)(2,1)S(1)} collective-permute-done((bf16[256,256]{1,0:T(8,128)(2,1)S(1)}, bf16[256,256]{1,0:T(8,128)(2,1)S(1)}, u32[]{:S(2)}, u32[]{:S(2)}) %collective-permute-start.9) | collective-permute-done | bytes 131104 | tf_op jit(solution)/shard_map/ppermute | solution.py:45
  23.5 2.7 %collective-permute-start.7 = (bf16[256,256]{1,0:T(8,128)(2,1)S(1)}, bf16[256,256]{1,0:T(8,128)(2,1)S(1)}, u32[]{:S(2)}, u32[]{:S(2)}) collective-permute-start(bf16[256,256]{1,0:T(8,128)(2,1)S(1)} %collective-permute-done.6), channel_id=1, source_target_pairs={{0,7},{1,0},{2,1},{3,2},{4,3},{5,4},{6,5},{7,6},{8,15},{9,8},{10,9... | collective-permute-start | bytes 393224 | tf_op jit(solution)/shard_map/ppermute | solution.py:45
  29.2 2.7 %collective-permute-start.11 = (bf16[256,256]{1,0:T(8,128)(2,1)S(1)}, bf16[256,256]{1,0:T(8,128)(2,1)S(1)}, u32[]{:S(2)}, u32[]{:S(2)}) collective-permute-start(bf16[256,256]{1,0:T(8,128)(2,1)S(1)} %get-tuple-element.90), channel_id=1, source_target_pairs={{0,1},{1,2},{2,3},{3,4},{4,5},{5,6},{6,7},{7,0},{8,9},{9,10},{10,1... | collective-permute-start | bytes 393224 | tf_op jit(solution)/shard_map/ppermute | solution.py:45
  32.2 2.1 %collective-permute-start.3 = (bf16[4,272,256]{2,1,0:T(8,128)(2,1)S(1)}, bf16[4,272,256]{2,1,0:T(8,128)(2,1)S(1)}, u32[]{:S(2)}, u32[]{:S(2)}) collective-permute-start(bf16[4,272,256]{2,1,0:T(8,128)(2,1)S(1)} %pad_maximum_fusion.own_ref.refs_3_), channel_id=1, source_target_pairs={{0,32},{32,0},{64,96},{96,64},{128,160},{160,128},{192,224},{224,1... | collective-permute-start | bytes 1671176 | tf_op jit(solution)/shard_map/ppermute | solution.py:45
  38.1 1.5 collective-permute-start.13
  42.4 8.0 %forward_tiles.1 = (bf16[8,128,256]{2,1,0:T(8,128)(2,1)}, bf16[8,128,256]{2,1,0:T(8,128)(2,1)}, bf16[8,128,256]{2,1,0:T(8,128)(2,1)}, bf16[8,128,256]{2,1,0:T(8,...) custom-call(s32[4,144]{1,0:T(4,128)} %pad_add_fusion.meta_ref, ...), custom_call_target="tpu_custom_call" | custom-call | flops 1000000 | bytes 10000 | tf_op jit(solution)/shard_map/forward_tiles/pallas_call | solution.py:248
  50.4 2.6 %collective-permute-start.4 = (bf16[8,128,256]{2,1,0:T(8,128)(2,1)}, bf16[8,128,256]{2,1,0:T(8,128)(2,1)S(1)}, u32[]{:S(2)}, u32[]{:S(2)}) collective-permute-start(bf16[8,128,256]{2,1,0:T(8,128)(2,1)} %get-tuple-element.46), channel_id=1, source_target_pairs={{0,1},{1,2},{2,3},{3,4},{4,5},{5,6},{6,7},{7,0},{8,9},{9,10},{10,1... | collective-permute-start | bytes 1572872 | tf_op jit(solution)/shard_map/ppermute | solution.py:45
  52.9 8.7 %collective-permute-done.4 = bf16[8,128,256]{2,1,0:T(8,128)(2,1)S(1)} collective-permute-done((bf16[8,128,256]{2,1,0:T(8,128)(2,1)}, bf16[8,128,256]{2,1,0:T(8,128)(2,1)S(1)}, u32[]{:S(2)}, u32[]{:S(2)}) %collective-permute-start.4) | collective-permute-done | bytes 524320 | tf_op jit(solution)/shard_map/ppermute | solution.py:45
  61.7 2.5 %fusion.3 = (bf16[8,128,256]{2,1,0:T(8,128)(2,1)}, bf16[8,128,256]{2,1,0:T(8,128)(2,1)}) fusion(bf16[8,128,256]{2,1,0:T(8,128)(2,1)S(1)} %collective-permute-done.4, bf16[8,128,256]{2,1,0:T(8,128)(2,1)} %get-tuple-element.47, pred[]{:T(512)S(6)} %eq.38, bf16[8,128,256]{2,1,0:T(8,128)(2,1)} %get-tuple-element.45), kind=kLoop, calls=%fused_computation.8 | loop fusion | flops 2359296 | bytes 2621441 | tf_op jit(solution)/shard_map/convert_element_type | solution.py:382
  64.2 2.3 %collective-permute-start.14 = (bf16[8,128,256]{2,1,0:T(8,128)(2,1)}, bf16[8,128,256]{2,1,0:T(8,128)(2,1)}, u32[]{:S(2)}, u32[]{:S(2)}) collective-permute-start(bf16[8,128,256]{2,1,0:T(8,128)(2,1)} %get-tuple-element.48), channel_id=1, source_target_pairs={{0,1},{1,2},{2,3},{3,4},{4,5},{5,6},{6,7},{7,0},{8,9},{9,10},{10,1... | collective-permute-start | bytes 1572872 | tf_op jit(solution)/shard_map/ppermute | solution.py:45
  68.1 1.8 %collective-permute-start.23 = (bf16[16,128,256]{2,1,0:T(8,128)(2,1)}, bf16[16,128,256]{2,1,0:T(8,128)(2,1)S(1)}, u32[]{:S(2)}, u32[]{:S(2)}) collective-permute-start(bf16[16,128,256]{2,1,0:T(8,128)(2,1)} %broadcast_select_fusion), channel_id=1, source_target_pairs={{0,8},{1,9},{2,10},{3,11},{4,12},{5,13},{6,14},{7,15},{8,16},{9,17... | collective-permute-start | bytes 3145736 | tf_op jit(solution)/shard_map/ppermute | solution.py:45
  69.8 8.6 %backward_near.1 = (f32[16,128,128]{2,1,0:T(8,128)}, f32[16,128,128]{2,1,0:T(8,128)}, bf16[8,256,256]{2,1,0:T(8,128)(2,1)}, f32[8,128]{1,0:T(8,128)}) custom-call(s32[4,144]{1,0:T(4,128)} %pad_add_fusion.meta_ref, s32[3]{0:T(128)} %pad_add_fusion.1.scalars_ref, s32[144,128,128]{2,1,0:T(8,128)} %bitcast.73, bf16[16,128,256]{2,1,0:T(8,128)(2,1)} %bitcast.15.refs_0_, ...), custom_call_target="tpu_custom_call" | custom-call | flops 1000000 | bytes 10000 | tf_op jit(solution)/shard_map/backward_near/pallas_call | solution.py:270
  81.8 2.4 %collective-permute-start.16 = (bf16[8,128,256]{2,1,0:T(8,128)(2,1)S(1)}, bf16[8,128,256]{2,1,0:T(8,128)(2,1)}, u32[]{:S(2)}, u32[]{:S(2)}) collective-permute-start(bf16[8,128,256]{2,1,0:T(8,128)(2,1)S(1)} %add_convert_fusion.3), channel_id=1, source_target_pairs={{0,1},{1,2},{2,3},{3,4},{4,5},{5,6},{6,7},{7,0},{8,9},{9,10},{10,1... | collective-permute-start | bytes 1572872 | tf_op jit(solution)/shard_map/ppermute | solution.py:45
  85.3 6.7 %backward_far.1 = (f32[4,256,256]{2,1,0:T(8,128)}, bf16[4,256,256]{2,1,0:T(8,128)(2,1)}, f32[4,32,256]{2,1,0:T(8,128)}, f32[4,32,256]{2,1,0:T(8,128)}) custom-call(s32[4,144]{1,0:T(4,128)} %pad_add_fusion.meta_ref, s32[3]{0:T(128)} %pad_add_fusion.1.scalars_ref, s32[144,128,128]{2,1,0:T(8,128)} %bitcast.74, bf16[16,128,256]{2,1,0:T(8,128)(2,1)} %copy-done.4, ...), custom_call_target="tpu_custom_call" | custom-call | flops 1000000 | bytes 10000 | tf_op jit(solution)/shard_map/backward_far/pallas_call | solution.py:300
  92.0 5.7 %collective-permute-start.28 = (f32[4,32,256]{2,1,0:T(8,128)}, f32[4,32,256]{2,1,0:T(8,128)S(1)}, u32[]{:S(2)}, u32[]{:S(2)}) collective-permute-start(f32[4,32,256]{2,1,0:T(8,128)} %get-tuple-element.68), channel_id=1, source_target_pairs={{0,32},{32,0},{64,96},{96,64},{128,160},{160,128},{192,224},{224,1... | collective-permute-start | bytes 393224 | tf_op jit(solution)/shard_map/ppermute | solution.py:45
  97.9 3.6 %collective-permute-start.19 = (bf16[8,128,256]{2,1,0:T(8,128)(2,1)S(1)}, bf16[8,128,256]{2,1,0:T(8,128)(2,1)S(1)}, u32[]{:S(2)}, u32[]{:S(2)}) collective-permute-start(bf16[8,128,256]{2,1,0:T(8,128)(2,1)S(1)} %add_convert_fusion), channel_id=1, source_target_pairs={{0,7},{1,0},{2,1},{3,2},{4,3},{5,4},{6,5},{7,6},{8,15},{9,8},{10,9... | collective-permute-start | bytes 1572872 | tf_op jit(solution)/shard_map/ppermute | solution.py:45
  106.5 1.7 %collective-permute-done.30 = f32[32,256]{1,0:T(8,128)S(1)} collective-permute-done((f32[32,256]{1,0:T(8,128)S(1)}, f32[32,256]{1,0:T(8,128)S(1)}, u32[]{:S(2)}, u32[]{:S(2)}) %collective-permute-start.30) | collective-permute-done | bytes 32800 | tf_op jit(solution)/shard_map/ppermute | solution.py:45
  108.7 1.8 %collective-permute-start.33 = (f32[32,256]{1,0:T(8,128)S(1)}, f32[32,256]{1,0:T(8,128)S(1)}, u32[]{:S(2)}, u32[]{:S(2)}) collective-permute-start(f32[32,256]{1,0:T(8,128)S(1)} %fusion.9), channel_id=1, source_target_pairs={{0,16},{1,17},{2,18},{3,19},{4,20},{5,21},{6,22},{7,23},{8,24},{9,... | collective-permute-start | bytes 98312 | tf_op jit(solution)/shard_map/ppermute | solution.py:45
  111.4 2.9 %collective-permute-start.24 = (bf16[4,256,256]{2,1,0:T(8,128)(2,1)}, bf16[4,256,256]{2,1,0:T(8,128)(2,1)S(1)}, u32[]{:S(2)}, u32[]{:S(2)}) collective-permute-start(bf16[4,256,256]{2,1,0:T(8,128)(2,1)} %get-tuple-element.62), channel_id=1, source_target_pairs={{0,32},{32,0},{64,96},{96,64},{128,160},{160,128},{192,224},{224,1... | collective-permute-start | bytes 1572872 | tf_op jit(solution)/shard_map/ppermute | solution.py:45
  116.2 6.1 %all-to-all-start = ((f32[8,32,256]{2,1,0:T(8,128)}), f32[8,32,256]{2,1,0:T(8,128)S(1)}, u32[]{:S(2)}, u32[]{:S(2)}) async-start(f32[8,32,256]{2,1,0:T(8,128)} %broadcast_in_dim.62), calls=%async_computation | async-start | bytes 524288 | tf_op jit(solution)/shard_map/all_to_all | solution.py:49
  128.7 2.2 %fold_cores.1 = (f32[256,256]{1,0:T(8,128)}, bf16[256,256]{1,0:T(8,128)(2,1)}, bf16[256,256]{1,0:T(8,128)(2,1)}, bf16[256,256]{1,0:T(8,128)(2,1)}) custom-call(f32[4,256,256]{2,1,0:T(8,128)} %get-tuple-element.61.keep, bf16[4,256,256]{2,1,0:T(8,128)(2,1)} %copy-done.8), custom_call_target="tpu_custom_call" | custom-call | tf_op jit(solution)/shard_map/fold_cores/pallas_call | solution.py:359
  132.6 2.1 %collective-permute-start.35 = (f32[32,256]{1,0:T(8,128)S(1)}, f32[32,256]{1,0:T(8,128)S(1)}, u32[]{:S(2)}, u32[]{:S(2)}) collective-permute-start(f32[32,256]{1,0:T(8,128)S(1)} %reduce_sum.49), channel_id=1, source_target_pairs={{0,64},{32,96},{64,128},{96,160},{128,192},{160,224},{192,0},{224,... | collective-permute-start | bytes 98312 | tf_op jit(solution)/shard_map/ppermute | solution.py:45
  134.7 1.7 %collective-permute-start.36 = (f32[32,256]{1,0:T(8,128)S(1)}, f32[32,256]{1,0:T(8,128)S(1)}, u32[]{:S(2)}, u32[]{:S(2)}) collective-permute-start(f32[32,256]{1,0:T(8,128)S(1)} %reduce_sum.49), channel_id=1, source_target_pairs={{0,128},{32,160},{64,192},{96,224},{128,0},{160,32},{192,64},{224,... | collective-permute-start | bytes 98312 | tf_op jit(solution)/shard_map/ppermute | solution.py:45
  137.1 1.7 %collective-permute-start.37 = (f32[32,256]{1,0:T(8,128)S(1)}, f32[32,256]{1,0:T(8,128)S(1)}, u32[]{:S(2)}, u32[]{:S(2)}) collective-permute-start(f32[32,256]{1,0:T(8,128)S(1)} %reduce_sum.49), channel_id=1, source_target_pairs={{0,192},{32,224},{64,0},{96,32},{128,64},{160,96},{192,128},{224,1... | collective-permute-start | bytes 98312 | tf_op jit(solution)/shard_map/ppermute | solution.py:45
  138.9 1.8 %convolution_convert_fusion = bf16[256,256]{1,0:T(8,128)(2,1)} fusion(bf16[256,256]{1,0:T(8,128)(2,1)S(1)} %copy-done.5, f32[256,256]{1,0:T(8,128)} %get-tuple-element.63, bf16[256,256]{1,0:T(8,128)(2,1)S(1)} %collective-permute-done.27, bf16[256,256]{1,0:T(8,128)(2,1)S(1)} %collective-permute-done.26, bf16[256,256]{1,0:T(8,128)(2,1)S(1)} %collective-permute-done.25, ...), kind=kOutput, calls=%fused_computation.4 | convolution fusion | flops 34144256 | bytes 918528 | tf_op jit(solution)/shard_map/dot_general | solution.py:469
  140.8 4.5 %collective-permute-start.38 = (f32[4,32,256]{2,1,0:T(8,128)S(1)}, f32[4,32,256]{2,1,0:T(8,128)S(1)}, u32[]{:S(2)}, u32[]{:S(2)}) collective-permute-start(f32[4,32,256]{2,1,0:T(8,128)S(1)} %pad_maximum_fusion.2), channel_id=1, source_target_pairs={{0,32},{32,0},{64,96},{96,64},{128,160},{160,128},{192,224},{224,1... | collective-permute-start | bytes 393224 | tf_op jit(solution)/shard_map/ppermute | solution.py:45
  (132 shorter events, 41.3 us)
Async XLA Ops:
  2.2 29.8 %collective-permute-start.2 = (bf16[272,256]{1,0:T(8,128)(2,1)S(1)}, bf16[272,256]{1,0:T(8,128)(2,1)S(1)}, u32[]{:S(2)}, u32[]{:S(2)}) collective-permute-start(bf16[272,256]{1,0:T(8,128)(2,1)S(1)} %get-tuple-element.86), channel_id=1, source_target_pairs={{0,64},{32,96},{64,128},{96,160},{128,192},{160,224},{192,0},{224,... | collective-permute-start | bytes 417800 | tf_op jit(solution)/shard_map/ppermute | solution.py:45
  4.5 27.6 %collective-permute-start.1 = (bf16[272,256]{1,0:T(8,128)(2,1)S(1)}, bf16[272,256]{1,0:T(8,128)(2,1)S(1)}, u32[]{:S(2)}, u32[]{:S(2)}) collective-permute-start(bf16[272,256]{1,0:T(8,128)(2,1)S(1)} %get-tuple-element.86), channel_id=1, source_target_pairs={{0,128},{32,160},{64,192},{96,224},{128,0},{160,32},{192,64},{224,... | collective-permute-start | bytes 417800 | tf_op jit(solution)/shard_map/ppermute | solution.py:45
  7.1 25.0 %collective-permute-start = (bf16[272,256]{1,0:T(8,128)(2,1)S(1)}, bf16[272,256]{1,0:T(8,128)(2,1)S(1)}, u32[]{:S(2)}, u32[]{:S(2)}) collective-permute-start(bf16[272,256]{1,0:T(8,128)(2,1)S(1)} %get-tuple-element.86), channel_id=1, source_target_pairs={{0,192},{32,224},{64,0},{96,32},{128,64},{160,96},{192,128},{224,1... | collective-permute-start | bytes 417800 | tf_op jit(solution)/shard_map/ppermute | solution.py:45
  10.5 7.9 %collective-permute-start.8 = (bf16[256,256]{1,0:T(8,128)(2,1)S(1)}, bf16[256,256]{1,0:T(8,128)(2,1)S(1)}, u32[]{:S(2)}, u32[]{:S(2)}) collective-permute-start(bf16[256,256]{1,0:T(8,128)(2,1)S(1)} %get-tuple-element.72), channel_id=1, source_target_pairs={{0,1},{1,2},{2,3},{3,4},{4,5},{5,6},{6,7},{7,0},{8,9},{9,10},{10,1... | collective-permute-start | bytes 393224 | tf_op jit(solution)/shard_map/ppermute | solution.py:45
  12.1 6.3 %collective-permute-start.5 = (bf16[256,256]{1,0:T(8,128)(2,1)S(1)}, bf16[256,256]{1,0:T(8,128)(2,1)S(1)}, u32[]{:S(2)}, u32[]{:S(2)}) collective-permute-start(bf16[256,256]{1,0:T(8,128)(2,1)S(1)} %get-tuple-element.72), channel_id=1, source_target_pairs={{0,7},{1,0},{2,1},{3,2},{4,3},{5,4},{6,5},{7,6},{8,15},{9,8},{10,9... | collective-permute-start | bytes 393224 | tf_op jit(solution)/shard_map/ppermute | solution.py:45
  18.4 5.0 %collective-permute-start.9 = (bf16[256,256]{1,0:T(8,128)(2,1)S(1)}, bf16[256,256]{1,0:T(8,128)(2,1)S(1)}, u32[]{:S(2)}, u32[]{:S(2)}) collective-permute-start(bf16[256,256]{1,0:T(8,128)(2,1)S(1)} %collective-permute-done.8), channel_id=1, source_target_pairs={{0,1},{1,2},{2,3},{3,4},{4,5},{5,6},{6,7},{7,0},{8,9},{9,10},{10,1... | collective-permute-start | bytes 393224 | tf_op jit(solution)/shard_map/ppermute | solution.py:45
  18.4 5.0 %collective-permute-start.6 = (bf16[256,256]{1,0:T(8,128)(2,1)S(1)}, bf16[256,256]{1,0:T(8,128)(2,1)S(1)}, u32[]{:S(2)}, u32[]{:S(2)}) collective-permute-start(bf16[256,256]{1,0:T(8,128)(2,1)S(1)} %collective-permute-done.5), channel_id=1, source_target_pairs={{0,7},{1,0},{2,1},{3,2},{4,3},{5,4},{6,5},{7,6},{8,15},{9,8},{10,9... | collective-permute-start | bytes 393224 | tf_op jit(solution)/shard_map/ppermute | solution.py:45
  29.2 5.1 %collective-permute-start.11 = (bf16[256,256]{1,0:T(8,128)(2,1)S(1)}, bf16[256,256]{1,0:T(8,128)(2,1)S(1)}, u32[]{:S(2)}, u32[]{:S(2)}) collective-permute-start(bf16[256,256]{1,0:T(8,128)(2,1)S(1)} %get-tuple-element.90), channel_id=1, source_target_pairs={{0,1},{1,2},{2,3},{3,4},{4,5},{5,6},{6,7},{7,0},{8,9},{9,10},{10,1... | collective-permute-start | bytes 393224 | tf_op jit(solution)/shard_map/ppermute | solution.py:45
  32.2 9.4 %collective-permute-start.3 = (bf16[4,272,256]{2,1,0:T(8,128)(2,1)S(1)}, bf16[4,272,256]{2,1,0:T(8,128)(2,1)S(1)}, u32[]{:S(2)}, u32[]{:S(2)}) collective-permute-start(bf16[4,272,256]{2,1,0:T(8,128)(2,1)S(1)} %pad_maximum_fusion.own_ref.refs_3_), channel_id=1, source_target_pairs={{0,32},{32,0},{64,96},{96,64},{128,160},{160,128},{192,224},{224,1... | collective-permute-start | bytes 1671176 | tf_op jit(solution)/shard_map/ppermute | solution.py:45
  36.9 27.3 %collective-permute-start.12 = (bf16[16,128,256]{2,1,0:T(8,128)(2,1)}, bf16[16,128,256]{2,1,0:T(8,128)(2,1)S(1)}, u32[]{:S(2)}, u32[]{:S(2)}) collective-permute-start(bf16[16,128,256]{2,1,0:T(8,128)(2,1)} %bitcast.15.refs_0_), channel_id=1, source_target_pairs={{0,8},{1,9},{2,10},{3,11},{4,12},{5,13},{6,14},{7,15},{8,16},{9,17... | collective-permute-start | bytes 3145736 | tf_op jit(solution)/shard_map/ppermute | solution.py:45
  38.1 26.1 %collective-permute-start.13 = (bf16[16,128,256]{2,1,0:T(8,128)(2,1)}, bf16[16,128,256]{2,1,0:T(8,128)(2,1)S(1)}, u32[]{:S(2)}, u32[]{:S(2)}) collective-permute-start(bf16[16,128,256]{2,1,0:T(8,128)(2,1)} %bitcast.15.refs_0_), channel_id=1, source_target_pairs={{0,24},{1,25},{2,26},{3,27},{4,28},{5,29},{6,30},{7,31},{8,0},{9,1... | collective-permute-start | bytes 3145736 | tf_op jit(solution)/shard_map/ppermute | solution.py:45
  50.4 11.3 %collective-permute-start.4 = (bf16[8,128,256]{2,1,0:T(8,128)(2,1)}, bf16[8,128,256]{2,1,0:T(8,128)(2,1)S(1)}, u32[]{:S(2)}, u32[]{:S(2)}) collective-permute-start(bf16[8,128,256]{2,1,0:T(8,128)(2,1)} %get-tuple-element.46), channel_id=1, source_target_pairs={{0,1},{1,2},{2,3},{3,4},{4,5},{5,6},{6,7},{7,0},{8,9},{9,10},{10,1... | collective-permute-start | bytes 1572872 | tf_op jit(solution)/shard_map/ppermute | solution.py:45
  64.2 14.2 %collective-permute-start.14 = (bf16[8,128,256]{2,1,0:T(8,128)(2,1)}, bf16[8,128,256]{2,1,0:T(8,128)(2,1)}, u32[]{:S(2)}, u32[]{:S(2)}) collective-permute-start(bf16[8,128,256]{2,1,0:T(8,128)(2,1)} %get-tuple-element.48), channel_id=1, source_target_pairs={{0,1},{1,2},{2,3},{3,4},{4,5},{5,6},{6,7},{7,0},{8,9},{9,10},{10,1... | collective-permute-start | bytes 1572872 | tf_op jit(solution)/shard_map/ppermute | solution.py:45
  66.5 13.3 %collective-permute-start.15 = (bf16[8,128,256]{2,1,0:T(8,128)(2,1)}, bf16[8,128,256]{2,1,0:T(8,128)(2,1)}, u32[]{:S(2)}, u32[]{:S(2)}) collective-permute-start(bf16[8,128,256]{2,1,0:T(8,128)(2,1)} %get-tuple-element.50), channel_id=1, source_target_pairs={{0,7},{1,0},{2,1},{3,2},{4,3},{5,4},{6,5},{7,6},{8,15},{9,8},{10,9... | collective-permute-start | bytes 1572872 | tf_op jit(solution)/shard_map/ppermute | solution.py:45
  68.1 16.2 %collective-permute-start.23 = (bf16[16,128,256]{2,1,0:T(8,128)(2,1)}, bf16[16,128,256]{2,1,0:T(8,128)(2,1)S(1)}, u32[]{:S(2)}, u32[]{:S(2)}) collective-permute-start(bf16[16,128,256]{2,1,0:T(8,128)(2,1)} %broadcast_select_fusion), channel_id=1, source_target_pairs={{0,8},{1,9},{2,10},{3,11},{4,12},{5,13},{6,14},{7,15},{8,16},{9,17... | collective-permute-start | bytes 3145736 | tf_op jit(solution)/shard_map/ppermute | solution.py:45
  81.0 16.7 %collective-permute-start.18 = (bf16[8,128,256]{2,1,0:T(8,128)(2,1)S(1)}, bf16[8,128,256]{2,1,0:T(8,128)(2,1)S(1)}, u32[]{:S(2)}, u32[]{:S(2)}) collective-permute-start(bf16[8,128,256]{2,1,0:T(8,128)(2,1)S(1)} %add_convert_fusion.2), channel_id=1, source_target_pairs={{0,7},{1,0},{2,1},{3,2},{4,3},{5,4},{6,5},{7,6},{8,15},{9,8},{10,9... | collective-permute-start | bytes 1572872 | tf_op jit(solution)/shard_map/ppermute | solution.py:45
  81.8 22.1 %collective-permute-start.16 = (bf16[8,128,256]{2,1,0:T(8,128)(2,1)S(1)}, bf16[8,128,256]{2,1,0:T(8,128)(2,1)}, u32[]{:S(2)}, u32[]{:S(2)}) collective-permute-start(bf16[8,128,256]{2,1,0:T(8,128)(2,1)S(1)} %add_convert_fusion.3), channel_id=1, source_target_pairs={{0,1},{1,2},{2,3},{3,4},{4,5},{5,6},{6,7},{7,0},{8,9},{9,10},{10,1... | collective-permute-start | bytes 1572872 | tf_op jit(solution)/shard_map/ppermute | solution.py:45
  92.0 9.4 %collective-permute-start.28 = (f32[4,32,256]{2,1,0:T(8,128)}, f32[4,32,256]{2,1,0:T(8,128)S(1)}, u32[]{:S(2)}, u32[]{:S(2)}) collective-permute-start(f32[4,32,256]{2,1,0:T(8,128)} %get-tuple-element.68), channel_id=1, source_target_pairs={{0,32},{32,0},{64,96},{96,64},{128,160},{160,128},{192,224},{224,1... | collective-permute-start | bytes 393224 | tf_op jit(solution)/shard_map/ppermute | solution.py:45
  97.9 24.4 %collective-permute-start.19 = (bf16[8,128,256]{2,1,0:T(8,128)(2,1)S(1)}, bf16[8,128,256]{2,1,0:T(8,128)(2,1)S(1)}, u32[]{:S(2)}, u32[]{:S(2)}) collective-permute-start(bf16[8,128,256]{2,1,0:T(8,128)(2,1)S(1)} %add_convert_fusion), channel_id=1, source_target_pairs={{0,7},{1,0},{2,1},{3,2},{4,3},{5,4},{6,5},{7,6},{8,15},{9,8},{10,9... | collective-permute-start | bytes 1572872 | tf_op jit(solution)/shard_map/ppermute | solution.py:45
  105.1 17.2 %collective-permute-start.17 = (bf16[8,128,256]{2,1,0:T(8,128)(2,1)S(1)}, bf16[8,128,256]{2,1,0:T(8,128)(2,1)S(1)}, u32[]{:S(2)}, u32[]{:S(2)}) collective-permute-start(bf16[8,128,256]{2,1,0:T(8,128)(2,1)S(1)} %add_convert_fusion.1), channel_id=1, source_target_pairs={{0,1},{1,2},{2,3},{3,4},{4,5},{5,6},{6,7},{7,0},{8,9},{9,10},{10,1... | collective-permute-start | bytes 1572872 | tf_op jit(solution)/shard_map/ppermute | solution.py:45
  108.7 5.5 %collective-permute-start.33 = (f32[32,256]{1,0:T(8,128)S(1)}, f32[32,256]{1,0:T(8,128)S(1)}, u32[]{:S(2)}, u32[]{:S(2)}) collective-permute-start(f32[32,256]{1,0:T(8,128)S(1)} %fusion.9), channel_id=1, source_target_pairs={{0,16},{1,17},{2,18},{3,19},{4,20},{5,21},{6,22},{7,23},{8,24},{9,... | collective-permute-start | bytes 98312 | tf_op jit(solution)/shard_map/ppermute | solution.py:45
  111.4 16.5 %collective-permute-start.24 = (bf16[4,256,256]{2,1,0:T(8,128)(2,1)}, bf16[4,256,256]{2,1,0:T(8,128)(2,1)S(1)}, u32[]{:S(2)}, u32[]{:S(2)}) collective-permute-start(bf16[4,256,256]{2,1,0:T(8,128)(2,1)} %get-tuple-element.62), channel_id=1, source_target_pairs={{0,32},{32,0},{64,96},{96,64},{128,160},{160,128},{192,224},{224,1... | collective-permute-start | bytes 1572872 | tf_op jit(solution)/shard_map/ppermute | solution.py:45
  116.2 16.2 %all-to-all-start = ((f32[8,32,256]{2,1,0:T(8,128)}), f32[8,32,256]{2,1,0:T(8,128)S(1)}, u32[]{:S(2)}, u32[]{:S(2)}) async-start(f32[8,32,256]{2,1,0:T(8,128)} %broadcast_in_dim.62), calls=%async_computation | async-start | bytes 524288 | tf_op jit(solution)/shard_map/all_to_all | solution.py:49
  123.6 8.8 %collective-permute-start.22 = (bf16[256,256]{1,0:T(8,128)(2,1)S(1)}, bf16[256,256]{1,0:T(8,128)(2,1)S(1)}, u32[]{:S(2)}, u32[]{:S(2)}) collective-permute-start(bf16[256,256]{1,0:T(8,128)(2,1)S(1)} %bitcast.81), channel_id=1, source_target_pairs={{0,24},{1,25},{2,26},{3,27},{4,28},{5,29},{6,30},{7,31},{8,0},{9,1... | collective-permute-start | bytes 393224 | tf_op jit(solution)/shard_map/ppermute | solution.py:45
  125.0 7.6 %collective-permute-start.21 = (bf16[256,256]{1,0:T(8,128)(2,1)S(1)}, bf16[256,256]{1,0:T(8,128)(2,1)S(1)}, u32[]{:S(2)}, u32[]{:S(2)}) collective-permute-start(bf16[256,256]{1,0:T(8,128)(2,1)S(1)} %bitcast.80), channel_id=1, source_target_pairs={{0,16},{1,17},{2,18},{3,19},{4,20},{5,21},{6,22},{7,23},{8,24},{9,... | collective-permute-start | bytes 393224 | tf_op jit(solution)/shard_map/ppermute | solution.py:45
  126.3 8.4 %collective-permute-start.20 = (bf16[256,256]{1,0:T(8,128)(2,1)S(1)}, bf16[256,256]{1,0:T(8,128)(2,1)S(1)}, u32[]{:S(2)}, u32[]{:S(2)}) collective-permute-start(bf16[256,256]{1,0:T(8,128)(2,1)S(1)} %bitcast.79), channel_id=1, source_target_pairs={{0,8},{1,9},{2,10},{3,11},{4,12},{5,13},{6,14},{7,15},{8,16},{9,17... | collective-permute-start | bytes 393224 | tf_op jit(solution)/shard_map/ppermute | solution.py:45
  130.9 6.3 %collective-permute-start.27 = (bf16[256,256]{1,0:T(8,128)(2,1)}, bf16[256,256]{1,0:T(8,128)(2,1)S(1)}, u32[]{:S(2)}, u32[]{:S(2)}) collective-permute-start(bf16[256,256]{1,0:T(8,128)(2,1)} %get-tuple-element.66), channel_id=1, source_target_pairs={{0,192},{32,224},{64,0},{96,32},{128,64},{160,96},{192,128},{224,1... | collective-permute-start | bytes 393224 | tf_op jit(solution)/shard_map/ppermute | solution.py:45
  131.9 7.0 %collective-permute-start.26 = (bf16[256,256]{1,0:T(8,128)(2,1)}, bf16[256,256]{1,0:T(8,128)(2,1)S(1)}, u32[]{:S(2)}, u32[]{:S(2)}) collective-permute-start(bf16[256,256]{1,0:T(8,128)(2,1)} %get-tuple-element.65), channel_id=1, source_target_pairs={{0,128},{32,160},{64,192},{96,224},{128,0},{160,32},{192,64},{224,... | collective-permute-start | bytes 393224 | tf_op jit(solution)/shard_map/ppermute | solution.py:45
  132.4 6.5 %collective-permute-start.25 = (bf16[256,256]{1,0:T(8,128)(2,1)}, bf16[256,256]{1,0:T(8,128)(2,1)S(1)}, u32[]{:S(2)}, u32[]{:S(2)}) collective-permute-start(bf16[256,256]{1,0:T(8,128)(2,1)} %get-tuple-element.64), channel_id=1, source_target_pairs={{0,64},{32,96},{64,128},{96,160},{128,192},{160,224},{192,0},{224,... | collective-permute-start | bytes 393224 | tf_op jit(solution)/shard_map/ppermute | solution.py:45
  132.6 8.1 %collective-permute-start.35 = (f32[32,256]{1,0:T(8,128)S(1)}, f32[32,256]{1,0:T(8,128)S(1)}, u32[]{:S(2)}, u32[]{:S(2)}) collective-permute-start(f32[32,256]{1,0:T(8,128)S(1)} %reduce_sum.49), channel_id=1, source_target_pairs={{0,64},{32,96},{64,128},{96,160},{128,192},{160,224},{192,0},{224,... | collective-permute-start | bytes 98312 | tf_op jit(solution)/shard_map/ppermute | solution.py:45
  134.7 6.1 %collective-permute-start.36 = (f32[32,256]{1,0:T(8,128)S(1)}, f32[32,256]{1,0:T(8,128)S(1)}, u32[]{:S(2)}, u32[]{:S(2)}) collective-permute-start(f32[32,256]{1,0:T(8,128)S(1)} %reduce_sum.49), channel_id=1, source_target_pairs={{0,128},{32,160},{64,192},{96,224},{128,0},{160,32},{192,64},{224,... | collective-permute-start | bytes 98312 | tf_op jit(solution)/shard_map/ppermute | solution.py:45
  140.8 5.5 %collective-permute-start.38 = (f32[4,32,256]{2,1,0:T(8,128)S(1)}, f32[4,32,256]{2,1,0:T(8,128)S(1)}, u32[]{:S(2)}, u32[]{:S(2)}) collective-permute-start(f32[4,32,256]{2,1,0:T(8,128)S(1)} %pad_maximum_fusion.2), channel_id=1, source_target_pairs={{0,32},{32,0},{64,96},{96,64},{128,160},{160,128},{192,224},{224,1... | collective-permute-start | bytes 393224 | tf_op jit(solution)/shard_map/ppermute | solution.py:45
  (19 other events, 180.8 us)

commit v4 on v3

--- a/solution.py
+++ b/solution.py
@@ -165,7 +165,7 @@
 
 def backward_far_kernel(
     base, meta_ref, scalars_ref, edges_hbm, piece, near_left, near_right, features_hbm, _,
-    keep_ref, far_ref, terms_keep_ref, terms_far_ref,
+    back_ref, terms_keep_ref, terms_far_ref,
     left, right, upstream, features_ref, terms, edges, sems, input_sems,
 ):
     row, count = scalars_ref[1], scalars_ref[2]
@@ -220,10 +220,7 @@
             ],
             axis=1,
         )
-        if far:
-            far_ref[dy] = value.astype(jnp.bfloat16)
-        else:
-            keep_ref[dy] = value
+        back_ref[((y + dy) % Y) * 2 + (core + far) % 2] = value.astype(jnp.bfloat16)
         term = jnp.dot(
             features_ref[block], value.astype(jnp.bfloat16), preferred_element_type=jnp.float32
         )
@@ -295,7 +292,7 @@
     width = piece.shape[-1]
     rows = width // (2 * Y)
     f32, bf16 = jnp.float32, jnp.bfloat16
-    outs = [((Y, 2 * size, width), f32), ((Y, 2 * size, width), bf16)]
+    outs = [((2 * Y, 2 * size, width), bf16)]
     outs += [((Y, rows, width), f32)] * 2
     return pl.pallas_call(
         functools.partial(backward_far_kernel, place),
@@ -318,6 +315,23 @@
     )(meta, scalars, edges, piece, left, right, features, after)
 
 
+def join_kernel(*refs):
+    *parts, out = refs
+    for k, part in enumerate(parts):
+        out[pl.ds(k * part.shape[0], part.shape[0])] = part[...]
+
+
+def join(parts, size):
+    rows, width = parts[0].shape
+    whole = pl.pallas_call(
+        join_kernel,
+        out_shape=jax.ShapeDtypeStruct((len(parts) * rows, width), parts[0].dtype),
+        cost_estimate=pl.CostEstimate(flops=10**6, bytes_accessed=10**4, transcendentals=0),
+        name="join",
+    )(*parts)
+    return whole.reshape(-1, size, width)
+
+
 def gather_z(own, size, core):
     parts = {0: own}
     up = down = own
@@ -325,7 +339,7 @@
         up, down = send(up, "col", along_z(1)), send(down, "col", along_z(-1))
         parts[Z - k], parts[k] = up, down
     parts[Z // 2] = send(jnp.where(core == 0, up, down), ("row", "col"), by_core(along_z))
-    return jnp.concatenate([parts[k] for k in range(Z)]).reshape(2 * Z, size, -1)
+    return parts[Z // 2 - 1], join([parts[k] for k in range(Z)], size)
 
 
 def gather_x(plane, core):
@@ -347,26 +361,6 @@
     return mine, send(mine, "row", OTHER_CORE)
 
 
-def fold_cores_kernel(keep, recv, own, *outs):
-    own[...] = keep[0] + recv[0].astype(jnp.float32)
-    for d, out in enumerate(outs, 1):
-        out[...] = (keep[d] + recv[d].astype(jnp.float32)).astype(out.dtype)
-
-
-def scatter_row(keep, far):
-    recv = send(far, "row", OTHER_CORE)
-    shape = keep.shape[1:]
-    own, *parts = pl.pallas_call(
-        fold_cores_kernel,
-        out_shape=[jax.ShapeDtypeStruct(shape, jnp.float32)]
-        + [jax.ShapeDtypeStruct(shape, far.dtype)] * (Y - 1),
-        name="fold_cores",
-    )(keep, recv)
-    return own + sum(
-        send(part, "row", along_y(d)).astype(jnp.float32) for d, part in enumerate(parts, 1)
-    )
-
-
 def all_rows(value, y, core):
     mine = jnp.stack([value] + [send(value, "row", along_y(d)) for d in range(1, Y)])
     got = jnp.concatenate([mine, send(mine, "row", OTHER_CORE)])
@@ -408,7 +402,9 @@
 
 
 def sum_z(value):
-    return jnp.sum(exchange_z(jnp.broadcast_to(value, (Z,) + value.shape)), axis=0)
+    for bit in (1, 2, 4):
+        value = value + send(value, "col", [(a, a ^ bit) for a in range(X * Z)])
+    return value
 
 
 def shards(features, weight, tile_coords, tile_live, tile_edges, row_degree, col_degree, cotangent):
@@ -423,10 +419,11 @@
     y, core = row // 2, row % 2
 
     upstream = (row_scale[:, None] * cotangent.astype(f32)).astype(bf16)
-    plane = gather_z(upstream, size, core)
+    arrived, plane = gather_z(upstream, size, core)
 
     degrees = jnp.zeros((16, width), bf16).at[0].set(col_degree.astype(bf16))
-    mine, other = gather_row(jnp.concatenate([features, degrees]))
+    sent, _ = lax.optimization_barrier((jnp.concatenate([features, degrees]), arrived))
+    mine, other = gather_row(sent)
 
     owner, half = coords[:, 0] // 2, coords[:, 0] % 2
     dx = (owner // Z - col // Z) % X
@@ -454,7 +451,7 @@
     up, down = fold(received, parts[2:4])
     up, down, token = lax.optimization_barrier((up, down, token))
     received = scatter_round(up, down)
-    keep, far, terms_keep, terms_far = backward_far(
+    back, terms_keep, terms_far = backward_far(
         meta, scalars, edges, last, places[-1], *sums, token
     )
     received = scatter_round(*fold(received, parts[4:6]))
@@ -462,9 +459,10 @@
 
     terms = terms_keep + send(terms_far, "row", OTHER_CORE)
     terms = terms[0] + sum(send(terms[d], "row", along_y(d)) for d in range(1, Y))
-    terms = sum_x(terms, col // Z)
-    grad_weight = all_rows(sum_z(terms), y, core)
-    back = scatter_row(keep, far)
+    back = lax.all_to_all(back, "row", 0, 0)
+    terms, back = lax.optimization_barrier((sum_z(sum_x(terms, col // Z)), back))
+    grad_weight = all_rows(terms, y, core)
+    back = jnp.sum(back.astype(f32), axis=0)
     grad_panel = (col_scale[:, None] * back).astype(bf16)
     grad_features = jnp.dot(grad_panel, weight.T, preferred_element_type=f32).astype(bf16)
     return aggregated, grad_features, grad_weight

time: 148 us -> 149 us (level)
  waiting for transfers between devices: 16.5 us -> 24.3 us
  local copies, waits for them, and re-layouts: 8.78 us -> 3.93 us
  starting transfers between devices: 71.8 us -> 74.1 us
  other arithmetic: 21.6 us -> 19.6 us
    ppermute x39 -> x38, waiting for transfers between devices: 16.5 us -> 22.8 us  [send(): return lax.ppermute(value, axis, pairs)]
    unnamed x31 -> x40, local copies, waits for them, and re-layouts: 6.01 us -> 2.58 us
    all_to_all x1, starting transfers between devices: 6.07 us -> 9.22 us  [shards(): back = lax.all_to_all(back, 'row', 0, 0)]
    unnamed x1 -> x0, other arithmetic: 1.67 us -> none
    all_to_all x1, waiting for transfers between devices: 0.01 us -> 1.54 us  [shards(): back = lax.all_to_all(back, 'row', 0, 0)]
    ppermute x39 -> x38, starting transfers between devices: 65.8 us -> 64.9 us  [send(): return lax.ppermute(value, axis, pairs)]
  transfers between devices with their start and end apart: 40 -> 39, of which waited for: 10 -> 16; matrix products, arithmetic and copies ran while one was open for 18% -> 13% of each run, Pallas kernels for 17% -> 16%
where the time goes in v4:
time: 149 us
  starting transfers between devices  74.1 us (50%)
  Pallas kernels  24.4 us (16%)
  waiting for transfers between devices  24.3 us (16%)
  other arithmetic  19.6 us (13%)
  local copies, waits for them, and re-layouts  3.93 us (3%)
  between operations  1.82 us (1%)
    ppermute x38, starting transfers between devices, send(): return lax.ppermute(value, axis, pairs)  64.9 us
    ppermute x38, waiting for transfers between devices, send(): return lax.ppermute(value, axis, pairs)  22.8 us
    all_to_all x1, starting transfers between devices, shards(): back = lax.all_to_all(back, 'row', 0, 0)  9.22 us
    pallas_call x1, Pallas kernels, backward_near(): pl.pallas_call(functools.partial(backward_near_kernel, base, places), in_...  8.08 us
    pallas_call x1, Pallas kernels, forward(): pl.pallas_call(functools.partial(forward_kernel, len(deps)), in_specs=[SM...  7.49 us
    pallas_call x1, Pallas kernels, backward_far(): pl.pallas_call(functools.partial(backward_far_kernel, place), in_specs=[S...  6.44 us
    convert_element_type x4, other arithmetic, fold(): (b.astype(jnp.float32) + a.astype(jnp.float32)).astype(a.dtype)  3.87 us
  transfers between devices with their start and end apart: 39, of which 16 were waited for; matrix products, arithmetic and copies ran while one was open for 13% of the time, Pallas kernels for 16%

profile of v4, /device:TPU:1, one launch (start us, length us, event | category | flops | bytes accessed | tf_op | source)
XLA Modules:
  0.0 149.0 jit_solution(5011477904162152277)
XLA Ops:
  2.3 6.5 %collective-permute-start = (bf16[256,256]{1,0:T(8,128)(2,1)S(1)}, bf16[256,256]{1,0:T(8,128)(2,1)S(1)}, u32[]{:S(2)}, u32[]{:S(2)}) collective-permute-start(bf16[256,256]{1,0:T(8,128)(2,1)S(1)} %multiply_convert_fusion.1.refs_0_), channel_id=1, source_target_pairs={{0,7},{1,0},{2,1},{3,2},{4,3},{5,4},{6,5},{7,6},{8,15},{9,8},{10,9... | collective-permute-start | bytes 393224 | tf_op jit(solution)/shard_map/ppermute | solution.py:45
  11.0 3.4 %collective-permute-start.1 = (bf16[256,256]{1,0:T(8,128)(2,1)S(1)}, bf16[256,256]{1,0:T(8,128)(2,1)S(1)}, u32[]{:S(2)}, u32[]{:S(2)}) collective-permute-start(bf16[256,256]{1,0:T(8,128)(2,1)S(1)} %collective-permute-done.refs_1_), channel_id=1, source_target_pairs={{0,7},{1,0},{2,1},{3,2},{4,3},{5,4},{6,5},{7,6},{8,15},{9,8},{10,9... | collective-permute-start | bytes 393224 | tf_op jit(solution)/shard_map/ppermute | solution.py:45
  16.4 3.1 %collective-permute-start.2 = (bf16[256,256]{1,0:T(8,128)(2,1)S(1)}, bf16[256,256]{1,0:T(8,128)(2,1)S(1)}, u32[]{:S(2)}, u32[]{:S(2)}) collective-permute-start(bf16[256,256]{1,0:T(8,128)(2,1)S(1)} %collective-permute-done.1.refs_2_), channel_id=1, source_target_pairs={{0,7},{1,0},{2,1},{3,2},{4,3},{5,4},{6,5},{7,6},{8,15},{9,8},{10,9... | collective-permute-start | bytes 393224 | tf_op jit(solution)/shard_map/ppermute | solution.py:45
  21.4 1.3 collective-permute-start.5
  22.7 2.6 %collective-permute-start.4 = (bf16[272,256]{1,0:T(8,128)(2,1)S(1)}, bf16[272,256]{1,0:T(8,128)(2,1)S(1)}, u32[]{:S(2)}, u32[]{:S(2)}) collective-permute-start(bf16[272,256]{1,0:T(8,128)(2,1)S(1)} %fusion.7), channel_id=1, source_target_pairs={{0,128},{32,160},{64,192},{96,224},{128,0},{160,32},{192,64},{224,... | collective-permute-start | bytes 417800 | tf_op jit(solution)/shard_map/ppermute | solution.py:45
  26.4 3.2 %collective-permute-start.11 = (bf16[256,256]{1,0:T(8,128)(2,1)S(1)}, bf16[256,256]{1,0:T(8,128)(2,1)S(1)}, u32[]{:S(2)}, u32[]{:S(2)}) collective-permute-start(bf16[256,256]{1,0:T(8,128)(2,1)S(1)} %broadcast_select_fusion.1), channel_id=1, source_target_pairs={{0,1},{1,2},{2,3},{3,4},{4,5},{5,6},{6,7},{7,0},{8,9},{9,10},{10,1... | collective-permute-start | bytes 393224 | tf_op jit(solution)/shard_map/ppermute | solution.py:45
  29.7 5.0 %collective-permute-start.6 = (bf16[4,272,256]{2,1,0:T(8,128)(2,1)S(1)}, bf16[4,272,256]{2,1,0:T(8,128)(2,1)S(1)}, u32[]{:S(2)}, u32[]{:S(2)}) collective-permute-start(bf16[4,272,256]{2,1,0:T(8,128)(2,1)S(1)} %pad_maximum_fusion.own_ref.refs_3_), channel_id=1, source_target_pairs={{0,32},{32,0},{64,96},{96,64},{128,160},{160,128},{192,224},{224,1... | collective-permute-start | bytes 1671176 | tf_op jit(solution)/shard_map/ppermute | solution.py:45
  36.3 2.3 %join.1 = bf16[2048,256]{1,0:T(8,128)(2,1)} custom-call(bf16[256,256]{1,0:T(8,128)(2,1)} %copy-done.9, bf16[256,256]{1,0:T(8,128)(2,1)} %copy-done.12, bf16[256,256]{1,0:T(8,128)(2,1)} %copy-done.14, bf16[256,256]{1,0:T(8,128)(2,1)} %copy-done.10, bf16[256,256]{1,0:T(8,128)(2,1)} %copy-done.16, bf16[256,256]{1,0:T(8,128)(2,1)} %copy-done.11, ...), custom_call_target="tpu_custom_call" | custom-call | flops 1000000 | bytes 10000 | tf_op jit(solution)/shard_map/join/pallas_call | solution.py:326
  39.9 1.5 collective-permute-start.13
  41.3 1.3 pad_add_fusion.1.scalars_ref
  44.2 7.5 %forward_tiles.1 = (bf16[8,128,256]{2,1,0:T(8,128)(2,1)}, bf16[8,128,256]{2,1,0:T(8,128)(2,1)}, bf16[8,128,256]{2,1,0:T(8,128)(2,1)}, bf16[8,128,256]{2,1,0:T(8,...) custom-call(s32[4,144]{1,0:T(4,128)} %pad_add_fusion.meta_ref, ...), custom_call_target="tpu_custom_call" | custom-call | flops 1000000 | bytes 10000 | tf_op jit(solution)/shard_map/forward_tiles/pallas_call | solution.py:245
  51.7 5.3 %collective-permute-start.7 = (bf16[8,128,256]{2,1,0:T(8,128)(2,1)}, bf16[8,128,256]{2,1,0:T(8,128)(2,1)S(1)}, u32[]{:S(2)}, u32[]{:S(2)}) collective-permute-start(bf16[8,128,256]{2,1,0:T(8,128)(2,1)} %get-tuple-element.45), channel_id=1, source_target_pairs={{0,1},{1,2},{2,3},{3,4},{4,5},{5,6},{6,7},{7,0},{8,9},{9,10},{10,1... | collective-permute-start | bytes 1572872 | tf_op jit(solution)/shard_map/ppermute | solution.py:45
  57.1 6.4 %collective-permute-done.7 = bf16[8,128,256]{2,1,0:T(8,128)(2,1)S(1)} collective-permute-done((bf16[8,128,256]{2,1,0:T(8,128)(2,1)}, bf16[8,128,256]{2,1,0:T(8,128)(2,1)S(1)}, u32[]{:S(2)}, u32[]{:S(2)}) %collective-permute-start.7) | collective-permute-done | bytes 524320 | tf_op jit(solution)/shard_map/ppermute | solution.py:45
  63.5 2.5 %fusion.3 = (bf16[8,128,256]{2,1,0:T(8,128)(2,1)}, bf16[8,128,256]{2,1,0:T(8,128)(2,1)}) fusion(bf16[8,128,256]{2,1,0:T(8,128)(2,1)S(1)} %collective-permute-done.7, bf16[8,128,256]{2,1,0:T(8,128)(2,1)} %get-tuple-element.46, pred[]{:T(512)S(6)} %eq.38, bf16[8,128,256]{2,1,0:T(8,128)(2,1)} %get-tuple-element.44), kind=kLoop, calls=%fused_computation.9 | loop fusion | flops 2359296 | bytes 2621441 | tf_op jit(solution)/shard_map/convert_element_type | solution.py:376
  66.1 3.4 %collective-permute-start.15 = (bf16[8,128,256]{2,1,0:T(8,128)(2,1)}, bf16[8,128,256]{2,1,0:T(8,128)(2,1)}, u32[]{:S(2)}, u32[]{:S(2)}) collective-permute-start(bf16[8,128,256]{2,1,0:T(8,128)(2,1)} %get-tuple-element.49), channel_id=1, source_target_pairs={{0,7},{1,0},{2,1},{3,2},{4,3},{5,4},{6,5},{7,6},{8,15},{9,8},{10,9... | collective-permute-start | bytes 1572872 | tf_op jit(solution)/shard_map/ppermute | solution.py:45
  71.5 8.1 %backward_near.1 = (f32[16,128,128]{2,1,0:T(8,128)}, f32[16,128,128]{2,1,0:T(8,128)}, bf16[8,256,256]{2,1,0:T(8,128)(2,1)}, f32[8,128]{1,0:T(8,128)}) custom-call(s32[4,144]{1,0:T(4,128)} %pad_add_fusion.meta_ref, s32[3]{0:T(128)} %pad_add_fusion.1.scalars_ref, s32[144,128,128]{2,1,0:T(8,128)} %bitcast.72, bf16[16,128,256]{2,1,0:T(8,128)(2,1)} %bitcast.76, ...), custom_call_target="tpu_custom_call" | custom-call | flops 1000000 | bytes 10000 | tf_op jit(solution)/shard_map/backward_near/pallas_call | solution.py:267
  79.6 1.4 add_convert_fusion.3
  82.2 4.0 %collective-permute-start.18 = (bf16[8,128,256]{2,1,0:T(8,128)(2,1)S(1)}, bf16[8,128,256]{2,1,0:T(8,128)(2,1)}, u32[]{:S(2)}, u32[]{:S(2)}) collective-permute-start(bf16[8,128,256]{2,1,0:T(8,128)(2,1)S(1)} %add_convert_fusion.2), channel_id=1, source_target_pairs={{0,7},{1,0},{2,1},{3,2},{4,3},{5,4},{6,5},{7,6},{8,15},{9,8},{10,9... | collective-permute-start | bytes 1572872 | tf_op jit(solution)/shard_map/ppermute | solution.py:45
  87.3 6.4 %backward_far.1 = (bf16[8,256,256]{2,1,0:T(8,128)(2,1)}, f32[4,32,256]{2,1,0:T(8,128)}, f32[4,32,256]{2,1,0:T(8,128)}) custom-call(s32[4,144]{1,0:T(4,128)} %pad_add_fusion.meta_ref, s32[3]{0:T(128)} %pad_add_fusion.1.scalars_ref, s32[144,128,128]{2,1,0:T(8,128)} %bitcast.73, bf16[16,128,256]{2,1,0:T(8,128)(2,1)} %copy-done.4, ...), custom_call_target="tpu_custom_call" | custom-call | flops 1000000 | bytes 10000 | tf_op jit(solution)/shard_map/backward_far/pallas_call | solution.py:297
  93.8 3.8 %collective-permute-start.24 = (f32[4,32,256]{2,1,0:T(8,128)}, f32[4,32,256]{2,1,0:T(8,128)S(1)}, u32[]{:S(2)}, u32[]{:S(2)}) collective-permute-start(f32[4,32,256]{2,1,0:T(8,128)} %get-tuple-element.61), channel_id=1, source_target_pairs={{0,32},{32,0},{64,96},{96,64},{128,160},{160,128},{192,224},{224,1... | collective-permute-start | bytes 393224 | tf_op jit(solution)/shard_map/ppermute | solution.py:45
  98.7 3.0 %collective-permute-start.19 = (bf16[8,128,256]{2,1,0:T(8,128)(2,1)S(1)}, bf16[8,128,256]{2,1,0:T(8,128)(2,1)}, u32[]{:S(2)}, u32[]{:S(2)}) collective-permute-start(bf16[8,128,256]{2,1,0:T(8,128)(2,1)S(1)} %add_convert_fusion), channel_id=1, source_target_pairs={{0,7},{1,0},{2,1},{3,2},{4,3},{5,4},{6,5},{7,6},{8,15},{9,8},{10,9... | collective-permute-start | bytes 1572872 | tf_op jit(solution)/shard_map/ppermute | solution.py:45
  105.9 1.9 %collective-permute-done.25 = f32[32,256]{1,0:T(8,128)S(1)} collective-permute-done((f32[32,256]{1,0:T(8,128)S(1)}, f32[32,256]{1,0:T(8,128)S(1)}, u32[]{:S(2)}, u32[]{:S(2)}) %collective-permute-start.25) | collective-permute-done | bytes 32800 | tf_op jit(solution)/shard_map/ppermute | solution.py:45
  110.3 1.4 collective-permute-done.30
  114.8 9.2 %all-to-all-start = ((bf16[8,256,256]{2,1,0:T(8,128)(2,1)}), bf16[8,256,256]{2,1,0:T(8,128)(2,1)S(1)}, u32[]{:S(2)}, u32[]{:S(2)}) async-start(bf16[8,256,256]{2,1,0:T(8,128)(2,1)} %get-tuple-element.62), calls=%async_computation | async-start | bytes 2097152 | tf_op jit(solution)/shard_map/all_to_all | solution.py:462
  124.2 1.4 fusion.37
  125.6 1.5 %collective-permute-start.22 = (bf16[256,256]{1,0:T(8,128)(2,1)S(1)}, bf16[256,256]{1,0:T(8,128)(2,1)S(1)}, u32[]{:S(2)}, u32[]{:S(2)}) collective-permute-start(bf16[256,256]{1,0:T(8,128)(2,1)S(1)} %bitcast.84), channel_id=1, source_target_pairs={{0,24},{1,25},{2,26},{3,27},{4,28},{5,29},{6,30},{7,31},{8,0},{9,1... | collective-permute-start | bytes 393224 | tf_op jit(solution)/shard_map/ppermute | solution.py:45
  127.8 3.3 %collective-permute-start.33 = (f32[32,256]{1,0:T(8,128)S(1)}, f32[32,256]{1,0:T(8,128)S(1)}, u32[]{:S(2)}, u32[]{:S(2)}) collective-permute-start(f32[32,256]{1,0:T(8,128)S(1)} %add.464), channel_id=1, source_target_pairs={{0,4},{1,5},{2,6},{3,7},{4,0},{5,1},{6,2},{7,3},{8,12},{9,13},{10,... | collective-permute-start | bytes 98312 | tf_op jit(solution)/shard_map/ppermute | solution.py:45
  131.3 3.3 %collective-permute-done.33 = f32[32,256]{1,0:T(8,128)S(1)} collective-permute-done((f32[32,256]{1,0:T(8,128)S(1)}, f32[32,256]{1,0:T(8,128)S(1)}, u32[]{:S(2)}, u32[]{:S(2)}) %collective-permute-start.33) | collective-permute-done | bytes 32800 | tf_op jit(solution)/shard_map/ppermute | solution.py:45
  134.6 2.2 %collective-permute-done.20 = bf16[256,256]{1,0:T(8,128)(2,1)S(1)} collective-permute-done((bf16[256,256]{1,0:T(8,128)(2,1)S(1)}, bf16[256,256]{1,0:T(8,128)(2,1)S(1)}, u32[]{:S(2)}, u32[]{:S(2)}) %collective-permute-start.20) | collective-permute-done | bytes 131104 | tf_op jit(solution)/shard_map/ppermute | solution.py:45
  137.6 1.5 %all-to-all-done = bf16[8,256,256]{2,1,0:T(8,128)(2,1)S(1)} async-done(((bf16[8,256,256]{2,1,0:T(8,128)(2,1)}), bf16[8,256,256]{2,1,0:T(8,128)(2,1)S(1)}, u32[]{:S(2)}, u32[]{:S(2)}) %all-to-all-start) | async-done | bytes 1048608 | tf_op jit(solution)/shard_map/all_to_all | solution.py:462
  139.4 2.0 %collective-permute-start.35 = (f32[32,256]{1,0:T(8,128)S(1)}, f32[32,256]{1,0:T(8,128)S(1)}, u32[]{:S(2)}, u32[]{:S(2)}) collective-permute-start(f32[32,256]{1,0:T(8,128)S(1)} %add.465), channel_id=1, source_target_pairs={{0,128},{32,160},{64,192},{96,224},{128,0},{160,32},{192,64},{224,... | collective-permute-start | bytes 98312 | tf_op jit(solution)/shard_map/ppermute | solution.py:45
  144.4 2.2 %collective-permute-start.37 = (f32[4,32,256]{2,1,0:T(8,128)S(1)}, f32[4,32,256]{2,1,0:T(8,128)S(1)}, u32[]{:S(2)}, u32[]{:S(2)}) collective-permute-start(f32[4,32,256]{2,1,0:T(8,128)S(1)} %pad_maximum_fusion.2), channel_id=1, source_target_pairs={{0,32},{32,0},{64,96},{96,64},{128,160},{160,128},{192,224},{224,1... | collective-permute-start | bytes 393224 | tf_op jit(solution)/shard_map/ppermute | solution.py:45
  (140 shorter events, 35.4 us)
Async XLA Ops:
  2.3 8.6 %collective-permute-start = (bf16[256,256]{1,0:T(8,128)(2,1)S(1)}, bf16[256,256]{1,0:T(8,128)(2,1)S(1)}, u32[]{:S(2)}, u32[]{:S(2)}) collective-permute-start(bf16[256,256]{1,0:T(8,128)(2,1)S(1)} %multiply_convert_fusion.1.refs_0_), channel_id=1, source_target_pairs={{0,7},{1,0},{2,1},{3,2},{4,3},{5,4},{6,5},{7,6},{8,15},{9,8},{10,9... | collective-permute-start | bytes 393224 | tf_op jit(solution)/shard_map/ppermute | solution.py:45
  8.8 5.6 %collective-permute-start.8 = (bf16[256,256]{1,0:T(8,128)(2,1)S(1)}, bf16[256,256]{1,0:T(8,128)(2,1)S(1)}, u32[]{:S(2)}, u32[]{:S(2)}) collective-permute-start(bf16[256,256]{1,0:T(8,128)(2,1)S(1)} %multiply_convert_fusion.1.refs_0_), channel_id=1, source_target_pairs={{0,1},{1,2},{2,3},{3,4},{4,5},{5,6},{6,7},{7,0},{8,9},{9,10},{10,1... | collective-permute-start | bytes 393224 | tf_op jit(solution)/shard_map/ppermute | solution.py:45
  11.0 5.4 %collective-permute-start.1 = (bf16[256,256]{1,0:T(8,128)(2,1)S(1)}, bf16[256,256]{1,0:T(8,128)(2,1)S(1)}, u32[]{:S(2)}, u32[]{:S(2)}) collective-permute-start(bf16[256,256]{1,0:T(8,128)(2,1)S(1)} %collective-permute-done.refs_1_), channel_id=1, source_target_pairs={{0,7},{1,0},{2,1},{3,2},{4,3},{5,4},{6,5},{7,6},{8,15},{9,8},{10,9... | collective-permute-start | bytes 393224 | tf_op jit(solution)/shard_map/ppermute | solution.py:45
  14.4 5.0 %collective-permute-start.9 = (bf16[256,256]{1,0:T(8,128)(2,1)S(1)}, bf16[256,256]{1,0:T(8,128)(2,1)S(1)}, u32[]{:S(2)}, u32[]{:S(2)}) collective-permute-start(bf16[256,256]{1,0:T(8,128)(2,1)S(1)} %collective-permute-done.8.refs_7_), channel_id=1, source_target_pairs={{0,1},{1,2},{2,3},{3,4},{4,5},{5,6},{6,7},{7,0},{8,9},{9,10},{10,1... | collective-permute-start | bytes 393224 | tf_op jit(solution)/shard_map/ppermute | solution.py:45
  16.4 5.0 %collective-permute-start.2 = (bf16[256,256]{1,0:T(8,128)(2,1)S(1)}, bf16[256,256]{1,0:T(8,128)(2,1)S(1)}, u32[]{:S(2)}, u32[]{:S(2)}) collective-permute-start(bf16[256,256]{1,0:T(8,128)(2,1)S(1)} %collective-permute-done.1.refs_2_), channel_id=1, source_target_pairs={{0,7},{1,0},{2,1},{3,2},{4,3},{5,4},{6,5},{7,6},{8,15},{9,8},{10,9... | collective-permute-start | bytes 393224 | tf_op jit(solution)/shard_map/ppermute | solution.py:45
  19.4 6.9 %collective-permute-start.10 = (bf16[256,256]{1,0:T(8,128)(2,1)S(1)}, bf16[256,256]{1,0:T(8,128)(2,1)S(1)}, u32[]{:S(2)}, u32[]{:S(2)}) collective-permute-start(bf16[256,256]{1,0:T(8,128)(2,1)S(1)} %collective-permute-done.9.refs_6_), channel_id=1, source_target_pairs={{0,1},{1,2},{2,3},{3,4},{4,5},{5,6},{6,7},{7,0},{8,9},{9,10},{10,1... | collective-permute-start | bytes 393224 | tf_op jit(solution)/shard_map/ppermute | solution.py:45
  21.4 8.2 %collective-permute-start.5 = (bf16[272,256]{1,0:T(8,128)(2,1)S(1)}, bf16[272,256]{1,0:T(8,128)(2,1)S(1)}, u32[]{:S(2)}, u32[]{:S(2)}) collective-permute-start(bf16[272,256]{1,0:T(8,128)(2,1)S(1)} %fusion.7), channel_id=1, source_target_pairs={{0,64},{32,96},{64,128},{96,160},{128,192},{160,224},{192,0},{224,... | collective-permute-start | bytes 417800 | tf_op jit(solution)/shard_map/ppermute | solution.py:45
  22.7 6.9 %collective-permute-start.4 = (bf16[272,256]{1,0:T(8,128)(2,1)S(1)}, bf16[272,256]{1,0:T(8,128)(2,1)S(1)}, u32[]{:S(2)}, u32[]{:S(2)}) collective-permute-start(bf16[272,256]{1,0:T(8,128)(2,1)S(1)} %fusion.7), channel_id=1, source_target_pairs={{0,128},{32,160},{64,192},{96,224},{128,0},{160,32},{192,64},{224,... | collective-permute-start | bytes 417800 | tf_op jit(solution)/shard_map/ppermute | solution.py:45
  26.4 9.2 %collective-permute-start.11 = (bf16[256,256]{1,0:T(8,128)(2,1)S(1)}, bf16[256,256]{1,0:T(8,128)(2,1)S(1)}, u32[]{:S(2)}, u32[]{:S(2)}) collective-permute-start(bf16[256,256]{1,0:T(8,128)(2,1)S(1)} %broadcast_select_fusion.1), channel_id=1, source_target_pairs={{0,1},{1,2},{2,3},{3,4},{4,5},{5,6},{6,7},{7,0},{8,9},{9,10},{10,1... | collective-permute-start | bytes 393224 | tf_op jit(solution)/shard_map/ppermute | solution.py:45
  29.7 13.7 %collective-permute-start.6 = (bf16[4,272,256]{2,1,0:T(8,128)(2,1)S(1)}, bf16[4,272,256]{2,1,0:T(8,128)(2,1)S(1)}, u32[]{:S(2)}, u32[]{:S(2)}) collective-permute-start(bf16[4,272,256]{2,1,0:T(8,128)(2,1)S(1)} %pad_maximum_fusion.own_ref.refs_3_), channel_id=1, source_target_pairs={{0,32},{32,0},{64,96},{96,64},{128,160},{160,128},{192,224},{224,1... | collective-permute-start | bytes 1671176 | tf_op jit(solution)/shard_map/ppermute | solution.py:45
  38.6 27.4 %collective-permute-start.12 = (bf16[16,128,256]{2,1,0:T(8,128)(2,1)}, bf16[16,128,256]{2,1,0:T(8,128)(2,1)S(1)}, u32[]{:S(2)}, u32[]{:S(2)}) collective-permute-start(bf16[16,128,256]{2,1,0:T(8,128)(2,1)} %bitcast.74), channel_id=1, source_target_pairs={{0,8},{1,9},{2,10},{3,11},{4,12},{5,13},{6,14},{7,15},{8,16},{9,17... | collective-permute-start | bytes 3145736 | tf_op jit(solution)/shard_map/ppermute | solution.py:45
  39.9 26.2 %collective-permute-start.13 = (bf16[16,128,256]{2,1,0:T(8,128)(2,1)}, bf16[16,128,256]{2,1,0:T(8,128)(2,1)S(1)}, u32[]{:S(2)}, u32[]{:S(2)}) collective-permute-start(bf16[16,128,256]{2,1,0:T(8,128)(2,1)} %bitcast.75), channel_id=1, source_target_pairs={{0,24},{1,25},{2,26},{3,27},{4,28},{5,29},{6,30},{7,31},{8,0},{9,1... | collective-permute-start | bytes 3145736 | tf_op jit(solution)/shard_map/ppermute | solution.py:45
  51.7 11.8 %collective-permute-start.7 = (bf16[8,128,256]{2,1,0:T(8,128)(2,1)}, bf16[8,128,256]{2,1,0:T(8,128)(2,1)S(1)}, u32[]{:S(2)}, u32[]{:S(2)}) collective-permute-start(bf16[8,128,256]{2,1,0:T(8,128)(2,1)} %get-tuple-element.45), channel_id=1, source_target_pairs={{0,1},{1,2},{2,3},{3,4},{4,5},{5,6},{6,7},{7,0},{8,9},{9,10},{10,1... | collective-permute-start | bytes 1572872 | tf_op jit(solution)/shard_map/ppermute | solution.py:45
  66.0 13.6 %collective-permute-start.14 = (bf16[8,128,256]{2,1,0:T(8,128)(2,1)}, bf16[8,128,256]{2,1,0:T(8,128)(2,1)}, u32[]{:S(2)}, u32[]{:S(2)}) collective-permute-start(bf16[8,128,256]{2,1,0:T(8,128)(2,1)} %get-tuple-element.47), channel_id=1, source_target_pairs={{0,1},{1,2},{2,3},{3,4},{4,5},{5,6},{6,7},{7,0},{8,9},{9,10},{10,1... | collective-permute-start | bytes 1572872 | tf_op jit(solution)/shard_map/ppermute | solution.py:45
  66.1 14.9 %collective-permute-start.15 = (bf16[8,128,256]{2,1,0:T(8,128)(2,1)}, bf16[8,128,256]{2,1,0:T(8,128)(2,1)}, u32[]{:S(2)}, u32[]{:S(2)}) collective-permute-start(bf16[8,128,256]{2,1,0:T(8,128)(2,1)} %get-tuple-element.49), channel_id=1, source_target_pairs={{0,7},{1,0},{2,1},{3,2},{4,3},{5,4},{6,5},{7,6},{8,15},{9,8},{10,9... | collective-permute-start | bytes 1572872 | tf_op jit(solution)/shard_map/ppermute | solution.py:45
  70.6 15.7 %collective-permute-start.23 = (bf16[16,128,256]{2,1,0:T(8,128)(2,1)}, bf16[16,128,256]{2,1,0:T(8,128)(2,1)S(1)}, u32[]{:S(2)}, u32[]{:S(2)}) collective-permute-start(bf16[16,128,256]{2,1,0:T(8,128)(2,1)} %broadcast_select_fusion), channel_id=1, source_target_pairs={{0,8},{1,9},{2,10},{3,11},{4,12},{5,13},{6,14},{7,15},{8,16},{9,17... | collective-permute-start | bytes 3145736 | tf_op jit(solution)/shard_map/ppermute | solution.py:45
  82.2 15.3 %collective-permute-start.18 = (bf16[8,128,256]{2,1,0:T(8,128)(2,1)S(1)}, bf16[8,128,256]{2,1,0:T(8,128)(2,1)}, u32[]{:S(2)}, u32[]{:S(2)}) collective-permute-start(bf16[8,128,256]{2,1,0:T(8,128)(2,1)S(1)} %add_convert_fusion.2), channel_id=1, source_target_pairs={{0,7},{1,0},{2,1},{3,2},{4,3},{5,4},{6,5},{7,6},{8,15},{9,8},{10,9... | collective-permute-start | bytes 1572872 | tf_op jit(solution)/shard_map/ppermute | solution.py:45
  86.2 18.9 %collective-permute-start.16 = (bf16[8,128,256]{2,1,0:T(8,128)(2,1)S(1)}, bf16[8,128,256]{2,1,0:T(8,128)(2,1)S(1)}, u32[]{:S(2)}, u32[]{:S(2)}) collective-permute-start(bf16[8,128,256]{2,1,0:T(8,128)(2,1)S(1)} %add_convert_fusion.3), channel_id=1, source_target_pairs={{0,1},{1,2},{2,3},{3,4},{4,5},{5,6},{6,7},{7,0},{8,9},{9,10},{10,1... | collective-permute-start | bytes 1572872 | tf_op jit(solution)/shard_map/ppermute | solution.py:45
  93.8 7.9 %collective-permute-start.24 = (f32[4,32,256]{2,1,0:T(8,128)}, f32[4,32,256]{2,1,0:T(8,128)S(1)}, u32[]{:S(2)}, u32[]{:S(2)}) collective-permute-start(f32[4,32,256]{2,1,0:T(8,128)} %get-tuple-element.61), channel_id=1, source_target_pairs={{0,32},{32,0},{64,96},{96,64},{128,160},{160,128},{192,224},{224,1... | collective-permute-start | bytes 393224 | tf_op jit(solution)/shard_map/ppermute | solution.py:45
  98.7 25.4 %collective-permute-start.19 = (bf16[8,128,256]{2,1,0:T(8,128)(2,1)S(1)}, bf16[8,128,256]{2,1,0:T(8,128)(2,1)}, u32[]{:S(2)}, u32[]{:S(2)}) collective-permute-start(bf16[8,128,256]{2,1,0:T(8,128)(2,1)S(1)} %add_convert_fusion), channel_id=1, source_target_pairs={{0,7},{1,0},{2,1},{3,2},{4,3},{5,4},{6,5},{7,6},{8,15},{9,8},{10,9... | collective-permute-start | bytes 1572872 | tf_op jit(solution)/shard_map/ppermute | solution.py:45
  104.2 4.3 %collective-permute-start.26 = (f32[32,256]{1,0:T(8,128)S(1)}, f32[32,256]{1,0:T(8,128)S(1)}, u32[]{:S(2)}, u32[]{:S(2)}) collective-permute-start(f32[32,256]{1,0:T(8,128)S(1)} %get-tuple-element.79), channel_id=1, source_target_pairs={{0,128},{32,160},{64,192},{96,224},{128,0},{160,32},{192,64},{224,... | collective-permute-start | bytes 98312 | tf_op jit(solution)/shard_map/ppermute | solution.py:45
  105.2 18.9 %collective-permute-start.17 = (bf16[8,128,256]{2,1,0:T(8,128)(2,1)S(1)}, bf16[8,128,256]{2,1,0:T(8,128)(2,1)S(1)}, u32[]{:S(2)}, u32[]{:S(2)}) collective-permute-start(bf16[8,128,256]{2,1,0:T(8,128)(2,1)S(1)} %add_convert_fusion.1), channel_id=1, source_target_pairs={{0,1},{1,2},{2,3},{3,4},{4,5},{5,6},{6,7},{7,0},{8,9},{9,10},{10,1... | collective-permute-start | bytes 1572872 | tf_op jit(solution)/shard_map/ppermute | solution.py:45
  108.6 4.4 %collective-permute-start.29 = (f32[32,256]{1,0:T(8,128)S(1)}, f32[32,256]{1,0:T(8,128)S(1)}, u32[]{:S(2)}, u32[]{:S(2)}) collective-permute-start(f32[32,256]{1,0:T(8,128)S(1)} %fusion.9), channel_id=1, source_target_pairs={{0,16},{1,17},{2,18},{3,19},{4,20},{5,21},{6,22},{7,23},{8,24},{9,... | collective-permute-start | bytes 98312 | tf_op jit(solution)/shard_map/ppermute | solution.py:45
  109.5 4.5 %collective-permute-start.28 = (f32[32,256]{1,0:T(8,128)S(1)}, f32[32,256]{1,0:T(8,128)S(1)}, u32[]{:S(2)}, u32[]{:S(2)}) collective-permute-start(f32[32,256]{1,0:T(8,128)S(1)} %fusion.9), channel_id=1, source_target_pairs={{0,8},{1,9},{2,10},{3,11},{4,12},{5,13},{6,14},{7,15},{8,16},{9,17... | collective-permute-start | bytes 98312 | tf_op jit(solution)/shard_map/ppermute | solution.py:45
  114.7 9.4 %collective-permute-start.31 = (f32[32,256]{1,0:T(8,128)S(1)}, f32[32,256]{1,0:T(8,128)S(1)}, u32[]{:S(2)}, u32[]{:S(2)}) collective-permute-start(f32[32,256]{1,0:T(8,128)S(1)} %select_reduce_fusion.1), channel_id=1, source_target_pairs={{0,1},{1,0},{2,3},{3,2},{4,5},{5,4},{6,7},{7,6},{8,9},{9,8},{10,11... | collective-permute-start | bytes 98312 | tf_op jit(solution)/shard_map/ppermute | solution.py:45
  114.8 24.3 %all-to-all-start = ((bf16[8,256,256]{2,1,0:T(8,128)(2,1)}), bf16[8,256,256]{2,1,0:T(8,128)(2,1)S(1)}, u32[]{:S(2)}, u32[]{:S(2)}) async-start(bf16[8,256,256]{2,1,0:T(8,128)(2,1)} %get-tuple-element.62), calls=%async_computation | async-start | bytes 2097152 | tf_op jit(solution)/shard_map/all_to_all | solution.py:462
  125.6 9.0 %collective-permute-start.22 = (bf16[256,256]{1,0:T(8,128)(2,1)S(1)}, bf16[256,256]{1,0:T(8,128)(2,1)S(1)}, u32[]{:S(2)}, u32[]{:S(2)}) collective-permute-start(bf16[256,256]{1,0:T(8,128)(2,1)S(1)} %bitcast.84), channel_id=1, source_target_pairs={{0,24},{1,25},{2,26},{3,27},{4,28},{5,29},{6,30},{7,31},{8,0},{9,1... | collective-permute-start | bytes 393224 | tf_op jit(solution)/shard_map/ppermute | solution.py:45
  127.1 7.5 %collective-permute-start.21 = (bf16[256,256]{1,0:T(8,128)(2,1)S(1)}, bf16[256,256]{1,0:T(8,128)(2,1)S(1)}, u32[]{:S(2)}, u32[]{:S(2)}) collective-permute-start(bf16[256,256]{1,0:T(8,128)(2,1)S(1)} %bitcast.83), channel_id=1, source_target_pairs={{0,16},{1,17},{2,18},{3,19},{4,20},{5,21},{6,22},{7,23},{8,24},{9,... | collective-permute-start | bytes 393224 | tf_op jit(solution)/shard_map/ppermute | solution.py:45
  127.7 9.1 %collective-permute-start.20 = (bf16[256,256]{1,0:T(8,128)(2,1)S(1)}, bf16[256,256]{1,0:T(8,128)(2,1)S(1)}, u32[]{:S(2)}, u32[]{:S(2)}) collective-permute-start(bf16[256,256]{1,0:T(8,128)(2,1)S(1)} %bitcast.82), channel_id=1, source_target_pairs={{0,8},{1,9},{2,10},{3,11},{4,12},{5,13},{6,14},{7,15},{8,16},{9,17... | collective-permute-start | bytes 393224 | tf_op jit(solution)/shard_map/ppermute | solution.py:45
  127.8 6.8 %collective-permute-start.33 = (f32[32,256]{1,0:T(8,128)S(1)}, f32[32,256]{1,0:T(8,128)S(1)}, u32[]{:S(2)}, u32[]{:S(2)}) collective-permute-start(f32[32,256]{1,0:T(8,128)S(1)} %add.464), channel_id=1, source_target_pairs={{0,4},{1,5},{2,6},{3,7},{4,0},{5,1},{6,2},{7,3},{8,12},{9,13},{10,... | collective-permute-start | bytes 98312 | tf_op jit(solution)/shard_map/ppermute | solution.py:45
  139.1 4.5 %collective-permute-start.34 = (f32[32,256]{1,0:T(8,128)S(1)}, f32[32,256]{1,0:T(8,128)S(1)}, u32[]{:S(2)}, u32[]{:S(2)}) collective-permute-start(f32[32,256]{1,0:T(8,128)S(1)} %add.465), channel_id=1, source_target_pairs={{0,64},{32,96},{64,128},{96,160},{128,192},{160,224},{192,0},{224,... | collective-permute-start | bytes 98312 | tf_op jit(solution)/shard_map/ppermute | solution.py:45
  139.4 4.5 %collective-permute-start.35 = (f32[32,256]{1,0:T(8,128)S(1)}, f32[32,256]{1,0:T(8,128)S(1)}, u32[]{:S(2)}, u32[]{:S(2)}) collective-permute-start(f32[32,256]{1,0:T(8,128)S(1)} %add.465), channel_id=1, source_target_pairs={{0,128},{32,160},{64,192},{96,224},{128,0},{160,32},{192,64},{224,... | collective-permute-start | bytes 98312 | tf_op jit(solution)/shard_map/ppermute | solution.py:45
  (25 other events, 317.6 us)
